TPU v7x, 256 devices: a whole 4x4x8 slice. The times are simulated.
256 devices in a mesh: dp: 16 (over z_lo, y, core), tensor: 16 (over z_hi, x).
Axes of the slice: x: 4, y: 4, z: 8 (z_hi: 4, z_lo: 2; z = z_hi * 2 + z_lo), core: 2. Of those that a mesh axis runs over, the one named last changes fastest.
Arguments:
- tokens: bfloat16 [131072, 3072], P(('dp', 'tensor')), parts along dimension 0, may hold values from -6 to 6
- expert_ids: int32 [131072, 4], P(('dp', 'tensor')), parts along dimension 0, may hold values from 0 to 15, as said below
- gate_probs: float32 [131072, 4], P(('dp', 'tensor')), parts along dimension 0, may hold values from 0.1 to 1
- gate_weight: bfloat16 [3072, 5376], P(None, 'tensor'), may hold values from -0.109375 to 0.109375
- up_weight: bfloat16 [3072, 5376], P(None, 'tensor'), may hold values from -0.109375 to 0.109375
- down_weight: bfloat16 [5376, 3072], P('tensor'), may hold values from -0.078125 to 0.078125
Outputs:
- mixed: bfloat16 [131072, 3072], P(('dp', 'tensor')), parts along dimension 0
There are 16 independent parts, one for each index of `dp`. A program takes and returns all parts, laid end to end along the dimension named above; an argument that names none is the same for every part. Nothing has to cross between parts.
Inputs may be any that keep to these rules, and one draw needn't show every extreme that they name: `expert_ids`: each row names 4 different experts. In each block of 128 consecutive tokens (rows b * 128 to (b + 1) * 128 - 1) between 1 and 32 rows name expert 0, and some block has exactly 32.
All inputs are finite; a program needn't handle non-finite values.
Results may differ from a plain program's by a relative error of at most 0.019.
Values may be sent and summed in bfloat16 or wider, within the bound.
No kernel may reach another device: no remote copies, remote signals or barrier semaphores. Data moves between devices by JAX's collectives and lax.ppermute only.
A program may use at most 128 MiB of HBM per device.

v0:
```python
import functools

import jax
import jax.numpy as jnp
import numpy as np
from jax import lax
from jax.experimental import pallas as pl
from jax.experimental.pallas import tpu as pltpu
from jax.sharding import Mesh, PartitionSpec as P

SPANS = 4
CT = 128
CAP = 32
AXES = ("z_lo", "y", "core", "z_hi", "x")
SIZES = (2, 4, 2, 4, 4)
UNITS = 168
SPLIT = 1536
ROWS = 512
ALL_VMEM_BYTES = 60 * 1024 * 1024


def moved(value, target, sends=None):
    pairs = []
    for source in range(int(np.prod(SIZES))):
        z_lo, y, core, z_hi, x = (int(i) for i in np.unravel_index(source, SIZES))
        z = 2 * z_hi + z_lo
        if sends is None or sends(z, y, core, x):
            z, y, core, x = target(z, y, core, x)
            z, y, core, x = z % 8, y % 4, core % 2, x % 4
            pairs.append((source, int(np.ravel_multi_index((z % 2, y, core, z // 2, x), SIZES))))
    return lax.ppermute(value, AXES, pairs)


def is_second(wanted):
    return lambda z, y, core, x: (z % 2 == core) == wanted


def along_z(z, y, core, x):
    return z + 1 - 2 * core, y, core, x


def along_y(z, y, core, x):
    return z, y + 1 - 2 * core, core, x


def other_core(z, y, core, x):
    return z, y, 1 - core, x


def along_x(step):
    return lambda z, y, core, x: (z, y, core, x + step)


def grouped(refs, counts):
    refs = list(refs)
    return [[refs.pop(0) for _ in range(count)] for count in counts]


class Staged:
    def __init__(self, place_ref, sources, staged, sems):
        self.sources, self.staged, self.sems = sources, staged, sems
        feeds = place_ref[0] == 1
        for option in (0, 1):

            @pl.when(feeds == (option == 1))
            def _(option=option):
                for index in range(len(sources)):
                    self.copy(index, option).start()

    def copy(self, index, option):
        options = self.sources[index]
        option = min(option, len(options) - 1)
        return pltpu.make_async_copy(options[option], self.staged.at[index], self.sems.at[index])

    def keep_units(self, place_ref, kept, owned=0):
        here = pl.multiple_of(place_ref[2] * SPLIT, SPLIT)
        lanes = [pl.ds(here, SPLIT), pl.ds(SPLIT - here, SPLIT)]
        for index in range(len(self.sources)):
            self.copy(index, 0).wait()
            start = (owned + index // 4) * UNITS
            kept[index // 2 % 2][start : start + UNITS, lanes[index % 2]] = self.staged[index]

    def keep_down(self, kept):
        for index in range(len(self.sources)):
            self.copy(index, 0).wait()
            kept[index * UNITS : (index + 1) * UNITS, :] = self.staged[index]


SPANS_OF_ROWS = [pl.ds(start, ROWS) for start in range(0, 2 * ROWS, ROWS)]


def row_copies(rows_ref, rows_kept, sems):
    return [
        pltpu.make_async_copy(rows_ref.at[span], rows_kept.at[span], sems.at[index])
        for index, span in enumerate(SPANS_OF_ROWS)
    ]


def hidden_of(rows, gate_kept, up_kept):
    gate_pre, up_pre = (
        lax.dot_general(rows, kept[...], (((1,), (1,)), ((), ())), preferred_element_type=jnp.float32)
        for kept in (gate_kept, up_kept)
    )
    return (gate_pre / (1.0 + jnp.exp(-gate_pre)) * up_pre).astype(jnp.bfloat16)


def early_kernel(counts, place_ref, rows_ref, *refs):
    total = sum(counts)
    own_ref, out_ref, rows_kept, own_kept, staged, gate_kept, up_kept, sems, row_sems = refs[total:]
    blocks = Staged(place_ref, grouped(refs[:total], counts), staged, sems)
    copies = row_copies(rows_ref, rows_kept, row_sems)
    for copy in copies:
        copy.start()
    own_copy = pltpu.make_async_copy(own_ref, own_kept, row_sems.at[2])
    own_copy.start()
    blocks.keep_units(place_ref, (gate_kept, up_kept), owned=1)
    own_copy.wait()
    gate_kept[:UNITS, :] = own_kept[:UNITS, :]
    up_kept[:UNITS, :] = own_kept[UNITS:, :]
    for copy, span in zip(copies, SPANS_OF_ROWS):
        copy.wait()
        out_ref[span, :] = hidden_of(rows_kept[span, :], gate_kept, up_kept)


def down_into(place_ref, outs, first, last, kept):
    core = place_ref[1]
    for owner, out_ref in zip((1 - core, core), outs):
        span = pl.ds(pl.multiple_of(owner * ROWS, ROWS), ROWS)
        units = jnp.concatenate([first[span, :], last[span, :]], axis=1)
        out_ref[...] = jnp.dot(units, kept[...], preferred_element_type=jnp.float32).astype(jnp.bfloat16)


def late_kernel(unit_counts, down_counts, place_ref, rows_ref, first_ref, *refs):
    split = sum(unit_counts)
    total = split + sum(down_counts)
    others_ref, mine_ref, last_ref = refs[total : total + 3]
    rows_kept, first_kept, staged, gate_kept, up_kept, down_kept, sems, row_sems = refs[total + 3 :]
    units = len(unit_counts)
    blocks = Staged(place_ref, grouped(refs[:split], unit_counts), staged.at[pl.ds(0, units)], sems.at[pl.ds(0, units)])
    copies = row_copies(rows_ref, rows_kept, row_sems)
    for copy in copies:
        copy.start()
    downs = Staged(
        place_ref, grouped(refs[split:total], down_counts), staged.at[pl.ds(units, 4)], sems.at[pl.ds(units, 4)]
    )
    first_copy = pltpu.make_async_copy(first_ref, first_kept, row_sems.at[2])
    first_copy.start()
    blocks.keep_units(place_ref, (gate_kept, up_kept))
    for copy, span in zip(copies, SPANS_OF_ROWS):
        copy.wait()
        last_ref[span, :] = hidden_of(rows_kept[span, :], gate_kept, up_kept)
    downs.keep_down(down_kept)
    first_copy.wait()
    down_into(place_ref, (others_ref, mine_ref), first_kept, last_ref, down_kept)


def down_kernel(down_counts, place_ref, first_ref, last_ref, *refs):
    total = sum(down_counts)
    others_ref, mine_ref, first_kept, last_kept, staged, down_kept, sems, row_sems = refs[total:]
    downs = Staged(place_ref, grouped(refs[:total], down_counts), staged, sems)
    copies = [
        pltpu.make_async_copy(first_ref, first_kept, row_sems.at[0]),
        pltpu.make_async_copy(last_ref, last_kept, row_sems.at[1]),
    ]
    for copy in copies:
        copy.start()
    downs.keep_down(down_kept)
    for copy in copies:
        copy.wait()
    down_into(place_ref, (others_ref, mine_ref), first_kept, last_kept, down_kept)


def whole(*shape):
    return pl.BlockSpec(shape, lambda: (0,) * len(shape))


def kernel_call(kernel, place, arrays, outs, scratch):
    return pl.pallas_call(
        kernel,
        out_shape=[jax.ShapeDtypeStruct(shape, jnp.bfloat16) for shape in outs],
        in_specs=[pl.BlockSpec(memory_space=pltpu.SMEM)]
        + [pl.BlockSpec(memory_space=pltpu.HBM)] * len(arrays),
        out_specs=[whole(*shape) for shape in outs],
        scratch_shapes=scratch,
        compiler_params=pltpu.CompilerParams(vmem_limit_bytes=ALL_VMEM_BYTES),
        cost_estimate=pl.CostEstimate(flops=1000000, bytes_accessed=100000, transcendentals=0),
    )(place, *arrays)


def vmem(*shape):
    return pltpu.VMEM(shape, jnp.bfloat16)


def flat(sources):
    return [array for source in sources for array in source]


def early_hidden(place, rows, sources, own):
    units = (1 + len(sources) // 4) * UNITS
    scratch = [
        vmem(2 * ROWS, 2 * SPLIT),
        vmem(*own.shape),
        vmem(len(sources), UNITS, SPLIT),
        vmem(units, 2 * SPLIT),
        vmem(units, 2 * SPLIT),
        pltpu.SemaphoreType.DMA((len(sources),)),
        pltpu.SemaphoreType.DMA((3,)),
    ]
    kernel = functools.partial(early_kernel, [len(source) for source in sources])
    return kernel_call(kernel, place, [rows, *flat(sources), own], [(2 * ROWS, units)], scratch)[0]


def late_products(place, rows, first, sources, down_sources):
    scratch = [
        vmem(2 * ROWS, 2 * SPLIT),
        vmem(*first.shape),
        vmem(8, UNITS, SPLIT),
        vmem(UNITS, 2 * SPLIT),
        vmem(UNITS, 2 * SPLIT),
        vmem(4 * UNITS, SPLIT),
        pltpu.SemaphoreType.DMA((8,)),
        pltpu.SemaphoreType.DMA((3,)),
    ]
    kernel = functools.partial(late_kernel, [len(source) for source in sources], [len(source) for source in down_sources])
    arrays = [rows, first, *flat(sources), *flat(down_sources)]
    return kernel_call(kernel, place, arrays, [(ROWS, SPLIT), (ROWS, SPLIT), (2 * ROWS, UNITS)], scratch)


def down_products(place, first, last, down_sources):
    scratch = [
        vmem(*first.shape),
        vmem(*last.shape),
        vmem(4, UNITS, SPLIT),
        vmem(4 * UNITS, SPLIT),
        pltpu.SemaphoreType.DMA((4,)),
        pltpu.SemaphoreType.DMA((2,)),
    ]
    kernel = functools.partial(down_kernel, [len(source) for source in down_sources])
    return kernel_call(kernel, place, [first, last, *flat(down_sources)], [(ROWS, SPLIT)] * 2, scratch)


def spread_kernel(place_ref, places_ref, share_ref, *refs):
    out_ref = refs[-1]
    here = pl.multiple_of(place_ref[2] * SPLIT, SPLIT)
    places = places_ref[...]
    for index, lanes in enumerate((pl.ds(here, SPLIT), pl.ds(SPLIT - here, SPLIT))):
        if index == 0:
            parts = [refs[0][...]]
        else:
            expert_out = refs[1][...] + refs[2][...].astype(jnp.float32) + refs[3][...].astype(jnp.float32)
            high = expert_out.astype(jnp.bfloat16)
            parts = [high, (expert_out - high.astype(jnp.float32)).astype(jnp.bfloat16)]
        picked = [jnp.dot(places, part, preferred_element_type=jnp.float32) for part in parts]
        out_ref[:, lanes] = (share_ref[...] * sum(picked[1:], picked[0])).astype(jnp.bfloat16)


def spread(place, places, share, terms):
    block = lambda shape: pl.BlockSpec(shape, lambda i, place: (i, 0))
    return pl.pallas_call(
        spread_kernel,
        out_shape=jax.ShapeDtypeStruct((SPANS * CT, 2 * SPLIT), jnp.bfloat16),
        grid_spec=pltpu.PrefetchScalarGridSpec(
            num_scalar_prefetch=1,
            grid=(SPANS,),
            in_specs=[block((CT, CAP)), block((CT, 1))] + [block((CAP, term.shape[1])) for term in terms],
            out_specs=block((CT, 2 * SPLIT)),
        ),
        compiler_params=pltpu.CompilerParams(vmem_limit_bytes=ALL_VMEM_BYTES),
    )(place, places, share, *terms)


def on_device(tokens, expert_ids, gate_probs, gate_weight, up_weight, down_weight):
    model_width = tokens.shape[1]
    z_lo, y, core, x = (lax.axis_index(name) for name in ("z_lo", "y", "core", "x"))
    first = z_lo != core
    half = y % 2

    is_window = expert_ids == 0
    routed = jnp.any(is_window, axis=1)
    gate_share = jnp.sum(jnp.where(is_window, gate_probs, 0.0), axis=1)
    routed_blocks = routed.reshape(SPANS, CT)
    slot_place = jnp.cumsum(routed_blocks.astype(jnp.int32), axis=1) - 1
    selector = (
        slot_place[:, None, :] == jnp.arange(CAP, dtype=jnp.int32)[None, :, None]
    ) & routed_blocks[:, None, :]
    slot_rows = jnp.einsum(
        "bst,btd->bsd",
        selector.astype(jnp.bfloat16),
        tokens.reshape(SPANS, CT, model_width),
        preferred_element_type=jnp.float32,
    ).astype(jnp.bfloat16).reshape(SPANS * CAP, model_width)
    near_units, far_units = core * UNITS, (1 - core) * UNITS

    def piece(array, start, side):
        return lax.dynamic_slice(array, (start, side * SPLIT), (UNITS, SPLIT))

    shard = [gate_weight.T, up_weight.T, down_weight]
    order = [(0, near_units), (1, near_units), (2, near_units), (0, far_units), (1, far_units), (2, far_units)]
    own = [piece(shard[0], near_units, half)]
    place = jnp.stack([first.astype(jnp.int32), core, half])

    def joined(*parts):
        return jnp.concatenate(parts, axis=0)

    def pick(parts, index):
        return (parts[index], parts[index + 2])

    from_z, from_y = [], []
    work = slot_rows
    for step in range(13):
        if step < 5:
            feed = own[step]
        elif step < 7:
            feed = from_z[step - 3]
        elif step < 9:
            feed = own[5] if step == 7 else from_z[4]
        if step < 2:
            block, sends = feed, is_second(False)
        elif step < 9:
            block, sends = jnp.where(first, feed, from_z[step - 2]), None
        else:
            block, sends = from_z[step - 2], is_second(True)
        landed = max(step - 1, 0)
        settled = from_y[max(step - 4, 0) : max(step - 3, 0)]
        if step == 8:
            work["rows"] = rows
        block, from_z[:landed], settled, own, shard, work = lax.optimization_barrier(
            (block, from_z[:landed], settled, own, shard, work)
        )
        if step >= 4:
            from_y[step - 4] = settled[0]
        if step < 5:
            own.append(piece(shard[order[step + 1][0]], order[step + 1][1], half))
        if step < 11:
            from_z.append(moved(block, along_z, sends))
        if step >= 2:
            gets = is_second(True) if step < 4 else None if step < 11 else is_second(False)
            from_y.append(moved(from_z[step - 2], along_y, gets))
        if step == 0:
            rows = lax.all_gather(work, ("core", "x"), axis=0, tiled=True)
            work = {}
        if step == 8:
            own_parts = [lax.dynamic_slice_in_dim(array, near_units, UNITS, 0) for array in shard[:2]]
            work["own"] = joined(*own_parts[:2])
            work["down"] = [piece(shard[2], near_units, side) for side in (half, 1 - half)]
        def block_at(index):
            return [pick(from_z, index), pick(from_y, index), pick(from_z, index + 1), pick(from_y, index + 1)]

        if step == 10:
            work["hidden"] = early_hidden(place, work["rows"], block_at(0) + block_at(3), work["own"])

    def downs(side, parts):
        return [(work["down"][side],), pick(parts, 2), pick(parts, 7), pick(parts, 8)]

    others_here, mine_here, last = late_products(place, work["rows"], work["hidden"], block_at(5), downs(0, from_z))
    others_here, last, from_y[9], from_y[10] = lax.optimization_barrier((others_here, last, from_y[9], from_y[10]))
    sums_here = (mine_here.astype(jnp.float32) + moved(others_here, other_core).astype(jnp.float32)).astype(jnp.bfloat16)
    out_here = lax.psum_scatter(sums_here, "x", scatter_dimension=0, tiled=True)
    others_there, mine_there = down_products(place, work["hidden"], last, downs(1, from_y))
    pair_there = (mine_there, moved(others_there, other_core))

    def summed(pair, step):
        start = (x + step) % 4 * (SPANS * CAP)
        first_part, second_part = (lax.dynamic_slice_in_dim(part, start, SPANS * CAP, 0) for part in pair)
        return first_part.astype(jnp.float32) + second_part.astype(jnp.float32)

    half_rows = SPANS * CAP // 2

    def far_pieces(pair):
        piece_on = summed(pair, 2).astype(jnp.bfloat16)
        return piece_on[:half_rows], piece_on[half_rows:]

    def far(pieces):
        return moved(pieces[0], along_x(1)), moved(pieces[1], along_x(3))

    def near(pair, arrived):
        above, below = summed(pair, 1), summed(pair, 3)
        above = joined(above[:half_rows] + arrived[0].astype(jnp.float32), above[half_rows:]).astype(jnp.bfloat16)
        below = joined(below[:half_rows], below[half_rows:] + arrived[1].astype(jnp.float32)).astype(jnp.bfloat16)
        return [moved(above, along_x(1)), moved(below, along_x(3))]

    pieces_there, pair_there = lax.optimization_barrier((far_pieces(pair_there), pair_there))
    near_there = near(pair_there, far(pieces_there))
    terms = [out_here, summed(pair_there, 0), *near_there]
    places = jnp.swapaxes(selector, 1, 2).reshape(SPANS * CT, CAP).astype(jnp.bfloat16)
    return spread(place, places, gate_share[:, None], terms)


def solution(mesh):
    grid = Mesh(mesh.devices.reshape(SIZES), AXES)
    shard = ("z_hi", "x")
    in_specs = (
        P(AXES, None),
        P(AXES, None),
        P(AXES, None),
        P(None, shard),
        P(None, shard),
        P(shard, None),
    )
    return jax.shard_map(
        on_device, mesh=grid, in_specs=in_specs, out_specs=P(AXES, None), check_vma=False
    )
```

profile of v0, /device:TPU:1, one launch (start us, length us, event | category | flops | bytes accessed | tf_op | source)
XLA Modules:
  0.0 172.9 jit_solution(5201584929663353859)
XLA Ops:
  7.5 1.2 reduce_window_sum.11
  8.7 1.8 %dynamic-slice_bitcast_fusion = bf16[168,1536]{1,0:T(8,128)(2,1)} fusion(bf16[3072,336]{0,1:T(8,128)(2,1)} %param.9, s32[]{:T(128)S(6)} %select_n.104, s32[]{:T(128)S(6)} %select_n.105), kind=kLoop, calls=%fused_computation.7 | loop fusion | bytes 1032200 | tf_op jit(solution)/shard_map/dynamic_slice | solution.py:295
  10.5 1.4 convolution_convert_fusion
  12.0 9.1 %collective-permute-start = (bf16[168,1536]{1,0:T(8,128)(2,1)}, bf16[168,1536]{1,0:T(8,128)(2,1)}, u32[]{:S(2)}, u32[]{:S(2)}) collective-permute-start(bf16[168,1536]{1,0:T(8,128)(2,1)} %dynamic-slice_bitcast_fusion), channel_id=1, source_target_pairs={{16,156},{17,157},{18,158},{19,159},{20,144},{21,145},{22,146},{23... | collective-permute-start | bytes 1548296 | tf_op jit(solution)/shard_map/ppermute | solution.py:31
  21.1 1.8 %dynamic_slice.55 = bf16[168,1536]{1,0:T(8,128)(2,1)} dynamic-slice(bf16[336,3072]{1,0:T(8,128)(2,1)} %bitcast.19, s32[]{:T(128)S(6)} %select_n.105, s32[]{:T(128)S(6)} %select_n.104), dynamic_slice_sizes={168,1536} | dynamic-slice | bytes 1032196 | tf_op jit(solution)/shard_map/dynamic_slice | solution.py:295
  23.0 2.1 %collective-permute-start.1 = (bf16[168,1536]{1,0:T(8,128)(2,1)}, bf16[168,1536]{1,0:T(8,128)(2,1)}, u32[]{:S(2)}, u32[]{:S(2)}) collective-permute-start(bf16[168,1536]{1,0:T(8,128)(2,1)} %dynamic_slice.55), channel_id=1, source_target_pairs={{16,156},{17,157},{18,158},{19,159},{20,144},{21,145},{22,146},{23... | collective-permute-start | bytes 1548296 | tf_op jit(solution)/shard_map/ppermute | solution.py:31
  25.1 1.6 collective-permute-done.refs_0_
  26.7 2.0 %broadcast_select_fusion.6 = bf16[168,1536]{1,0:T(8,128)(2,1)} fusion(bf16[168,1536]{1,0:T(8,128)(2,1)} %collective-permute-done.refs_0_, pred[]{:T(512)S(6)} %ne.25, bf16[336,3072]{1,0:T(8,128)(2,1)} %param.11, s32[]{:T(128)S(6)} %select_n.105, s32[]{:T(128)S(6)} %select_n.104), kind=kLoop, calls=%fused_computation.14 | loop fusion | flops 258048 | bytes 1548297 | tf_op jit(solution)/shard_map/jit(_where)/select_n | solution.py:320
  28.7 3.3 %collective-permute-start.2 = (bf16[168,1536]{1,0:T(8,128)(2,1)}, bf16[168,1536]{1,0:T(8,128)(2,1)}, u32[]{:S(2)}, u32[]{:S(2)}) collective-permute-start(bf16[168,1536]{1,0:T(8,128)(2,1)} %broadcast_select_fusion.6), channel_id=1, source_target_pairs={{0,128},{1,129},{2,130},{3,131},{4,132},{5,133},{6,134},{7,135},{8... | collective-permute-start | bytes 1548296 | tf_op jit(solution)/shard_map/ppermute | solution.py:31
  32.7 1.2 broadcast_select_fusion.5
  33.9 4.2 %collective-permute-start.4 = (bf16[168,1536]{1,0:T(8,128)(2,1)S(1)}, bf16[168,1536]{1,0:T(8,128)(2,1)}, u32[]{:S(2)}, u32[]{:S(2)}) collective-permute-start(bf16[168,1536]{1,0:T(8,128)(2,1)S(1)} %broadcast_select_fusion.5), channel_id=1, source_target_pairs={{0,128},{1,129},{2,130},{3,131},{4,132},{5,133},{6,134},{7,135},{8... | collective-permute-start | bytes 1548296 | tf_op jit(solution)/shard_map/ppermute | solution.py:31
  38.8 1.2 broadcast_select_fusion.4
  40.0 3.2 %collective-permute-start.6 = (bf16[168,1536]{1,0:T(8,128)(2,1)S(1)}, bf16[168,1536]{1,0:T(8,128)(2,1)S(1)}, u32[]{:S(2)}, u32[]{:S(2)}) collective-permute-start(bf16[168,1536]{1,0:T(8,128)(2,1)S(1)} %broadcast_select_fusion.4), channel_id=1, source_target_pairs={{0,128},{1,129},{2,130},{3,131},{4,132},{5,133},{6,134},{7,135},{8... | collective-permute-start | bytes 1548296 | tf_op jit(solution)/shard_map/ppermute | solution.py:31
  43.2 3.2 %collective-permute-start.7 = (bf16[168,1536]{1,0:T(8,128)(2,1)}, bf16[168,1536]{1,0:T(8,128)(2,1)}, u32[]{:S(2)}, u32[]{:S(2)}) collective-permute-start(bf16[168,1536]{1,0:T(8,128)(2,1)} %collective-permute-done.2.refs_1_.refs_9_), channel_id=1, source_target_pairs={{0,32},{1,33},{2,34},{3,35},{4,36},{5,37},{6,38},{7,39},{8,40},{9,... | collective-permute-start | bytes 1548296 | tf_op jit(solution)/shard_map/ppermute | solution.py:31
  46.4 1.9 %broadcast_select_fusion.3 = bf16[168,1536]{1,0:T(8,128)(2,1)} fusion(bf16[168,1536]{1,0:T(8,128)(2,1)} %collective-permute-done.2.refs_1_.refs_9_, bf16[168,1536]{1,0:T(8,128)(2,1)} %collective-permute-done.4.refs_5_.refs_8_, pred[]{:T(512)S(6)} %ne.25), kind=kLoop, calls=%fused_computation.11 | loop fusion | flops 258048 | bytes 1548289 | tf_op jit(solution)/shard_map/jit(_where)/select_n | solution.py:320
  48.3 1.9 %dynamic_slice.59 = bf16[168,1536]{1,0:T(8,128)(2,1)} dynamic-slice(bf16[336,3072]{1,0:T(8,128)(2,1)} %param.11, s32[]{:T(128)S(6)} %select_n.107, s32[]{:T(128)S(6)} %select_n.104), dynamic_slice_sizes={168,1536} | dynamic-slice | bytes 1032196 | tf_op jit(solution)/shard_map/dynamic_slice | solution.py:295
  50.2 1.2 collective-permute-start.8
  51.4 2.4 %collective-permute-start.9 = (bf16[168,1536]{1,0:T(8,128)(2,1)}, bf16[168,1536]{1,0:T(8,128)(2,1)}, u32[]{:S(2)}, u32[]{:S(2)}) collective-permute-start(bf16[168,1536]{1,0:T(8,128)(2,1)} %collective-permute-done.4.refs_5_.refs_8_), channel_id=1, source_target_pairs={{0,32},{1,33},{2,34},{3,35},{4,36},{5,37},{6,38},{7,39},{8,40},{9,... | collective-permute-start | bytes 1548296 | tf_op jit(solution)/shard_map/ppermute | solution.py:31
  54.7 1.9 %broadcast_select_fusion.2 = bf16[168,1536]{1,0:T(8,128)(2,1)} fusion(bf16[168,1536]{1,0:T(8,128)(2,1)} %collective-permute-done.4.refs_5_.refs_8_, bf16[168,1536]{1,0:T(8,128)(2,1)S(1)} %collective-permute-done.6.refs_12_.refs_10_, pred[]{:T(512)S(6)} %ne.25), kind=kLoop, calls=%fused_computation.10 | loop fusion | flops 258048 | bytes 1548289 | tf_op jit(solution)/shard_map/jit(_where)/select_n | solution.py:320
  58.8 1.9 %broadcast_select_fusion.1 = bf16[168,1536]{1,0:T(8,128)(2,1)} fusion(bf16[168,1536]{1,0:T(8,128)(2,1)} %dynamic_slice.59, bf16[168,1536]{1,0:T(8,128)(2,1)} %collective-permute-done.8.refs_9_.refs_0_, pred[]{:T(512)S(6)} %ne.25), kind=kLoop, calls=%fused_computation.9 | loop fusion | flops 258048 | bytes 1548289 | tf_op jit(solution)/shard_map/jit(_where)/select_n | solution.py:320
  60.7 2.4 %collective-permute-start.13 = (bf16[168,1536]{1,0:T(8,128)(2,1)}, bf16[168,1536]{1,0:T(8,128)(2,1)}, u32[]{:S(2)}, u32[]{:S(2)}) collective-permute-start(bf16[168,1536]{1,0:T(8,128)(2,1)} %broadcast_select_fusion.1), channel_id=1, source_target_pairs={{0,128},{1,129},{2,130},{3,131},{4,132},{5,133},{6,134},{7,135},{8... | collective-permute-start | bytes 1548296 | tf_op jit(solution)/shard_map/ppermute | solution.py:31
  63.1 2.4 %collective-permute-start.14 = (bf16[168,1536]{1,0:T(8,128)(2,1)}, bf16[168,1536]{1,0:T(8,128)(2,1)}, u32[]{:S(2)}, u32[]{:S(2)}) collective-permute-start(bf16[168,1536]{1,0:T(8,128)(2,1)} %collective-permute-done.8.refs_9_.refs_0_), channel_id=1, source_target_pairs={{0,32},{1,33},{2,34},{3,35},{4,36},{5,37},{6,38},{7,39},{8,40},{9,... | collective-permute-start | bytes 1548296 | tf_op jit(solution)/shard_map/ppermute | solution.py:31
  65.6 1.9 %broadcast_select_fusion = bf16[168,1536]{1,0:T(8,128)(2,1)} fusion(bf16[168,1536]{1,0:T(8,128)(2,1)} %copy-done.1, bf16[168,1536]{1,0:T(8,128)(2,1)} %collective-permute-done.10.refs_13_.refs_4_, pred[]{:T(512)S(6)} %ne.25), kind=kLoop, calls=%fused_computation.8 | loop fusion | flops 258048 | bytes 1548289 | tf_op jit(solution)/shard_map/jit(_where)/select_n | solution.py:320
  67.5 1.2 collective-permute-start.12
  68.7 2.1 %collective-permute-start.15 = (bf16[168,1536]{1,0:T(8,128)(2,1)}, bf16[168,1536]{1,0:T(8,128)(2,1)}, u32[]{:S(2)}, u32[]{:S(2)}) collective-permute-start(bf16[168,1536]{1,0:T(8,128)(2,1)} %collective-permute-done.10.refs_13_.refs_4_), channel_id=1, source_target_pairs={{0,32},{1,33},{2,34},{3,35},{4,36},{5,37},{6,38},{7,39},{8,40},{9,... | collective-permute-start | bytes 1548296 | tf_op jit(solution)/shard_map/ppermute | solution.py:31
  70.8 1.7 constant_dynamic-slice_fusion
  72.5 1.1 fusion.8
  73.6 1.4 pad_maximum_fusion.refs_16_
  75.0 1.3 collective-permute-start.16
  77.5 1.3 collective-permute-start.18
  78.7 3.5 %collective-permute-start.19 = (bf16[168,1536]{1,0:T(8,128)(2,1)}, bf16[168,1536]{1,0:T(8,128)(2,1)}, u32[]{:S(2)}, u32[]{:S(2)}) collective-permute-start(bf16[168,1536]{1,0:T(8,128)(2,1)} %collective-permute-done.12.refs_5_.refs_13_), channel_id=1, source_target_pairs={{0,32},{1,33},{2,34},{3,35},{4,36},{5,37},{6,38},{7,39},{8,40},{9,... | collective-permute-start | bytes 1548296 | tf_op jit(solution)/shard_map/ppermute | solution.py:31
  82.9 13.6 %shard_map.64.first_ref = bf16[1024,504]{1,0:T(8,128)(2,1)} custom-call(s32[3]{0:T(128)} %pad_add_fusion.place_ref, bf16[1024,3072]{1,0:T(8,128)(2,1)} %all-gather.2.cloned.1.call-done.rows_ref, bf16[168,1536]{1,0:T(8,128)(2,1)} %collective-permute-done.refs_0_, bf16[168,1536]{1,0:T(8,128)(2,1)} %collective-permute-done.2.refs_1_.refs_9_, ...), custom_call_target="tpu_custom_call" | custom-call | flops 1000000 | bytes 100000 | tf_op jit(solution)/shard_map/pallas_call | solution.py:178
  96.5 1.9 %collective-permute-start.20 = (bf16[168,1536]{1,0:T(8,128)(2,1)}, bf16[168,1536]{1,0:T(8,128)(2,1)S(1)}, u32[]{:S(2)}, u32[]{:S(2)}) collective-permute-start(bf16[168,1536]{1,0:T(8,128)(2,1)} %collective-permute-done.16.refs_12_), channel_id=1, source_target_pairs={{16,112},{17,113},{18,114},{19,115},{20,116},{21,117},{22,118},{23... | collective-permute-start | bytes 1548296 | tf_op jit(solution)/shard_map/ppermute | solution.py:31
  98.4 1.9 %collective-permute-start.21 = (bf16[168,1536]{1,0:T(8,128)(2,1)}, bf16[168,1536]{1,0:T(8,128)(2,1)}, u32[]{:S(2)}, u32[]{:S(2)}) collective-permute-start(bf16[168,1536]{1,0:T(8,128)(2,1)} %collective-permute-done.18.refs_14_), channel_id=1, source_target_pairs={{16,112},{17,113},{18,114},{19,115},{20,116},{21,117},{22,118},{23... | collective-permute-start | bytes 1548296 | tf_op jit(solution)/shard_map/ppermute | solution.py:31
  100.4 11.7 %shard_map.65 = (bf16[512,1536]{1,0:T(8,128)(2,1)}, bf16[512,1536]{1,0:T(8,128)(2,1)}, bf16[1024,168]{1,0:T(8,128)(2,1)}) custom-call(s32[3]{0:T(128)} %pad_add_fusion.place_ref, bf16[1024,3072]{1,0:T(8,128)(2,1)} %all-gather.2.cloned.1.call-done.rows_ref, bf16[1024,504]{1,0:T(8,128)(2,1)} %shard_map.64.first_ref, ...), custom_call_target="tpu_custom_call" | custom-call | flops 1000000 | bytes 100000 | tf_op jit(solution)/shard_map/pallas_call | solution.py:178
  112.2 1.8 %collective-permute-start.22 = (bf16[512,1536]{1,0:T(8,128)(2,1)}, bf16[512,1536]{1,0:T(8,128)(2,1)}, u32[]{:S(2)}, u32[]{:S(2)}) collective-permute-start(bf16[512,1536]{1,0:T(8,128)(2,1)} %get-tuple-element.274), channel_id=1, source_target_pairs={{0,16},{1,17},{2,18},{3,19},{4,20},{5,21},{6,22},{7,23},{8,24},{9,... | collective-permute-start | bytes 4718600 | tf_op jit(solution)/shard_map/ppermute | solution.py:31
  113.9 6.5 %shard_map.66 = (bf16[512,1536]{1,0:T(8,128)(2,1)}, bf16[512,1536]{1,0:T(8,128)(2,1)}) custom-call(s32[3]{0:T(128)} %pad_add_fusion.place_ref, bf16[1024,504]{1,0:T(8,128)(2,1)} %shard_map.64.first_ref, bf16[1024,168]{1,0:T(8,128)(2,1)} %get-tuple-element.275.last_ref, bf16[168,1536]{1,0:T(8,128)(2,1)} %get-tuple-element.276.refs_0_, ...), custom_call_target="tpu_custom_call" | custom-call | flops 1000000 | bytes 100000 | tf_op jit(solution)/shard_map/pallas_call | solution.py:178
  121.0 3.4 %add_convert_fusion = bf16[512,1536]{1,0:T(8,128)(2,1)} fusion(bf16[512,1536]{1,0:T(8,128)(2,1)} %collective-permute-done.22, bf16[512,1536]{1,0:T(8,128)(2,1)} %get-tuple-element.271), kind=kLoop, calls=%fused_computation.1 | loop fusion | flops 3145728 | bytes 4718592 | tf_op jit(solution)/shard_map/convert_element_type | solution.py:357
  124.5 1.3 add_convert_fusion.1
  125.8 2.5 %collective-permute-start.26 = (bf16[64,1536]{1,0:T(8,128)(2,1)S(1)}, bf16[64,1536]{1,0:T(8,128)(2,1)S(1)}, u32[]{:S(2)}, u32[]{:S(2)}) collective-permute-start(bf16[64,1536]{1,0:T(8,128)(2,1)S(1)} %get-tuple-element.284), channel_id=1, source_target_pairs={{0,3},{1,0},{2,1},{3,2},{4,7},{5,4},{6,5},{7,6},{8,11},{9,8},{10,9... | collective-permute-start | bytes 589832 | tf_op jit(solution)/shard_map/ppermute | solution.py:31
  128.4 2.4 %convert_add_fusion = (f32[128,1536]{1,0:T(8,128)S(1)}, f32[128,1536]{1,0:T(8,128)S(1)}, f32[128,1536]{1,0:T(8,128)}) fusion(bf16[512,1536]{1,0:T(8,128)(2,1)} %collective-permute-done.23, s32[]{:T(128)S(6)} %select_n.122, bf16[512,1536]{1,0:T(8,128)(2,1)S(1)} %copy-done.3, s32[]{:T(128)S(6)} %select_n.120, s32[]{:T(128)S(6)} %select_n.118), kind=kLoop, calls=%fused_computation.3 | loop fusion | flops 1769472 | bytes 4718604 | tf_op jit(solution)/shard_map/add | solution.py:365
  130.9 1.6 collective-permute-done.26
  133.3 3.4 %collective-permute-start.27 = (bf16[128,1536]{1,0:T(8,128)(2,1)}, bf16[128,1536]{1,0:T(8,128)(2,1)S(1)}, u32[]{:S(2)}, u32[]{:S(2)}) collective-permute-start(bf16[128,1536]{1,0:T(8,128)(2,1)} %pad_maximum_fusion.2), channel_id=1, source_target_pairs={{0,3},{1,0},{2,1},{3,2},{4,7},{5,4},{6,5},{7,6},{8,11},{9,8},{10,9... | collective-permute-start | bytes 1179656 | tf_op jit(solution)/shard_map/ppermute | solution.py:31
  136.7 1.3 collective-permute-done.24
  140.5 12.8 %collective-permute-done.27.refs_3_ = bf16[128,1536]{1,0:T(8,128)(2,1)S(1)} collective-permute-done((bf16[128,1536]{1,0:T(8,128)(2,1)}, bf16[128,1536]{1,0:T(8,128)(2,1)S(1)}, u32[]{:S(2)}, u32[]{:S(2)}) %collective-permute-start.27) | collective-permute-done | bytes 393248 | tf_op jit(solution)/shard_map/ppermute | solution.py:31
  153.3 5.7 %collective-permute-done.25.refs_2_ = bf16[128,1536]{1,0:T(8,128)(2,1)} collective-permute-done((bf16[128,1536]{1,0:T(8,128)(2,1)}, bf16[128,1536]{1,0:T(8,128)(2,1)}, u32[]{:S(2)}, u32[]{:S(2)}) %collective-permute-start.25) | collective-permute-done | bytes 393248 | tf_op jit(solution)/shard_map/ppermute | solution.py:31
  159.0 1.3 reduce-scatter.2.cloned.1.call-done.refs_0_
  160.3 5.7 %shard_map.67 = bf16[512,3072]{1,0:T(8,128)(2,1)} custom-call(s32[3]{0:T(128)} %pad_add_fusion.place_ref, bf16[512,32]{1,0:T(8,128)(2,1)} %fusion.3.places_ref, f32[512,1]{1,0:T(8,128)} %copy.7.share_ref, bf16[128,1536]{1,0:T(8,128)(2,1)} %reduce-scatter.2.cloned.1.call-done.refs_0_, f32[128,1536]{1,0:T(8,128)} %get-tuple-element.295.refs_1_, ...), custom_call_target="tpu_custom_call" | custom-call | tf_op jit(solution)/shard_map/pallas_call | solution.py:259
  (66 shorter events, 11.3 us)
Async XLA Ops:
  6.5 4.0 %copy-start = (bf16[512,3072]{1,0:T(8,128)(2,1)S(1)}, bf16[512,3072]{1,0:T(8,128)(2,1)}, u32[]{:S(2)}) copy-start(bf16[512,3072]{1,0:T(8,128)(2,1)} %param.6) | copy-start | bytes 9437188
  6.5 61.0 %all-gather.2.cloned.1.call-start = ((), (), s32[]{:S(2)}) async-start(), calls=%async_computation.1 | async-start | bytes 7077888 | tf_op jit(solution)/shard_map/all_gather | solution.py:340
  12.0 148.4 %reduce-scatter.2.cloned.1.call-start = ((), (), s32[]{:S(2)}) async-start(), calls=%async_computation.2 | async-start | bytes 1966080 | tf_op jit(solution)/shard_map/reduce_scatter | solution.py:358
  12.0 14.7 %collective-permute-start = (bf16[168,1536]{1,0:T(8,128)(2,1)}, bf16[168,1536]{1,0:T(8,128)(2,1)}, u32[]{:S(2)}, u32[]{:S(2)}) collective-permute-start(bf16[168,1536]{1,0:T(8,128)(2,1)} %dynamic-slice_bitcast_fusion), channel_id=1, source_target_pairs={{16,156},{17,157},{18,158},{19,159},{20,144},{21,145},{22,146},{23... | collective-permute-start | bytes 1548296 | tf_op jit(solution)/shard_map/ppermute | solution.py:31
  23.0 9.7 %collective-permute-start.1 = (bf16[168,1536]{1,0:T(8,128)(2,1)}, bf16[168,1536]{1,0:T(8,128)(2,1)}, u32[]{:S(2)}, u32[]{:S(2)}) collective-permute-start(bf16[168,1536]{1,0:T(8,128)(2,1)} %dynamic_slice.55), channel_id=1, source_target_pairs={{16,156},{17,157},{18,158},{19,159},{20,144},{21,145},{22,146},{23... | collective-permute-start | bytes 1548296 | tf_op jit(solution)/shard_map/ppermute | solution.py:31
  28.7 10.1 %collective-permute-start.2 = (bf16[168,1536]{1,0:T(8,128)(2,1)}, bf16[168,1536]{1,0:T(8,128)(2,1)}, u32[]{:S(2)}, u32[]{:S(2)}) collective-permute-start(bf16[168,1536]{1,0:T(8,128)(2,1)} %broadcast_select_fusion.6), channel_id=1, source_target_pairs={{0,128},{1,129},{2,130},{3,131},{4,132},{5,133},{6,134},{7,135},{8... | collective-permute-start | bytes 1548296 | tf_op jit(solution)/shard_map/ppermute | solution.py:31
  32.0 7.9 %collective-permute-start.3 = (bf16[168,1536]{1,0:T(8,128)(2,1)}, bf16[168,1536]{1,0:T(8,128)(2,1)S(1)}, u32[]{:S(2)}, u32[]{:S(2)}) collective-permute-start(bf16[168,1536]{1,0:T(8,128)(2,1)} %collective-permute-done.refs_0_), channel_id=1, source_target_pairs={{0,32},{1,33},{2,34},{3,35},{4,36},{5,37},{6,38},{7,39},{8,40},{9,... | collective-permute-start | bytes 1548296 | tf_op jit(solution)/shard_map/ppermute | solution.py:31
  33.9 12.5 %collective-permute-start.4 = (bf16[168,1536]{1,0:T(8,128)(2,1)S(1)}, bf16[168,1536]{1,0:T(8,128)(2,1)}, u32[]{:S(2)}, u32[]{:S(2)}) collective-permute-start(bf16[168,1536]{1,0:T(8,128)(2,1)S(1)} %broadcast_select_fusion.5), channel_id=1, source_target_pairs={{0,128},{1,129},{2,130},{3,131},{4,132},{5,133},{6,134},{7,135},{8... | collective-permute-start | bytes 1548296 | tf_op jit(solution)/shard_map/ppermute | solution.py:31
  38.1 12.1 %collective-permute-start.5 = (bf16[168,1536]{1,0:T(8,128)(2,1)}, bf16[168,1536]{1,0:T(8,128)(2,1)S(1)}, u32[]{:S(2)}, u32[]{:S(2)}) collective-permute-start(bf16[168,1536]{1,0:T(8,128)(2,1)} %collective-permute-done.1.refs_4_), channel_id=1, source_target_pairs={{0,32},{1,33},{2,34},{3,35},{4,36},{5,37},{6,38},{7,39},{8,40},{9,... | collective-permute-start | bytes 1548296 | tf_op jit(solution)/shard_map/ppermute | solution.py:31
  40.0 16.6 %copy-start.4 = (bf16[168,1536]{1,0:T(8,128)(2,1)}, bf16[168,1536]{1,0:T(8,128)(2,1)S(1)}, u32[]{:S(2)}) copy-start(bf16[168,1536]{1,0:T(8,128)(2,1)S(1)} %collective-permute-done.3.refs_2_) | copy-start | bytes 1548292
  40.0 13.9 %collective-permute-start.6 = (bf16[168,1536]{1,0:T(8,128)(2,1)S(1)}, bf16[168,1536]{1,0:T(8,128)(2,1)S(1)}, u32[]{:S(2)}, u32[]{:S(2)}) collective-permute-start(bf16[168,1536]{1,0:T(8,128)(2,1)S(1)} %broadcast_select_fusion.4), channel_id=1, source_target_pairs={{0,128},{1,129},{2,130},{3,131},{4,132},{5,133},{6,134},{7,135},{8... | collective-permute-start | bytes 1548296 | tf_op jit(solution)/shard_map/ppermute | solution.py:31
  43.2 13.4 %collective-permute-start.7 = (bf16[168,1536]{1,0:T(8,128)(2,1)}, bf16[168,1536]{1,0:T(8,128)(2,1)}, u32[]{:S(2)}, u32[]{:S(2)}) collective-permute-start(bf16[168,1536]{1,0:T(8,128)(2,1)} %collective-permute-done.2.refs_1_.refs_9_), channel_id=1, source_target_pairs={{0,32},{1,33},{2,34},{3,35},{4,36},{5,37},{6,38},{7,39},{8,40},{9,... | collective-permute-start | bytes 1548296 | tf_op jit(solution)/shard_map/ppermute | solution.py:31
  50.2 6.4 %copy-start.5 = (bf16[168,1536]{1,0:T(8,128)(2,1)}, bf16[168,1536]{1,0:T(8,128)(2,1)S(1)}, u32[]{:S(2)}) copy-start(bf16[168,1536]{1,0:T(8,128)(2,1)S(1)} %collective-permute-done.5.refs_6_) | copy-start | bytes 1548292
  50.2 8.6 %collective-permute-start.8 = (bf16[168,1536]{1,0:T(8,128)(2,1)}, bf16[168,1536]{1,0:T(8,128)(2,1)}, u32[]{:S(2)}, u32[]{:S(2)}) collective-permute-start(bf16[168,1536]{1,0:T(8,128)(2,1)} %broadcast_select_fusion.3), channel_id=1, source_target_pairs={{0,128},{1,129},{2,130},{3,131},{4,132},{5,133},{6,134},{7,135},{8... | collective-permute-start | bytes 1548296 | tf_op jit(solution)/shard_map/ppermute | solution.py:31
  51.4 9.3 %collective-permute-start.9 = (bf16[168,1536]{1,0:T(8,128)(2,1)}, bf16[168,1536]{1,0:T(8,128)(2,1)}, u32[]{:S(2)}, u32[]{:S(2)}) collective-permute-start(bf16[168,1536]{1,0:T(8,128)(2,1)} %collective-permute-done.4.refs_5_.refs_8_), channel_id=1, source_target_pairs={{0,32},{1,33},{2,34},{3,35},{4,36},{5,37},{6,38},{7,39},{8,40},{9,... | collective-permute-start | bytes 1548296 | tf_op jit(solution)/shard_map/ppermute | solution.py:31
  53.8 0.8 copy-start.1
  56.6 9.0 %collective-permute-start.10 = (bf16[168,1536]{1,0:T(8,128)(2,1)}, bf16[168,1536]{1,0:T(8,128)(2,1)}, u32[]{:S(2)}, u32[]{:S(2)}) collective-permute-start(bf16[168,1536]{1,0:T(8,128)(2,1)} %broadcast_select_fusion.2), channel_id=1, source_target_pairs={{0,128},{1,129},{2,130},{3,131},{4,132},{5,133},{6,134},{7,135},{8... | collective-permute-start | bytes 1548296 | tf_op jit(solution)/shard_map/ppermute | solution.py:31
  56.7 10.8 %collective-permute-start.11 = (bf16[168,1536]{1,0:T(8,128)(2,1)}, bf16[168,1536]{1,0:T(8,128)(2,1)}, u32[]{:S(2)}, u32[]{:S(2)}) collective-permute-start(bf16[168,1536]{1,0:T(8,128)(2,1)} %copy-done.1), channel_id=1, source_target_pairs={{0,32},{1,33},{2,34},{3,35},{4,36},{5,37},{6,38},{7,39},{8,40},{9,... | collective-permute-start | bytes 1548296 | tf_op jit(solution)/shard_map/ppermute | solution.py:31
  60.7 14.3 %collective-permute-start.13 = (bf16[168,1536]{1,0:T(8,128)(2,1)}, bf16[168,1536]{1,0:T(8,128)(2,1)}, u32[]{:S(2)}, u32[]{:S(2)}) collective-permute-start(bf16[168,1536]{1,0:T(8,128)(2,1)} %broadcast_select_fusion.1), channel_id=1, source_target_pairs={{0,128},{1,129},{2,130},{3,131},{4,132},{5,133},{6,134},{7,135},{8... | collective-permute-start | bytes 1548296 | tf_op jit(solution)/shard_map/ppermute | solution.py:31
  63.1 11.9 %collective-permute-start.14 = (bf16[168,1536]{1,0:T(8,128)(2,1)}, bf16[168,1536]{1,0:T(8,128)(2,1)}, u32[]{:S(2)}, u32[]{:S(2)}) collective-permute-start(bf16[168,1536]{1,0:T(8,128)(2,1)} %collective-permute-done.8.refs_9_.refs_0_), channel_id=1, source_target_pairs={{0,32},{1,33},{2,34},{3,35},{4,36},{5,37},{6,38},{7,39},{8,40},{9,... | collective-permute-start | bytes 1548296 | tf_op jit(solution)/shard_map/ppermute | solution.py:31
  67.5 5.0 %copy-start.2 = (bf16[336,3072]{1,0:T(8,128)(2,1)S(1)}, bf16[336,3072]{1,0:T(8,128)(2,1)}, u32[]{:S(2)}) copy-start(bf16[336,3072]{1,0:T(8,128)(2,1)} %param.11) | copy-start | bytes 6193156
  67.5 9.5 %collective-permute-start.12 = (bf16[168,1536]{1,0:T(8,128)(2,1)}, bf16[168,1536]{1,0:T(8,128)(2,1)}, u32[]{:S(2)}, u32[]{:S(2)}) collective-permute-start(bf16[168,1536]{1,0:T(8,128)(2,1)} %broadcast_select_fusion), channel_id=1, source_target_pairs={{0,128},{1,129},{2,130},{3,131},{4,132},{5,133},{6,134},{7,135},{8... | collective-permute-start | bytes 1548296 | tf_op jit(solution)/shard_map/ppermute | solution.py:31
  68.7 8.7 %collective-permute-start.15 = (bf16[168,1536]{1,0:T(8,128)(2,1)}, bf16[168,1536]{1,0:T(8,128)(2,1)}, u32[]{:S(2)}, u32[]{:S(2)}) collective-permute-start(bf16[168,1536]{1,0:T(8,128)(2,1)} %collective-permute-done.10.refs_13_.refs_4_), channel_id=1, source_target_pairs={{0,32},{1,33},{2,34},{3,35},{4,36},{5,37},{6,38},{7,39},{8,40},{9,... | collective-permute-start | bytes 1548296 | tf_op jit(solution)/shard_map/ppermute | solution.py:31
  75.0 21.4 %collective-permute-start.16 = (bf16[168,1536]{1,0:T(8,128)(2,1)}, bf16[168,1536]{1,0:T(8,128)(2,1)}, u32[]{:S(2)}, u32[]{:S(2)}) collective-permute-start(bf16[168,1536]{1,0:T(8,128)(2,1)} %collective-permute-done.13.refs_1_.refs_11_), channel_id=1, source_target_pairs={{0,128},{1,129},{2,130},{3,131},{4,132},{5,133},{6,134},{7,135},{8... | collective-permute-start | bytes 1548296 | tf_op jit(solution)/shard_map/ppermute | solution.py:31
  76.3 20.2 %collective-permute-start.17 = (bf16[168,1536]{1,0:T(8,128)(2,1)}, bf16[168,1536]{1,0:T(8,128)(2,1)}, u32[]{:S(2)}, u32[]{:S(2)}) collective-permute-start(bf16[168,1536]{1,0:T(8,128)(2,1)} %collective-permute-done.13.refs_1_.refs_11_), channel_id=1, source_target_pairs={{0,32},{1,33},{2,34},{3,35},{4,36},{5,37},{6,38},{7,39},{8,40},{9,... | collective-permute-start | bytes 1548296 | tf_op jit(solution)/shard_map/ppermute | solution.py:31
  77.5 21.0 %collective-permute-start.18 = (bf16[168,1536]{1,0:T(8,128)(2,1)}, bf16[168,1536]{1,0:T(8,128)(2,1)}, u32[]{:S(2)}, u32[]{:S(2)}) collective-permute-start(bf16[168,1536]{1,0:T(8,128)(2,1)} %collective-permute-done.12.refs_5_.refs_13_), channel_id=1, source_target_pairs={{0,128},{1,129},{2,130},{3,131},{4,132},{5,133},{6,134},{7,135},{8... | collective-permute-start | bytes 1548296 | tf_op jit(solution)/shard_map/ppermute | solution.py:31
  78.7 19.7 %collective-permute-start.19 = (bf16[168,1536]{1,0:T(8,128)(2,1)}, bf16[168,1536]{1,0:T(8,128)(2,1)}, u32[]{:S(2)}, u32[]{:S(2)}) collective-permute-start(bf16[168,1536]{1,0:T(8,128)(2,1)} %collective-permute-done.12.refs_5_.refs_13_), channel_id=1, source_target_pairs={{0,32},{1,33},{2,34},{3,35},{4,36},{5,37},{6,38},{7,39},{8,40},{9,... | collective-permute-start | bytes 1548296 | tf_op jit(solution)/shard_map/ppermute | solution.py:31
  96.5 15.6 %collective-permute-start.20 = (bf16[168,1536]{1,0:T(8,128)(2,1)}, bf16[168,1536]{1,0:T(8,128)(2,1)S(1)}, u32[]{:S(2)}, u32[]{:S(2)}) collective-permute-start(bf16[168,1536]{1,0:T(8,128)(2,1)} %collective-permute-done.16.refs_12_), channel_id=1, source_target_pairs={{16,112},{17,113},{18,114},{19,115},{20,116},{21,117},{22,118},{23... | collective-permute-start | bytes 1548296 | tf_op jit(solution)/shard_map/ppermute | solution.py:31
  98.4 13.7 %collective-permute-start.21 = (bf16[168,1536]{1,0:T(8,128)(2,1)}, bf16[168,1536]{1,0:T(8,128)(2,1)}, u32[]{:S(2)}, u32[]{:S(2)}) collective-permute-start(bf16[168,1536]{1,0:T(8,128)(2,1)} %collective-permute-done.18.refs_14_), channel_id=1, source_target_pairs={{16,112},{17,113},{18,114},{19,115},{20,116},{21,117},{22,118},{23... | collective-permute-start | bytes 1548296 | tf_op jit(solution)/shard_map/ppermute | solution.py:31
  112.1 1.9 %copy-start.6 = (bf16[168,1536]{1,0:T(8,128)(2,1)}, bf16[168,1536]{1,0:T(8,128)(2,1)S(1)}, u32[]{:S(2)}) copy-start(bf16[168,1536]{1,0:T(8,128)(2,1)S(1)} %collective-permute-done.20.refs_4_) | copy-start | bytes 1548292
  112.2 8.8 %collective-permute-start.22 = (bf16[512,1536]{1,0:T(8,128)(2,1)}, bf16[512,1536]{1,0:T(8,128)(2,1)}, u32[]{:S(2)}, u32[]{:S(2)}) collective-permute-start(bf16[512,1536]{1,0:T(8,128)(2,1)} %get-tuple-element.274), channel_id=1, source_target_pairs={{0,16},{1,17},{2,18},{3,19},{4,20},{5,21},{6,22},{7,23},{8,24},{9,... | collective-permute-start | bytes 4718600 | tf_op jit(solution)/shard_map/ppermute | solution.py:31
  120.4 4.0 %collective-permute-start.23 = (bf16[512,1536]{1,0:T(8,128)(2,1)}, bf16[512,1536]{1,0:T(8,128)(2,1)}, u32[]{:S(2)}, u32[]{:S(2)}) collective-permute-start(bf16[512,1536]{1,0:T(8,128)(2,1)} %get-tuple-element.280), channel_id=1, source_target_pairs={{0,16},{1,17},{2,18},{3,19},{4,20},{5,21},{6,22},{7,23},{8,24},{9,... | collective-permute-start | bytes 4718600 | tf_op jit(solution)/shard_map/ppermute | solution.py:31
  124.4 3.9 %copy-start.3 = (bf16[512,1536]{1,0:T(8,128)(2,1)S(1)}, bf16[512,1536]{1,0:T(8,128)(2,1)}, u32[]{:S(2)}) copy-start(bf16[512,1536]{1,0:T(8,128)(2,1)} %get-tuple-element.281) | copy-start | bytes 4718596
  125.8 6.6 %collective-permute-start.26 = (bf16[64,1536]{1,0:T(8,128)(2,1)S(1)}, bf16[64,1536]{1,0:T(8,128)(2,1)S(1)}, u32[]{:S(2)}, u32[]{:S(2)}) collective-permute-start(bf16[64,1536]{1,0:T(8,128)(2,1)S(1)} %get-tuple-element.284), channel_id=1, source_target_pairs={{0,3},{1,0},{2,1},{3,2},{4,7},{5,4},{6,5},{7,6},{8,11},{9,8},{10,9... | collective-permute-start | bytes 589832 | tf_op jit(solution)/shard_map/ppermute | solution.py:31
  130.8 7.2 %collective-permute-start.24 = (bf16[64,1536]{1,0:T(8,128)(2,1)S(1)}, bf16[64,1536]{1,0:T(8,128)(2,1)S(1)}, u32[]{:S(2)}, u32[]{:S(2)}) collective-permute-start(bf16[64,1536]{1,0:T(8,128)(2,1)S(1)} %get-tuple-element.283), channel_id=1, source_target_pairs={{0,1},{1,2},{2,3},{3,0},{4,5},{5,6},{6,7},{7,4},{8,9},{9,10},{10,1... | collective-permute-start | bytes 589832 | tf_op jit(solution)/shard_map/ppermute | solution.py:31
  133.3 20.0 %collective-permute-start.27 = (bf16[128,1536]{1,0:T(8,128)(2,1)}, bf16[128,1536]{1,0:T(8,128)(2,1)S(1)}, u32[]{:S(2)}, u32[]{:S(2)}) collective-permute-start(bf16[128,1536]{1,0:T(8,128)(2,1)} %pad_maximum_fusion.2), channel_id=1, source_target_pairs={{0,3},{1,0},{2,1},{3,2},{4,7},{5,4},{6,5},{7,6},{8,11},{9,8},{10,9... | collective-permute-start | bytes 1179656 | tf_op jit(solution)/shard_map/ppermute | solution.py:31
  138.8 20.2 %collective-permute-start.25 = (bf16[128,1536]{1,0:T(8,128)(2,1)}, bf16[128,1536]{1,0:T(8,128)(2,1)}, u32[]{:S(2)}, u32[]{:S(2)}) collective-permute-start(bf16[128,1536]{1,0:T(8,128)(2,1)} %pad_maximum_fusion.1), channel_id=1, source_target_pairs={{0,1},{1,2},{2,3},{3,0},{4,5},{5,6},{6,7},{7,4},{8,9},{9,10},{10,1... | collective-permute-start | bytes 1179656 | tf_op jit(solution)/shard_map/ppermute | solution.py:31
  153.3 7.0 %copy-start.7 = (bf16[128,1536]{1,0:T(8,128)(2,1)}, bf16[128,1536]{1,0:T(8,128)(2,1)S(1)}, u32[]{:S(2)}) copy-start(bf16[128,1536]{1,0:T(8,128)(2,1)S(1)} %collective-permute-done.27.refs_3_) | copy-start | bytes 1179652
Sparse Core Ops, SparseCore 0:
  12.1 47.6 all-gather.1
  124.5 35.7 reduce-scatter.1
where the time goes:
time: 174 us; the launch traced here: 173 us
  starting transfers between devices  58.4 us (34%)
  Pallas kernels  37.4 us (21%)
  waiting for transfers between devices  26 us (15%)
  other arithmetic  25.8 us (15%)
  between operations  13.7 us (8%)
  local copies, waits for them, and re-layouts  10.1 us (6%)
    ppermute x28, starting transfers between devices, moved(): return lax.ppermute(value, AXES, pairs)  58.4 us
    pallas_call x3, Pallas kernels, kernel_call(): pl.pallas_call(kernel, out_shape=[jax.ShapeDtypeStruct(shape, jnp.bfloat1...  31.7 us
    ppermute x28, waiting for transfers between devices, moved(): return lax.ppermute(value, AXES, pairs)  24.6 us
    select_n x7, other arithmetic, on_device(): block, sends = (jnp.where(first, feed, from_z[step - 2]), None)  12.1 us
    dynamic_slice x4, local copies, waits for them, and re-layouts, piece(): return lax.dynamic_slice(array, (start, side * SPLIT), (UNITS, SPLIT))  6.67 us
    pallas_call x1, Pallas kernels, spread(): pl.pallas_call(spread_kernel, out_shape=jax.ShapeDtypeStruct((SPANS * CT,...  5.72 us
  transfers between devices with their start and end apart: 30, of which 9 were waited for; matrix products, arithmetic and copies ran while one was open for 18% of the time, Pallas kernels for 18%

commit v1 on v0

--- a/solution.py
+++ b/solution.py
@@ -19,20 +19,15 @@
 ALL_VMEM_BYTES = 60 * 1024 * 1024
 
 
-def moved(value, target, sends=None):
+def moved(value, target):
     pairs = []
     for source in range(int(np.prod(SIZES))):
         z_lo, y, core, z_hi, x = (int(i) for i in np.unravel_index(source, SIZES))
         z = 2 * z_hi + z_lo
-        if sends is None or sends(z, y, core, x):
-            z, y, core, x = target(z, y, core, x)
-            z, y, core, x = z % 8, y % 4, core % 2, x % 4
-            pairs.append((source, int(np.ravel_multi_index((z % 2, y, core, z // 2, x), SIZES))))
+        z, y, core, x = target(z, y, core, x)
+        z, y, core, x = z % 8, y % 4, core % 2, x % 4
+        pairs.append((source, int(np.ravel_multi_index((z % 2, y, core, z // 2, x), SIZES))))
     return lax.ppermute(value, AXES, pairs)
-
-
-def is_second(wanted):
-    return lambda z, y, core, x: (z % 2 == core) == wanted
 
 
 def along_z(z, y, core, x):
@@ -96,30 +91,39 @@
     ]
 
 
-def hidden_of(rows, gate_kept, up_kept):
-    gate_pre, up_pre = (
-        lax.dot_general(rows, kept[...], (((1,), (1,)), ((), ())), preferred_element_type=jnp.float32)
-        for kept in (gate_kept, up_kept)
-    )
-    return (gate_pre / (1.0 + jnp.exp(-gate_pre)) * up_pre).astype(jnp.bfloat16)
+def hidden_rows(copies, rows_kept, gate_kept, up_kept, out_ref):
+    for copy in copies:
+        copy.wait()
+
+    @pl.loop(0, 2 * ROWS, step=ROWS)
+    def _(start):
+        span = pl.ds(pl.multiple_of(start, ROWS), ROWS)
+        gate_pre, up_pre = (
+            lax.dot_general(
+                rows_kept[span, :], kept[...], (((1,), (1,)), ((), ())), preferred_element_type=jnp.float32
+            )
+            for kept in (gate_kept, up_kept)
+        )
+        out_ref[span, :] = (gate_pre / (1.0 + jnp.exp(-gate_pre)) * up_pre).astype(jnp.bfloat16)
 
 
 def early_kernel(counts, place_ref, rows_ref, *refs):
     total = sum(counts)
-    own_ref, out_ref, rows_kept, own_kept, staged, gate_kept, up_kept, sems, row_sems = refs[total:]
+    own_refs, (out_ref, rows_kept, own_kept, staged, gate_kept, up_kept, sems, row_sems) = refs[total : total + 2], refs[total + 2 :]
+    own_copies = [
+        pltpu.make_async_copy(own_refs[index], own_kept.at[index], row_sems.at[2 + index]) for index in (0, 1)
+    ]
+    for copy in own_copies:
+        copy.start()
     blocks = Staged(place_ref, grouped(refs[:total], counts), staged, sems)
     copies = row_copies(rows_ref, rows_kept, row_sems)
     for copy in copies:
         copy.start()
-    own_copy = pltpu.make_async_copy(own_ref, own_kept, row_sems.at[2])
-    own_copy.start()
+    for index, kept in enumerate((gate_kept, up_kept)):
+        own_copies[index].wait()
+        kept[:UNITS, :] = own_kept[index]
     blocks.keep_units(place_ref, (gate_kept, up_kept), owned=1)
-    own_copy.wait()
-    gate_kept[:UNITS, :] = own_kept[:UNITS, :]
-    up_kept[:UNITS, :] = own_kept[UNITS:, :]
-    for copy, span in zip(copies, SPANS_OF_ROWS):
-        copy.wait()
-        out_ref[span, :] = hidden_of(rows_kept[span, :], gate_kept, up_kept)
+    hidden_rows(copies, rows_kept, gate_kept, up_kept, out_ref)
 
 
 def down_into(place_ref, outs, first, last, kept):
@@ -146,9 +150,7 @@
     first_copy = pltpu.make_async_copy(first_ref, first_kept, row_sems.at[2])
     first_copy.start()
     blocks.keep_units(place_ref, (gate_kept, up_kept))
-    for copy, span in zip(copies, SPANS_OF_ROWS):
-        copy.wait()
-        last_ref[span, :] = hidden_of(rows_kept[span, :], gate_kept, up_kept)
+    hidden_rows(copies, rows_kept, gate_kept, up_kept, last_ref)
     downs.keep_down(down_kept)
     first_copy.wait()
     down_into(place_ref, (others_ref, mine_ref), first_kept, last_ref, down_kept)
@@ -199,15 +201,15 @@
     units = (1 + len(sources) // 4) * UNITS
     scratch = [
         vmem(2 * ROWS, 2 * SPLIT),
-        vmem(*own.shape),
+        vmem(2, UNITS, 2 * SPLIT),
         vmem(len(sources), UNITS, SPLIT),
         vmem(units, 2 * SPLIT),
         vmem(units, 2 * SPLIT),
         pltpu.SemaphoreType.DMA((len(sources),)),
-        pltpu.SemaphoreType.DMA((3,)),
+        pltpu.SemaphoreType.DMA((4,)),
     ]
     kernel = functools.partial(early_kernel, [len(source) for source in sources])
-    return kernel_call(kernel, place, [rows, *flat(sources), own], [(2 * ROWS, units)], scratch)[0]
+    return kernel_call(kernel, place, [rows, *flat(sources), *own], [(2 * ROWS, units)], scratch)[0]
 
 
 def late_products(place, rows, first, sources, down_sources):
@@ -315,11 +317,11 @@
         elif step < 9:
             feed = own[5] if step == 7 else from_z[4]
         if step < 2:
-            block, sends = feed, is_second(False)
+            block = feed
         elif step < 9:
-            block, sends = jnp.where(first, feed, from_z[step - 2]), None
+            block = jnp.where(first, feed, from_z[step - 2])
         else:
-            block, sends = from_z[step - 2], is_second(True)
+            block = from_z[step - 2]
         landed = max(step - 1, 0)
         settled = from_y[max(step - 4, 0) : max(step - 3, 0)]
         if step == 8:
@@ -329,34 +331,34 @@
         )
         if step >= 4:
             from_y[step - 4] = settled[0]
-        if step < 5:
-            own.append(piece(shard[order[step + 1][0]], order[step + 1][1], half))
+        if step == 0:
+            own.append(piece(shard[order[1][0]], order[1][1], half))
+        if step == 1:
+            own += [piece(shard[which], start, half) for which, start in order[2:]]
+            work["own"] = [lax.dynamic_slice_in_dim(array, near_units, UNITS, 0) for array in shard[:2]]
+            work["down"] = [piece(shard[2], near_units, side) for side in (half, 1 - half)]
+            work["place"] = place
         if step < 11:
-            from_z.append(moved(block, along_z, sends))
+            from_z.append(moved(block, along_z))
         if step >= 2:
-            gets = is_second(True) if step < 4 else None if step < 11 else is_second(False)
-            from_y.append(moved(from_z[step - 2], along_y, gets))
+            from_y.append(moved(from_z[step - 2], along_y))
         if step == 0:
             rows = lax.all_gather(work, ("core", "x"), axis=0, tiled=True)
             work = {}
-        if step == 8:
-            own_parts = [lax.dynamic_slice_in_dim(array, near_units, UNITS, 0) for array in shard[:2]]
-            work["own"] = joined(*own_parts[:2])
-            work["down"] = [piece(shard[2], near_units, side) for side in (half, 1 - half)]
         def block_at(index):
             return [pick(from_z, index), pick(from_y, index), pick(from_z, index + 1), pick(from_y, index + 1)]
 
         if step == 10:
-            work["hidden"] = early_hidden(place, work["rows"], block_at(0) + block_at(3), work["own"])
+            work["hidden"] = early_hidden(work["place"], work["rows"], block_at(0) + block_at(3), work["own"])
 
     def downs(side, parts):
         return [(work["down"][side],), pick(parts, 2), pick(parts, 7), pick(parts, 8)]
 
-    others_here, mine_here, last = late_products(place, work["rows"], work["hidden"], block_at(5), downs(0, from_z))
+    others_here, mine_here, last = late_products(work["place"], work["rows"], work["hidden"], block_at(5), downs(0, from_z))
     others_here, last, from_y[9], from_y[10] = lax.optimization_barrier((others_here, last, from_y[9], from_y[10]))
     sums_here = (mine_here.astype(jnp.float32) + moved(others_here, other_core).astype(jnp.float32)).astype(jnp.bfloat16)
     out_here = lax.psum_scatter(sums_here, "x", scatter_dimension=0, tiled=True)
-    others_there, mine_there = down_products(place, work["hidden"], last, downs(1, from_y))
+    others_there, mine_there = down_products(work["place"], work["hidden"], last, downs(1, from_y))
     pair_there = (mine_there, moved(others_there, other_core))
 
     def summed(pair, step):
@@ -383,7 +385,7 @@
     near_there = near(pair_there, far(pieces_there))
     terms = [out_here, summed(pair_there, 0), *near_there]
     places = jnp.swapaxes(selector, 1, 2).reshape(SPANS * CT, CAP).astype(jnp.bfloat16)
-    return spread(place, places, gate_share[:, None], terms)
+    return spread(work["place"], places, gate_share[:, None], terms)
 
 
 def solution(mesh):

time: 174 us -> 167 us (0.960)
  other arithmetic: 25.8 us -> 15.5 us
  waiting for transfers between devices: 26 us -> 33 us
  starting transfers between devices: 58.4 us -> 51.5 us
  local copies, waits for them, and re-layouts: 10.1 us -> 13.2 us
    select_n x7 -> x6, other arithmetic: 12.1 us -> 1.99 us  [on_device(): block = jnp.where(first, feed, from_z[step - 2])]
    ppermute x28, waiting for transfers between devices: 24.6 us -> 32.9 us  [moved(): return lax.ppermute(value, AXES, pairs)]
    ppermute x28, starting transfers between devices: 58.4 us -> 51.5 us  [moved(): return lax.ppermute(value, AXES, pairs)]
  transfers between devices with their start and end apart: 30 -> 30, of which waited for: 9 -> 15; matrix products, arithmetic and copies ran while one was open for 18% -> 14% of each run, Pallas kernels for 18% -> 19%
where the time goes in v1:
time: 167 us
  starting transfers between devices  51.5 us (31%)
  Pallas kernels  38.2 us (23%)
  waiting for transfers between devices  33 us (20%)
  other arithmetic  15.5 us (9%)
  between operations  13.7 us (8%)
  local copies, waits for them, and re-layouts  13.2 us (8%)
    ppermute x28, starting transfers between devices, moved(): return lax.ppermute(value, AXES, pairs)  51.5 us
    ppermute x28, waiting for transfers between devices, moved(): return lax.ppermute(value, AXES, pairs)  32.9 us
    pallas_call x3, Pallas kernels, kernel_call(): pl.pallas_call(kernel, out_shape=[jax.ShapeDtypeStruct(shape, jnp.bfloat1...  32.5 us
    dynamic_slice x4, local copies, waits for them, and re-layouts, piece(): return lax.dynamic_slice(array, (start, side * SPLIT), (UNITS, SPLIT))  7.48 us
    pallas_call x1, Pallas kernels, spread(): pl.pallas_call(spread_kernel, out_shape=jax.ShapeDtypeStruct((SPANS * CT,...  5.7 us
    convert_element_type x1, other arithmetic, on_device(): (mine_here.astype(jnp.float32) + moved(others_here, other_core).astype(jn...  3.41 us
  transfers between devices with their start and end apart: 30, of which 15 were waited for; matrix products, arithmetic and copies ran while one was open for 14% of the time, Pallas kernels for 19%

profile of v1, /device:TPU:1, one launch (start us, length us, event | category | flops | bytes accessed | tf_op | source)
XLA Modules:
  0.0 166.5 jit_solution(13568961061588328234)
XLA Ops:
  6.5 0.9 select_reduce_fusion
  7.5 1.2 reduce_window_sum.11
  8.7 1.9 %dynamic-slice_bitcast_fusion = bf16[168,1536]{1,0:T(8,128)(2,1)} fusion(bf16[3072,336]{0,1:T(8,128)(2,1)} %param.9, s32[]{:T(128)S(6)} %select_n.103, s32[]{:T(128)S(6)} %select_n.104), kind=kLoop, calls=%fused_computation.6 | loop fusion | bytes 1032200 | tf_op jit(solution)/shard_map/dynamic_slice | solution.py:297
  10.6 1.4 convolution_convert_fusion
  12.1 6.5 %collective-permute-start = (bf16[168,1536]{1,0:T(8,128)(2,1)}, bf16[168,1536]{1,0:T(8,128)(2,1)}, u32[]{:S(2)}, u32[]{:S(2)}) collective-permute-start(bf16[168,1536]{1,0:T(8,128)(2,1)} %dynamic-slice_bitcast_fusion), channel_id=1, source_target_pairs={{0,128},{1,129},{2,130},{3,131},{4,132},{5,133},{6,134},{7,135},{8... | collective-permute-start | bytes 1548296 | tf_op jit(solution)/shard_map/ppermute | solution.py:30
  18.5 1.9 %dynamic_slice.53 = bf16[168,1536]{1,0:T(8,128)(2,1)} dynamic-slice(bf16[336,3072]{1,0:T(8,128)(2,1)} %bitcast.19, s32[]{:T(128)S(6)} %select_n.104, s32[]{:T(128)S(6)} %select_n.103), dynamic_slice_sizes={168,1536} | dynamic-slice | bytes 1032196 | tf_op jit(solution)/shard_map/dynamic_slice | solution.py:297
  21.1 1.9 %dynamic_slice.55 = bf16[168,1536]{1,0:T(8,128)(2,1)} dynamic-slice(bf16[336,3072]{1,0:T(8,128)(2,1)} %bitcast.17, s32[]{:T(128)S(6)} %select_n.106, s32[]{:T(128)S(6)} %select_n.103), dynamic_slice_sizes={168,1536} | dynamic-slice | bytes 1032196 | tf_op jit(solution)/shard_map/dynamic_slice | solution.py:297
  23.0 1.9 %dynamic_slice.56 = bf16[168,1536]{1,0:T(8,128)(2,1)} dynamic-slice(bf16[336,3072]{1,0:T(8,128)(2,1)} %bitcast.20, s32[]{:T(128)S(6)} %select_n.106, s32[]{:T(128)S(6)} %select_n.103), dynamic_slice_sizes={168,1536} | dynamic-slice | bytes 1032196 | tf_op jit(solution)/shard_map/dynamic_slice | solution.py:297
  25.5 3.1 %constant_dynamic-slice_fusion = (bf16[168,3072]{1,0:T(8,128)(2,1)}, bf16[168,3072]{1,0:T(8,128)(2,1)}) fusion(bf16[336,3072]{1,0:T(8,128)(2,1)} %bitcast.21, s32[]{:T(128)S(6)} %select_n.104, bf16[336,3072]{1,0:T(8,128)(2,1)} %bitcast.18), kind=kLoop, calls=%fused_computation.31 | loop fusion | bytes 4128772 | tf_op jit(solution)/shard_map/dynamic_slice | solution.py:338
  28.6 1.2 fusion.8
  29.9 1.8 %collective-permute-start.2 = (bf16[168,1536]{1,0:T(8,128)(2,1)S(1)}, bf16[168,1536]{1,0:T(8,128)(2,1)S(1)}, u32[]{:S(2)}, u32[]{:S(2)}) collective-permute-start(bf16[168,1536]{1,0:T(8,128)(2,1)S(1)} %get-tuple-element.189), channel_id=1, source_target_pairs={{0,128},{1,129},{2,130},{3,131},{4,132},{5,133},{6,134},{7,135},{8... | collective-permute-start | bytes 1548296 | tf_op jit(solution)/shard_map/ppermute | solution.py:30
  31.7 2.8 %collective-permute-start.3 = (bf16[168,1536]{1,0:T(8,128)(2,1)}, bf16[168,1536]{1,0:T(8,128)(2,1)}, u32[]{:S(2)}, u32[]{:S(2)}) collective-permute-start(bf16[168,1536]{1,0:T(8,128)(2,1)} %collective-permute-done.refs_0_), channel_id=1, source_target_pairs={{0,32},{1,33},{2,34},{3,35},{4,36},{5,37},{6,38},{7,39},{8,40},{9,... | collective-permute-start | bytes 1548296 | tf_op jit(solution)/shard_map/ppermute | solution.py:30
  34.6 1.1 collective-permute-start.4
  35.7 1.8 %collective-permute-start.5 = (bf16[168,1536]{1,0:T(8,128)(2,1)}, bf16[168,1536]{1,0:T(8,128)(2,1)S(1)}, u32[]{:S(2)}, u32[]{:S(2)}) collective-permute-start(bf16[168,1536]{1,0:T(8,128)(2,1)} %collective-permute-done.1.refs_4_), channel_id=1, source_target_pairs={{0,32},{1,33},{2,34},{3,35},{4,36},{5,37},{6,38},{7,39},{8,40},{9,... | collective-permute-start | bytes 1548296 | tf_op jit(solution)/shard_map/ppermute | solution.py:30
  37.5 1.2 collective-permute-done.2.refs_1_.refs_9_
  38.7 2.1 %collective-permute-done.3.refs_2_ = bf16[168,1536]{1,0:T(8,128)(2,1)} collective-permute-done((bf16[168,1536]{1,0:T(8,128)(2,1)}, bf16[168,1536]{1,0:T(8,128)(2,1)}, u32[]{:S(2)}, u32[]{:S(2)}) %collective-permute-start.3) | collective-permute-done | bytes 516128 | tf_op jit(solution)/shard_map/ppermute | solution.py:30
  41.4 2.8 %collective-permute-start.7 = (bf16[168,1536]{1,0:T(8,128)(2,1)S(1)}, bf16[168,1536]{1,0:T(8,128)(2,1)S(1)}, u32[]{:S(2)}, u32[]{:S(2)}) collective-permute-start(bf16[168,1536]{1,0:T(8,128)(2,1)S(1)} %collective-permute-done.2.refs_1_.refs_9_), channel_id=1, source_target_pairs={{0,32},{1,33},{2,34},{3,35},{4,36},{5,37},{6,38},{7,39},{8,40},{9,... | collective-permute-start | bytes 1548296 | tf_op jit(solution)/shard_map/ppermute | solution.py:30
  44.3 2.1 %collective-permute-done.5.refs_6_ = bf16[168,1536]{1,0:T(8,128)(2,1)S(1)} collective-permute-done((bf16[168,1536]{1,0:T(8,128)(2,1)}, bf16[168,1536]{1,0:T(8,128)(2,1)S(1)}, u32[]{:S(2)}, u32[]{:S(2)}) %collective-permute-start.5) | collective-permute-done | bytes 516128 | tf_op jit(solution)/shard_map/ppermute | solution.py:30
  47.7 2.8 %collective-permute-start.9 = (bf16[168,1536]{1,0:T(8,128)(2,1)S(1)}, bf16[168,1536]{1,0:T(8,128)(2,1)S(1)}, u32[]{:S(2)}, u32[]{:S(2)}) collective-permute-start(bf16[168,1536]{1,0:T(8,128)(2,1)S(1)} %collective-permute-done.4.refs_5_.refs_8_), channel_id=1, source_target_pairs={{0,32},{1,33},{2,34},{3,35},{4,36},{5,37},{6,38},{7,39},{8,40},{9,... | collective-permute-start | bytes 1548296 | tf_op jit(solution)/shard_map/ppermute | solution.py:30
  50.6 1.1 collective-permute-done.7.refs_3_.refs_1_
  52.5 2.8 %collective-permute-start.11 = (bf16[168,1536]{1,0:T(8,128)(2,1)S(1)}, bf16[168,1536]{1,0:T(8,128)(2,1)}, u32[]{:S(2)}, u32[]{:S(2)}) collective-permute-start(bf16[168,1536]{1,0:T(8,128)(2,1)S(1)} %collective-permute-done.6.refs_12_.refs_10_), channel_id=1, source_target_pairs={{0,32},{1,33},{2,34},{3,35},{4,36},{5,37},{6,38},{7,39},{8,40},{9,... | collective-permute-start | bytes 1548296 | tf_op jit(solution)/shard_map/ppermute | solution.py:30
  55.5 0.9 broadcast_select_fusion.1
  56.4 0.9 collective-permute-done.9.refs_7_.refs_10_
  57.3 2.5 %collective-permute-start.13 = (bf16[168,1536]{1,0:T(8,128)(2,1)}, bf16[168,1536]{1,0:T(8,128)(2,1)}, u32[]{:S(2)}, u32[]{:S(2)}) collective-permute-start(bf16[168,1536]{1,0:T(8,128)(2,1)} %broadcast_select_fusion.1), channel_id=1, source_target_pairs={{0,128},{1,129},{2,130},{3,131},{4,132},{5,133},{6,134},{7,135},{8... | collective-permute-start | bytes 1548296 | tf_op jit(solution)/shard_map/ppermute | solution.py:30
  59.9 2.8 %collective-permute-start.14 = (bf16[168,1536]{1,0:T(8,128)(2,1)}, bf16[168,1536]{1,0:T(8,128)(2,1)}, u32[]{:S(2)}, u32[]{:S(2)}) collective-permute-start(bf16[168,1536]{1,0:T(8,128)(2,1)} %collective-permute-done.8.refs_9_.refs_0_), channel_id=1, source_target_pairs={{0,32},{1,33},{2,34},{3,35},{4,36},{5,37},{6,38},{7,39},{8,40},{9,... | collective-permute-start | bytes 1548296 | tf_op jit(solution)/shard_map/ppermute | solution.py:30
  63.5 0.9 broadcast_select_fusion
  65.2 2.4 %collective-permute-start.15 = (bf16[168,1536]{1,0:T(8,128)(2,1)}, bf16[168,1536]{1,0:T(8,128)(2,1)S(1)}, u32[]{:S(2)}, u32[]{:S(2)}) collective-permute-start(bf16[168,1536]{1,0:T(8,128)(2,1)} %copy-done.4), channel_id=1, source_target_pairs={{0,32},{1,33},{2,34},{3,35},{4,36},{5,37},{6,38},{7,39},{8,40},{9,... | collective-permute-start | bytes 1548296 | tf_op jit(solution)/shard_map/ppermute | solution.py:30
  67.6 1.4 collective-permute-done.14.refs_11_.refs_2_
  69.6 2.8 %collective-permute-start.17 = (bf16[168,1536]{1,0:T(8,128)(2,1)}, bf16[168,1536]{1,0:T(8,128)(2,1)}, u32[]{:S(2)}, u32[]{:S(2)}) collective-permute-start(bf16[168,1536]{1,0:T(8,128)(2,1)} %collective-permute-done.13.refs_1_.refs_11_), channel_id=1, source_target_pairs={{0,32},{1,33},{2,34},{3,35},{4,36},{5,37},{6,38},{7,39},{8,40},{9,... | collective-permute-start | bytes 1548296 | tf_op jit(solution)/shard_map/ppermute | solution.py:30
  73.0 1.5 collective-permute-done.15.refs_15_.refs_6_
  75.0 2.9 %collective-permute-start.19 = (bf16[168,1536]{1,0:T(8,128)(2,1)}, bf16[168,1536]{1,0:T(8,128)(2,1)}, u32[]{:S(2)}, u32[]{:S(2)}) collective-permute-start(bf16[168,1536]{1,0:T(8,128)(2,1)} %collective-permute-done.12.refs_5_.refs_13_), channel_id=1, source_target_pairs={{0,32},{1,33},{2,34},{3,35},{4,36},{5,37},{6,38},{7,39},{8,40},{9,... | collective-permute-start | bytes 1548296 | tf_op jit(solution)/shard_map/ppermute | solution.py:30
  77.9 13.4 %shard_map.64.first_ref = bf16[1024,504]{1,0:T(8,128)(2,1)} custom-call(s32[3]{0:T(128)} %pad_add_fusion.place_ref, bf16[1024,3072]{1,0:T(8,128)(2,1)} %all-gather.2.cloned.1.call-done.rows_ref, bf16[168,1536]{1,0:T(8,128)(2,1)} %collective-permute-done.refs_0_, bf16[168,1536]{1,0:T(8,128)(2,1)} %copy-done.2, ...), custom_call_target="tpu_custom_call" | custom-call | flops 1000000 | bytes 100000 | tf_op jit(solution)/shard_map/pallas_call | solution.py:180
  91.3 0.9 collective-permute-start.20
  92.5 12.6 %shard_map.65 = (bf16[512,1536]{1,0:T(8,128)(2,1)}, bf16[512,1536]{1,0:T(8,128)(2,1)}, bf16[1024,168]{1,0:T(8,128)(2,1)}) custom-call(s32[3]{0:T(128)} %pad_add_fusion.place_ref, bf16[1024,3072]{1,0:T(8,128)(2,1)} %all-gather.2.cloned.1.call-done.rows_ref, bf16[1024,504]{1,0:T(8,128)(2,1)} %shard_map.64.first_ref, ...), custom_call_target="tpu_custom_call" | custom-call | flops 1000000 | bytes 100000 | tf_op jit(solution)/shard_map/pallas_call | solution.py:180
  105.5 3.7 %collective-permute-start.22 = (bf16[512,1536]{1,0:T(8,128)(2,1)}, bf16[512,1536]{1,0:T(8,128)(2,1)}, u32[]{:S(2)}, u32[]{:S(2)}) collective-permute-start(bf16[512,1536]{1,0:T(8,128)(2,1)} %get-tuple-element.326), channel_id=1, source_target_pairs={{0,16},{1,17},{2,18},{3,19},{4,20},{5,21},{6,22},{7,23},{8,24},{9,... | collective-permute-start | bytes 4718600 | tf_op jit(solution)/shard_map/ppermute | solution.py:30
  109.2 6.5 %shard_map.66 = (bf16[512,1536]{1,0:T(8,128)(2,1)}, bf16[512,1536]{1,0:T(8,128)(2,1)}) custom-call(s32[3]{0:T(128)} %pad_add_fusion.place_ref, bf16[1024,504]{1,0:T(8,128)(2,1)} %shard_map.64.first_ref, bf16[1024,168]{1,0:T(8,128)(2,1)} %get-tuple-element.327.last_ref, bf16[168,1536]{1,0:T(8,128)(2,1)} %get-tuple-element.328.refs_0_, ...), custom_call_target="tpu_custom_call" | custom-call | flops 1000000 | bytes 100000 | tf_op jit(solution)/shard_map/pallas_call | solution.py:180
  115.8 3.4 %add_convert_fusion = bf16[512,1536]{1,0:T(8,128)(2,1)} fusion(bf16[512,1536]{1,0:T(8,128)(2,1)} %collective-permute-done.22, bf16[512,1536]{1,0:T(8,128)(2,1)} %get-tuple-element.323), kind=kLoop, calls=%fused_computation.1 | loop fusion | flops 3145728 | bytes 4718592 | tf_op jit(solution)/shard_map/convert_element_type | solution.py:359
  119.5 1.3 add_convert_fusion.1
  120.9 2.6 %collective-permute-start.26 = (bf16[64,1536]{1,0:T(8,128)(2,1)S(1)}, bf16[64,1536]{1,0:T(8,128)(2,1)S(1)}, u32[]{:S(2)}, u32[]{:S(2)}) collective-permute-start(bf16[64,1536]{1,0:T(8,128)(2,1)S(1)} %get-tuple-element.336), channel_id=1, source_target_pairs={{0,3},{1,0},{2,1},{3,2},{4,7},{5,4},{6,5},{7,6},{8,11},{9,8},{10,9... | collective-permute-start | bytes 589832 | tf_op jit(solution)/shard_map/ppermute | solution.py:30
  123.5 2.4 %convert_add_fusion = (f32[128,1536]{1,0:T(8,128)S(1)}, f32[128,1536]{1,0:T(8,128)S(1)}, f32[128,1536]{1,0:T(8,128)}) fusion(bf16[512,1536]{1,0:T(8,128)(2,1)} %collective-permute-done.23, s32[]{:T(128)S(6)} %select_n.122, bf16[512,1536]{1,0:T(8,128)(2,1)S(1)} %copy-done.10, s32[]{:T(128)S(6)} %select_n.120, s32[]{:T(128)S(6)} %select_n.118), kind=kLoop, calls=%fused_computation.2 | loop fusion | flops 1769472 | bytes 4718604 | tf_op jit(solution)/shard_map/add | solution.py:367
  126.0 1.5 collective-permute-done.26
  128.3 3.4 %collective-permute-start.27 = (bf16[128,1536]{1,0:T(8,128)(2,1)}, bf16[128,1536]{1,0:T(8,128)(2,1)S(1)}, u32[]{:S(2)}, u32[]{:S(2)}) collective-permute-start(bf16[128,1536]{1,0:T(8,128)(2,1)} %pad_maximum_fusion.1), channel_id=1, source_target_pairs={{0,3},{1,0},{2,1},{3,2},{4,7},{5,4},{6,5},{7,6},{8,11},{9,8},{10,9... | collective-permute-start | bytes 1179656 | tf_op jit(solution)/shard_map/ppermute | solution.py:30
  131.7 3.2 %collective-permute-done.24 = bf16[64,1536]{1,0:T(8,128)(2,1)S(1)} collective-permute-done((bf16[64,1536]{1,0:T(8,128)(2,1)S(1)}, bf16[64,1536]{1,0:T(8,128)(2,1)S(1)}, u32[]{:S(2)}, u32[]{:S(2)}) %collective-permute-start.24) | collective-permute-done | bytes 196640 | tf_op jit(solution)/shard_map/ppermute | solution.py:30
  135.7 0.8 copy.7.share_ref
  136.5 0.9 fusion.3.places_ref
  137.4 9.8 %collective-permute-done.27.refs_3_ = bf16[128,1536]{1,0:T(8,128)(2,1)S(1)} collective-permute-done((bf16[128,1536]{1,0:T(8,128)(2,1)}, bf16[128,1536]{1,0:T(8,128)(2,1)S(1)}, u32[]{:S(2)}, u32[]{:S(2)}) %collective-permute-start.27) | collective-permute-done | bytes 393248 | tf_op jit(solution)/shard_map/ppermute | solution.py:30
  147.2 6.7 %collective-permute-done.25.refs_2_ = bf16[128,1536]{1,0:T(8,128)(2,1)} collective-permute-done((bf16[128,1536]{1,0:T(8,128)(2,1)}, bf16[128,1536]{1,0:T(8,128)(2,1)}, u32[]{:S(2)}, u32[]{:S(2)}) %collective-permute-start.25) | collective-permute-done | bytes 393248 | tf_op jit(solution)/shard_map/ppermute | solution.py:30
  154.0 5.7 %shard_map.67 = bf16[512,3072]{1,0:T(8,128)(2,1)} custom-call(s32[3]{0:T(128)} %pad_add_fusion.place_ref, bf16[512,32]{1,0:T(8,128)(2,1)} %fusion.3.places_ref, f32[512,1]{1,0:T(8,128)} %copy.7.share_ref, bf16[128,1536]{1,0:T(8,128)(2,1)} %reduce-scatter.2.cloned.1.call-done.refs_0_, f32[128,1536]{1,0:T(8,128)} %get-tuple-element.343.refs_1_, ...), custom_call_target="tpu_custom_call" | custom-call | tf_op jit(solution)/shard_map/pallas_call | solution.py:261
  (79 shorter events, 10.9 us)
Async XLA Ops:
  6.5 4.0 %copy-start = (bf16[512,3072]{1,0:T(8,128)(2,1)S(1)}, bf16[512,3072]{1,0:T(8,128)(2,1)}, u32[]{:S(2)}) copy-start(bf16[512,3072]{1,0:T(8,128)(2,1)} %param.6) | copy-start | bytes 9437188
  6.5 57.8 %all-gather.2.cloned.1.call-start = ((), (), s32[]{:S(2)}) async-start(), calls=%async_computation.1 | async-start | bytes 7077888 | tf_op jit(solution)/shard_map/all_gather | solution.py:346
  12.0 142.0 %reduce-scatter.2.cloned.1.call-start = ((), (), s32[]{:S(2)}) async-start(), calls=%async_computation.2 | async-start | bytes 1966080 | tf_op jit(solution)/shard_map/reduce_scatter | solution.py:360
  12.1 16.6 %collective-permute-start = (bf16[168,1536]{1,0:T(8,128)(2,1)}, bf16[168,1536]{1,0:T(8,128)(2,1)}, u32[]{:S(2)}, u32[]{:S(2)}) collective-permute-start(bf16[168,1536]{1,0:T(8,128)(2,1)} %dynamic-slice_bitcast_fusion), channel_id=1, source_target_pairs={{0,128},{1,129},{2,130},{3,131},{4,132},{5,133},{6,134},{7,135},{8... | collective-permute-start | bytes 1548296 | tf_op jit(solution)/shard_map/ppermute | solution.py:30
  20.4 14.1 %collective-permute-start.1 = (bf16[168,1536]{1,0:T(8,128)(2,1)}, bf16[168,1536]{1,0:T(8,128)(2,1)}, u32[]{:S(2)}, u32[]{:S(2)}) collective-permute-start(bf16[168,1536]{1,0:T(8,128)(2,1)} %dynamic_slice.53), channel_id=1, source_target_pairs={{0,128},{1,129},{2,130},{3,131},{4,132},{5,133},{6,134},{7,135},{8... | collective-permute-start | bytes 1548296 | tf_op jit(solution)/shard_map/ppermute | solution.py:30
  25.5 3.1 %copy-start.11 = (bf16[336,3072]{1,0:T(8,128)(2,1)S(1)}, bf16[336,3072]{1,0:T(8,128)(2,1)}, u32[]{:S(2)}) copy-start(bf16[336,3072]{1,0:T(8,128)(2,1)} %param.11) | copy-start | bytes 6193156
  28.6 5.9 %copy-start.7 = (bf16[168,1536]{1,0:T(8,128)(2,1)S(1)}, bf16[168,1536]{1,0:T(8,128)(2,1)}, u32[]{:S(2)}) copy-start(bf16[168,1536]{1,0:T(8,128)(2,1)} %dynamic_slice.55) | copy-start | bytes 1548292
  28.6 10.0 %copy-start.6 = (bf16[168,1536]{1,0:T(8,128)(2,1)S(1)}, bf16[168,1536]{1,0:T(8,128)(2,1)}, u32[]{:S(2)}) copy-start(bf16[168,1536]{1,0:T(8,128)(2,1)} %dynamic_slice.56) | copy-start | bytes 1548292
  29.9 8.8 %collective-permute-start.2 = (bf16[168,1536]{1,0:T(8,128)(2,1)S(1)}, bf16[168,1536]{1,0:T(8,128)(2,1)S(1)}, u32[]{:S(2)}, u32[]{:S(2)}) collective-permute-start(bf16[168,1536]{1,0:T(8,128)(2,1)S(1)} %get-tuple-element.189), channel_id=1, source_target_pairs={{0,128},{1,129},{2,130},{3,131},{4,132},{5,133},{6,134},{7,135},{8... | collective-permute-start | bytes 1548296 | tf_op jit(solution)/shard_map/ppermute | solution.py:30
  31.7 9.1 %collective-permute-start.3 = (bf16[168,1536]{1,0:T(8,128)(2,1)}, bf16[168,1536]{1,0:T(8,128)(2,1)}, u32[]{:S(2)}, u32[]{:S(2)}) collective-permute-start(bf16[168,1536]{1,0:T(8,128)(2,1)} %collective-permute-done.refs_0_), channel_id=1, source_target_pairs={{0,32},{1,33},{2,34},{3,35},{4,36},{5,37},{6,38},{7,39},{8,40},{9,... | collective-permute-start | bytes 1548296 | tf_op jit(solution)/shard_map/ppermute | solution.py:30
  34.6 9.7 %collective-permute-start.4 = (bf16[168,1536]{1,0:T(8,128)(2,1)S(1)}, bf16[168,1536]{1,0:T(8,128)(2,1)S(1)}, u32[]{:S(2)}, u32[]{:S(2)}) collective-permute-start(bf16[168,1536]{1,0:T(8,128)(2,1)S(1)} %broadcast_select_fusion.5), channel_id=1, source_target_pairs={{0,128},{1,129},{2,130},{3,131},{4,132},{5,133},{6,134},{7,135},{8... | collective-permute-start | bytes 1548296 | tf_op jit(solution)/shard_map/ppermute | solution.py:30
  35.7 10.7 %collective-permute-start.5 = (bf16[168,1536]{1,0:T(8,128)(2,1)}, bf16[168,1536]{1,0:T(8,128)(2,1)S(1)}, u32[]{:S(2)}, u32[]{:S(2)}) collective-permute-start(bf16[168,1536]{1,0:T(8,128)(2,1)} %collective-permute-done.1.refs_4_), channel_id=1, source_target_pairs={{0,32},{1,33},{2,34},{3,35},{4,36},{5,37},{6,38},{7,39},{8,40},{9,... | collective-permute-start | bytes 1548296 | tf_op jit(solution)/shard_map/ppermute | solution.py:30
  38.6 12.0 %copy-start.2 = (bf16[168,1536]{1,0:T(8,128)(2,1)}, bf16[168,1536]{1,0:T(8,128)(2,1)S(1)}, u32[]{:S(2)}) copy-start(bf16[168,1536]{1,0:T(8,128)(2,1)S(1)} %collective-permute-done.2.refs_1_.refs_9_) | copy-start | bytes 1548292
  40.8 9.7 %collective-permute-start.6 = (bf16[168,1536]{1,0:T(8,128)(2,1)S(1)}, bf16[168,1536]{1,0:T(8,128)(2,1)S(1)}, u32[]{:S(2)}, u32[]{:S(2)}) collective-permute-start(bf16[168,1536]{1,0:T(8,128)(2,1)S(1)} %broadcast_select_fusion.4), channel_id=1, source_target_pairs={{0,128},{1,129},{2,130},{3,131},{4,132},{5,133},{6,134},{7,135},{8... | collective-permute-start | bytes 1548296 | tf_op jit(solution)/shard_map/ppermute | solution.py:30
  41.4 10.4 %collective-permute-start.7 = (bf16[168,1536]{1,0:T(8,128)(2,1)S(1)}, bf16[168,1536]{1,0:T(8,128)(2,1)S(1)}, u32[]{:S(2)}, u32[]{:S(2)}) collective-permute-start(bf16[168,1536]{1,0:T(8,128)(2,1)S(1)} %collective-permute-done.2.refs_1_.refs_9_), channel_id=1, source_target_pairs={{0,32},{1,33},{2,34},{3,35},{4,36},{5,37},{6,38},{7,39},{8,40},{9,... | collective-permute-start | bytes 1548296 | tf_op jit(solution)/shard_map/ppermute | solution.py:30
  44.2 12.1 %copy-start.1 = (bf16[168,1536]{1,0:T(8,128)(2,1)}, bf16[168,1536]{1,0:T(8,128)(2,1)S(1)}, u32[]{:S(2)}) copy-start(bf16[168,1536]{1,0:T(8,128)(2,1)S(1)} %collective-permute-done.4.refs_5_.refs_8_) | copy-start | bytes 1548292
  46.4 0.8 copy-start.12
  47.1 8.3 %collective-permute-start.8 = (bf16[168,1536]{1,0:T(8,128)(2,1)S(1)}, bf16[168,1536]{1,0:T(8,128)(2,1)}, u32[]{:S(2)}, u32[]{:S(2)}) collective-permute-start(bf16[168,1536]{1,0:T(8,128)(2,1)S(1)} %broadcast_select_fusion.3), channel_id=1, source_target_pairs={{0,128},{1,129},{2,130},{3,131},{4,132},{5,133},{6,134},{7,135},{8... | collective-permute-start | bytes 1548296 | tf_op jit(solution)/shard_map/ppermute | solution.py:30
  47.7 9.6 %collective-permute-start.9 = (bf16[168,1536]{1,0:T(8,128)(2,1)S(1)}, bf16[168,1536]{1,0:T(8,128)(2,1)S(1)}, u32[]{:S(2)}, u32[]{:S(2)}) collective-permute-start(bf16[168,1536]{1,0:T(8,128)(2,1)S(1)} %collective-permute-done.4.refs_5_.refs_8_), channel_id=1, source_target_pairs={{0,32},{1,33},{2,34},{3,35},{4,36},{5,37},{6,38},{7,39},{8,40},{9,... | collective-permute-start | bytes 1548296 | tf_op jit(solution)/shard_map/ppermute | solution.py:30
  50.6 13.8 %copy-start.3 = (bf16[168,1536]{1,0:T(8,128)(2,1)}, bf16[168,1536]{1,0:T(8,128)(2,1)S(1)}, u32[]{:S(2)}) copy-start(bf16[168,1536]{1,0:T(8,128)(2,1)S(1)} %collective-permute-done.6.refs_12_.refs_10_) | copy-start | bytes 1548292
  51.8 12.5 %copy-start.8 = (bf16[168,1536]{1,0:T(8,128)(2,1)}, bf16[168,1536]{1,0:T(8,128)(2,1)S(1)}, u32[]{:S(2)}) copy-start(bf16[168,1536]{1,0:T(8,128)(2,1)S(1)} %collective-permute-done.7.refs_3_.refs_1_) | copy-start | bytes 1548292
  51.8 10.8 %collective-permute-start.10 = (bf16[168,1536]{1,0:T(8,128)(2,1)S(1)}, bf16[168,1536]{1,0:T(8,128)(2,1)S(1)}, u32[]{:S(2)}, u32[]{:S(2)}) collective-permute-start(bf16[168,1536]{1,0:T(8,128)(2,1)S(1)} %broadcast_select_fusion.2), channel_id=1, source_target_pairs={{0,128},{1,129},{2,130},{3,131},{4,132},{5,133},{6,134},{7,135},{8... | collective-permute-start | bytes 1548296 | tf_op jit(solution)/shard_map/ppermute | solution.py:30
  52.5 11.8 %collective-permute-start.11 = (bf16[168,1536]{1,0:T(8,128)(2,1)S(1)}, bf16[168,1536]{1,0:T(8,128)(2,1)}, u32[]{:S(2)}, u32[]{:S(2)}) collective-permute-start(bf16[168,1536]{1,0:T(8,128)(2,1)S(1)} %collective-permute-done.6.refs_12_.refs_10_), channel_id=1, source_target_pairs={{0,32},{1,33},{2,34},{3,35},{4,36},{5,37},{6,38},{7,39},{8,40},{9,... | collective-permute-start | bytes 1548296 | tf_op jit(solution)/shard_map/ppermute | solution.py:30
  57.3 7.0 %copy-start.5 = (bf16[168,1536]{1,0:T(8,128)(2,1)}, bf16[168,1536]{1,0:T(8,128)(2,1)S(1)}, u32[]{:S(2)}) copy-start(bf16[168,1536]{1,0:T(8,128)(2,1)S(1)} %collective-permute-done.9.refs_7_.refs_10_) | copy-start | bytes 1548292
  57.3 10.3 %collective-permute-start.13 = (bf16[168,1536]{1,0:T(8,128)(2,1)}, bf16[168,1536]{1,0:T(8,128)(2,1)}, u32[]{:S(2)}, u32[]{:S(2)}) collective-permute-start(bf16[168,1536]{1,0:T(8,128)(2,1)} %broadcast_select_fusion.1), channel_id=1, source_target_pairs={{0,128},{1,129},{2,130},{3,131},{4,132},{5,133},{6,134},{7,135},{8... | collective-permute-start | bytes 1548296 | tf_op jit(solution)/shard_map/ppermute | solution.py:30
  59.9 9.1 %collective-permute-start.14 = (bf16[168,1536]{1,0:T(8,128)(2,1)}, bf16[168,1536]{1,0:T(8,128)(2,1)}, u32[]{:S(2)}, u32[]{:S(2)}) collective-permute-start(bf16[168,1536]{1,0:T(8,128)(2,1)} %collective-permute-done.8.refs_9_.refs_0_), channel_id=1, source_target_pairs={{0,32},{1,33},{2,34},{3,35},{4,36},{5,37},{6,38},{7,39},{8,40},{9,... | collective-permute-start | bytes 1548296 | tf_op jit(solution)/shard_map/ppermute | solution.py:30
  62.6 0.8 copy-start.4
  64.4 8.6 %collective-permute-start.12 = (bf16[168,1536]{1,0:T(8,128)(2,1)}, bf16[168,1536]{1,0:T(8,128)(2,1)}, u32[]{:S(2)}, u32[]{:S(2)}) collective-permute-start(bf16[168,1536]{1,0:T(8,128)(2,1)} %broadcast_select_fusion), channel_id=1, source_target_pairs={{0,128},{1,129},{2,130},{3,131},{4,132},{5,133},{6,134},{7,135},{8... | collective-permute-start | bytes 1548296 | tf_op jit(solution)/shard_map/ppermute | solution.py:30
  65.2 9.3 %collective-permute-start.15 = (bf16[168,1536]{1,0:T(8,128)(2,1)}, bf16[168,1536]{1,0:T(8,128)(2,1)S(1)}, u32[]{:S(2)}, u32[]{:S(2)}) collective-permute-start(bf16[168,1536]{1,0:T(8,128)(2,1)} %copy-done.4), channel_id=1, source_target_pairs={{0,32},{1,33},{2,34},{3,35},{4,36},{5,37},{6,38},{7,39},{8,40},{9,... | collective-permute-start | bytes 1548296 | tf_op jit(solution)/shard_map/ppermute | solution.py:30
  69.0 22.3 %collective-permute-start.16 = (bf16[168,1536]{1,0:T(8,128)(2,1)}, bf16[168,1536]{1,0:T(8,128)(2,1)}, u32[]{:S(2)}, u32[]{:S(2)}) collective-permute-start(bf16[168,1536]{1,0:T(8,128)(2,1)} %collective-permute-done.13.refs_1_.refs_11_), channel_id=1, source_target_pairs={{0,128},{1,129},{2,130},{3,131},{4,132},{5,133},{6,134},{7,135},{8... | collective-permute-start | bytes 1548296 | tf_op jit(solution)/shard_map/ppermute | solution.py:30
  69.6 21.7 %collective-permute-start.17 = (bf16[168,1536]{1,0:T(8,128)(2,1)}, bf16[168,1536]{1,0:T(8,128)(2,1)}, u32[]{:S(2)}, u32[]{:S(2)}) collective-permute-start(bf16[168,1536]{1,0:T(8,128)(2,1)} %collective-permute-done.13.refs_1_.refs_11_), channel_id=1, source_target_pairs={{0,32},{1,33},{2,34},{3,35},{4,36},{5,37},{6,38},{7,39},{8,40},{9,... | collective-permute-start | bytes 1548296 | tf_op jit(solution)/shard_map/ppermute | solution.py:30
  74.5 3.4 %copy-start.9 = (bf16[168,1536]{1,0:T(8,128)(2,1)}, bf16[168,1536]{1,0:T(8,128)(2,1)S(1)}, u32[]{:S(2)}) copy-start(bf16[168,1536]{1,0:T(8,128)(2,1)S(1)} %collective-permute-done.15.refs_15_.refs_6_) | copy-start | bytes 1548292
  74.5 17.7 %collective-permute-start.18 = (bf16[168,1536]{1,0:T(8,128)(2,1)}, bf16[168,1536]{1,0:T(8,128)(2,1)}, u32[]{:S(2)}, u32[]{:S(2)}) collective-permute-start(bf16[168,1536]{1,0:T(8,128)(2,1)} %collective-permute-done.12.refs_5_.refs_13_), channel_id=1, source_target_pairs={{0,128},{1,129},{2,130},{3,131},{4,132},{5,133},{6,134},{7,135},{8... | collective-permute-start | bytes 1548296 | tf_op jit(solution)/shard_map/ppermute | solution.py:30
  75.0 17.2 %collective-permute-start.19 = (bf16[168,1536]{1,0:T(8,128)(2,1)}, bf16[168,1536]{1,0:T(8,128)(2,1)}, u32[]{:S(2)}, u32[]{:S(2)}) collective-permute-start(bf16[168,1536]{1,0:T(8,128)(2,1)} %collective-permute-done.12.refs_5_.refs_13_), channel_id=1, source_target_pairs={{0,32},{1,33},{2,34},{3,35},{4,36},{5,37},{6,38},{7,39},{8,40},{9,... | collective-permute-start | bytes 1548296 | tf_op jit(solution)/shard_map/ppermute | solution.py:30
  91.3 13.8 %collective-permute-start.20 = (bf16[168,1536]{1,0:T(8,128)(2,1)}, bf16[168,1536]{1,0:T(8,128)(2,1)S(1)}, u32[]{:S(2)}, u32[]{:S(2)}) collective-permute-start(bf16[168,1536]{1,0:T(8,128)(2,1)} %collective-permute-done.16.refs_12_), channel_id=1, source_target_pairs={{0,32},{1,33},{2,34},{3,35},{4,36},{5,37},{6,38},{7,39},{8,40},{9,... | collective-permute-start | bytes 1548296 | tf_op jit(solution)/shard_map/ppermute | solution.py:30
  92.2 13.3 %collective-permute-start.21 = (bf16[168,1536]{1,0:T(8,128)(2,1)}, bf16[168,1536]{1,0:T(8,128)(2,1)}, u32[]{:S(2)}, u32[]{:S(2)}) collective-permute-start(bf16[168,1536]{1,0:T(8,128)(2,1)} %collective-permute-done.18.refs_14_), channel_id=1, source_target_pairs={{0,32},{1,33},{2,34},{3,35},{4,36},{5,37},{6,38},{7,39},{8,40},{9,... | collective-permute-start | bytes 1548296 | tf_op jit(solution)/shard_map/ppermute | solution.py:30
  105.2 4.0 %copy-start.13 = (bf16[168,1536]{1,0:T(8,128)(2,1)}, bf16[168,1536]{1,0:T(8,128)(2,1)S(1)}, u32[]{:S(2)}) copy-start(bf16[168,1536]{1,0:T(8,128)(2,1)S(1)} %collective-permute-done.20.refs_4_) | copy-start | bytes 1548292
  105.5 10.3 %collective-permute-start.22 = (bf16[512,1536]{1,0:T(8,128)(2,1)}, bf16[512,1536]{1,0:T(8,128)(2,1)}, u32[]{:S(2)}, u32[]{:S(2)}) collective-permute-start(bf16[512,1536]{1,0:T(8,128)(2,1)} %get-tuple-element.326), channel_id=1, source_target_pairs={{0,16},{1,17},{2,18},{3,19},{4,20},{5,21},{6,22},{7,23},{8,24},{9,... | collective-permute-start | bytes 4718600 | tf_op jit(solution)/shard_map/ppermute | solution.py:30
  115.7 3.8 %collective-permute-start.23 = (bf16[512,1536]{1,0:T(8,128)(2,1)}, bf16[512,1536]{1,0:T(8,128)(2,1)}, u32[]{:S(2)}, u32[]{:S(2)}) collective-permute-start(bf16[512,1536]{1,0:T(8,128)(2,1)} %get-tuple-element.332), channel_id=1, source_target_pairs={{0,16},{1,17},{2,18},{3,19},{4,20},{5,21},{6,22},{7,23},{8,24},{9,... | collective-permute-start | bytes 4718600 | tf_op jit(solution)/shard_map/ppermute | solution.py:30
  119.3 4.2 %copy-start.10 = (bf16[512,1536]{1,0:T(8,128)(2,1)S(1)}, bf16[512,1536]{1,0:T(8,128)(2,1)}, u32[]{:S(2)}) copy-start(bf16[512,1536]{1,0:T(8,128)(2,1)} %get-tuple-element.333) | copy-start | bytes 4718596
  120.9 6.6 %collective-permute-start.26 = (bf16[64,1536]{1,0:T(8,128)(2,1)S(1)}, bf16[64,1536]{1,0:T(8,128)(2,1)S(1)}, u32[]{:S(2)}, u32[]{:S(2)}) collective-permute-start(bf16[64,1536]{1,0:T(8,128)(2,1)S(1)} %get-tuple-element.336), channel_id=1, source_target_pairs={{0,3},{1,0},{2,1},{3,2},{4,7},{5,4},{6,5},{7,6},{8,11},{9,8},{10,9... | collective-permute-start | bytes 589832 | tf_op jit(solution)/shard_map/ppermute | solution.py:30
  125.8 9.0 %collective-permute-start.24 = (bf16[64,1536]{1,0:T(8,128)(2,1)S(1)}, bf16[64,1536]{1,0:T(8,128)(2,1)S(1)}, u32[]{:S(2)}, u32[]{:S(2)}) collective-permute-start(bf16[64,1536]{1,0:T(8,128)(2,1)S(1)} %get-tuple-element.335), channel_id=1, source_target_pairs={{0,1},{1,2},{2,3},{3,0},{4,5},{5,6},{6,7},{7,4},{8,9},{9,10},{10,1... | collective-permute-start | bytes 589832 | tf_op jit(solution)/shard_map/ppermute | solution.py:30
  128.3 18.9 %collective-permute-start.27 = (bf16[128,1536]{1,0:T(8,128)(2,1)}, bf16[128,1536]{1,0:T(8,128)(2,1)S(1)}, u32[]{:S(2)}, u32[]{:S(2)}) collective-permute-start(bf16[128,1536]{1,0:T(8,128)(2,1)} %pad_maximum_fusion.1), channel_id=1, source_target_pairs={{0,3},{1,0},{2,1},{3,2},{4,7},{5,4},{6,5},{7,6},{8,11},{9,8},{10,9... | collective-permute-start | bytes 1179656 | tf_op jit(solution)/shard_map/ppermute | solution.py:30
  135.7 18.3 %collective-permute-start.25 = (bf16[128,1536]{1,0:T(8,128)(2,1)}, bf16[128,1536]{1,0:T(8,128)(2,1)}, u32[]{:S(2)}, u32[]{:S(2)}) collective-permute-start(bf16[128,1536]{1,0:T(8,128)(2,1)} %pad_maximum_fusion), channel_id=1, source_target_pairs={{0,1},{1,2},{2,3},{3,0},{4,5},{5,6},{6,7},{7,4},{8,9},{9,10},{10,1... | collective-permute-start | bytes 1179656 | tf_op jit(solution)/shard_map/ppermute | solution.py:30
  147.2 6.7 %copy-start.14 = (bf16[128,1536]{1,0:T(8,128)(2,1)}, bf16[128,1536]{1,0:T(8,128)(2,1)S(1)}, u32[]{:S(2)}) copy-start(bf16[128,1536]{1,0:T(8,128)(2,1)S(1)} %collective-permute-done.27.refs_3_) | copy-start | bytes 1179652
Sparse Core Ops, SparseCore 0:
  12.1 47.6 all-gather.1
  119.3 33.7 reduce-scatter.1

commit v2 on v1

--- a/solution.py
+++ b/solution.py
@@ -92,11 +92,14 @@
 
 
 def hidden_rows(copies, rows_kept, gate_kept, up_kept, out_ref):
-    for copy in copies:
-        copy.wait()
+    copies[0].wait()
 
     @pl.loop(0, 2 * ROWS, step=ROWS)
     def _(start):
+        @pl.when(start == ROWS)
+        def _():
+            copies[1].wait()
+
         span = pl.ds(pl.multiple_of(start, ROWS), ROWS)
         gate_pre, up_pre = (
             lax.dot_general(
@@ -249,26 +252,29 @@
         if index == 0:
             parts = [refs[0][...]]
         else:
-            expert_out = refs[1][...] + refs[2][...].astype(jnp.float32) + refs[3][...].astype(jnp.float32)
+            expert_out = sum((ref[...].astype(jnp.float32) for ref in refs[2:5]), refs[1][...].astype(jnp.float32))
             high = expert_out.astype(jnp.bfloat16)
             parts = [high, (expert_out - high.astype(jnp.float32)).astype(jnp.bfloat16)]
         picked = [jnp.dot(places, part, preferred_element_type=jnp.float32) for part in parts]
         out_ref[:, lanes] = (share_ref[...] * sum(picked[1:], picked[0])).astype(jnp.bfloat16)
 
 
-def spread(place, places, share, terms):
-    block = lambda shape: pl.BlockSpec(shape, lambda i, place: (i, 0))
+def spread(place, places, share, pair, terms):
+    def block(*shape):
+        return pl.BlockSpec(shape, lambda i, place: (i, 0))
+
+    own = pl.BlockSpec((CAP, SPLIT), lambda i, place: (place[3] * SPANS + i, 0))
     return pl.pallas_call(
         spread_kernel,
         out_shape=jax.ShapeDtypeStruct((SPANS * CT, 2 * SPLIT), jnp.bfloat16),
         grid_spec=pltpu.PrefetchScalarGridSpec(
             num_scalar_prefetch=1,
             grid=(SPANS,),
-            in_specs=[block((CT, CAP)), block((CT, 1))] + [block((CAP, term.shape[1])) for term in terms],
-            out_specs=block((CT, 2 * SPLIT)),
+            in_specs=[block(CT, CAP), block(CT, 1), block(CAP, SPLIT), own, own, block(CAP, SPLIT), block(CAP, SPLIT)],
+            out_specs=block(CT, 2 * SPLIT),
         ),
         compiler_params=pltpu.CompilerParams(vmem_limit_bytes=ALL_VMEM_BYTES),
-    )(place, places, share, *terms)
+    )(place, places, share, terms[0], *pair, *terms[1:])
 
 
 def on_device(tokens, expert_ids, gate_probs, gate_weight, up_weight, down_weight):
@@ -299,7 +305,7 @@
     shard = [gate_weight.T, up_weight.T, down_weight]
     order = [(0, near_units), (1, near_units), (2, near_units), (0, far_units), (1, far_units), (2, far_units)]
     own = [piece(shard[0], near_units, half)]
-    place = jnp.stack([first.astype(jnp.int32), core, half])
+    place = jnp.stack([first.astype(jnp.int32), core, half, x])
 
     def joined(*parts):
         return jnp.concatenate(parts, axis=0)
@@ -383,9 +389,9 @@
 
     pieces_there, pair_there = lax.optimization_barrier((far_pieces(pair_there), pair_there))
     near_there = near(pair_there, far(pieces_there))
-    terms = [out_here, summed(pair_there, 0), *near_there]
+    terms = [out_here, *near_there]
     places = jnp.swapaxes(selector, 1, 2).reshape(SPANS * CT, CAP).astype(jnp.bfloat16)
-    return spread(work["place"], places, gate_share[:, None], terms)
+    return spread(work["place"], places, gate_share[:, None], pair_there, terms)
 
 
 def solution(mesh):

time: 167 us -> 166 us (level)
  Pallas kernels: 38.2 us -> 36.4 us
    pallas_call x3, Pallas kernels: 32.5 us -> 30.7 us  [kernel_call(): pl.pallas_call(kernel, out_shape=[jax.ShapeDtypeStruct(shape, jnp.bfloat1...]
  transfers between devices with their start and end apart: 30 -> 30, of which waited for: 15 -> 16; matrix products, arithmetic and copies ran while one was open for 14% -> 13% of each run, Pallas kernels for 19% -> 19%
where the time goes in v2:
time: 166 us; the launch traced here: 165 us
  starting transfers between devices  51.5 us (31%)
  Pallas kernels  36.4 us (22%)
  waiting for transfers between devices  34.2 us (21%)
  other arithmetic  14.5 us (9%)
  between operations  13.7 us (8%)
  local copies, waits for them, and re-layouts  13.2 us (8%)
    ppermute x28, starting transfers between devices, moved(): return lax.ppermute(value, AXES, pairs)  51.5 us
    ppermute x28, waiting for transfers between devices, moved(): return lax.ppermute(value, AXES, pairs)  33.9 us
    pallas_call x3, Pallas kernels, kernel_call(): pl.pallas_call(kernel, out_shape=[jax.ShapeDtypeStruct(shape, jnp.bfloat1...  30.7 us
    dynamic_slice x4, local copies, waits for them, and re-layouts, piece(): return lax.dynamic_slice(array, (start, side * SPLIT), (UNITS, SPLIT))  7.51 us
    pallas_call x1, Pallas kernels, spread(): pl.pallas_call(spread_kernel, out_shape=jax.ShapeDtypeStruct((SPANS * CT,...  5.68 us
    convert_element_type x1, other arithmetic, on_device(): (mine_here.astype(jnp.float32) + moved(others_here, other_core).astype(jn...  3.41 us
  transfers between devices with their start and end apart: 30, of which 16 were waited for; matrix products, arithmetic and copies ran while one was open for 13% of the time, Pallas kernels for 19%

profile of v2, /device:TPU:1, one launch (start us, length us, event | category | flops | bytes accessed | tf_op | source)
XLA Modules:
  0.0 164.9 jit_solution(4301431791014117469)
XLA Ops:
  6.5 0.9 select_reduce_fusion
  7.5 1.2 reduce_window_sum.11
  8.7 1.9 %dynamic-slice_bitcast_fusion = bf16[168,1536]{1,0:T(8,128)(2,1)} fusion(bf16[3072,336]{0,1:T(8,128)(2,1)} %param.9, s32[]{:T(128)S(6)} %select_n.95, s32[]{:T(128)S(6)} %select_n.96), kind=kLoop, calls=%fused_computation.5 | loop fusion | bytes 1032200 | tf_op jit(solution)/shard_map/dynamic_slice | solution.py:303
  10.6 1.4 convolution_convert_fusion
  12.1 6.5 %collective-permute-start = (bf16[168,1536]{1,0:T(8,128)(2,1)}, bf16[168,1536]{1,0:T(8,128)(2,1)}, u32[]{:S(2)}, u32[]{:S(2)}) collective-permute-start(bf16[168,1536]{1,0:T(8,128)(2,1)} %dynamic-slice_bitcast_fusion), channel_id=1, source_target_pairs={{0,128},{1,129},{2,130},{3,131},{4,132},{5,133},{6,134},{7,135},{8... | collective-permute-start | bytes 1548296 | tf_op jit(solution)/shard_map/ppermute | solution.py:30
  18.6 1.9 %dynamic_slice.47 = bf16[168,1536]{1,0:T(8,128)(2,1)} dynamic-slice(bf16[336,3072]{1,0:T(8,128)(2,1)} %bitcast.20, s32[]{:T(128)S(6)} %select_n.96, s32[]{:T(128)S(6)} %select_n.95), dynamic_slice_sizes={168,1536} | dynamic-slice | bytes 1032196 | tf_op jit(solution)/shard_map/dynamic_slice | solution.py:303
  21.2 1.9 %dynamic_slice.49 = bf16[168,1536]{1,0:T(8,128)(2,1)} dynamic-slice(bf16[336,3072]{1,0:T(8,128)(2,1)} %bitcast.18, s32[]{:T(128)S(6)} %select_n.98, s32[]{:T(128)S(6)} %select_n.95), dynamic_slice_sizes={168,1536} | dynamic-slice | bytes 1032196 | tf_op jit(solution)/shard_map/dynamic_slice | solution.py:303
  23.1 1.9 %dynamic_slice.50 = bf16[168,1536]{1,0:T(8,128)(2,1)} dynamic-slice(bf16[336,3072]{1,0:T(8,128)(2,1)} %bitcast.21, s32[]{:T(128)S(6)} %select_n.98, s32[]{:T(128)S(6)} %select_n.95), dynamic_slice_sizes={168,1536} | dynamic-slice | bytes 1032196 | tf_op jit(solution)/shard_map/dynamic_slice | solution.py:303
  25.5 3.1 %constant_dynamic-slice_fusion = (bf16[168,3072]{1,0:T(8,128)(2,1)}, bf16[168,3072]{1,0:T(8,128)(2,1)}) fusion(bf16[336,3072]{1,0:T(8,128)(2,1)} %bitcast.22, s32[]{:T(128)S(6)} %select_n.96, bf16[336,3072]{1,0:T(8,128)(2,1)} %bitcast.19), kind=kLoop, calls=%fused_computation.30 | loop fusion | bytes 4128772 | tf_op jit(solution)/shard_map/dynamic_slice | solution.py:344
  28.7 1.2 fusion.8
  29.9 1.8 %collective-permute-start.2 = (bf16[168,1536]{1,0:T(8,128)(2,1)S(1)}, bf16[168,1536]{1,0:T(8,128)(2,1)S(1)}, u32[]{:S(2)}, u32[]{:S(2)}) collective-permute-start(bf16[168,1536]{1,0:T(8,128)(2,1)S(1)} %get-tuple-element.189), channel_id=1, source_target_pairs={{0,128},{1,129},{2,130},{3,131},{4,132},{5,133},{6,134},{7,135},{8... | collective-permute-start | bytes 1548296 | tf_op jit(solution)/shard_map/ppermute | solution.py:30
  31.7 2.8 %collective-permute-start.3 = (bf16[168,1536]{1,0:T(8,128)(2,1)}, bf16[168,1536]{1,0:T(8,128)(2,1)}, u32[]{:S(2)}, u32[]{:S(2)}) collective-permute-start(bf16[168,1536]{1,0:T(8,128)(2,1)} %collective-permute-done.refs_0_), channel_id=1, source_target_pairs={{0,32},{1,33},{2,34},{3,35},{4,36},{5,37},{6,38},{7,39},{8,40},{9,... | collective-permute-start | bytes 1548296 | tf_op jit(solution)/shard_map/ppermute | solution.py:30
  34.6 1.1 collective-permute-start.4
  35.7 1.8 %collective-permute-start.5 = (bf16[168,1536]{1,0:T(8,128)(2,1)}, bf16[168,1536]{1,0:T(8,128)(2,1)S(1)}, u32[]{:S(2)}, u32[]{:S(2)}) collective-permute-start(bf16[168,1536]{1,0:T(8,128)(2,1)} %collective-permute-done.1.refs_4_), channel_id=1, source_target_pairs={{0,32},{1,33},{2,34},{3,35},{4,36},{5,37},{6,38},{7,39},{8,40},{9,... | collective-permute-start | bytes 1548296 | tf_op jit(solution)/shard_map/ppermute | solution.py:30
  37.5 1.2 collective-permute-done.2.refs_1_.refs_9_
  38.8 2.1 %collective-permute-done.3.refs_2_ = bf16[168,1536]{1,0:T(8,128)(2,1)} collective-permute-done((bf16[168,1536]{1,0:T(8,128)(2,1)}, bf16[168,1536]{1,0:T(8,128)(2,1)}, u32[]{:S(2)}, u32[]{:S(2)}) %collective-permute-start.3) | collective-permute-done | bytes 516128 | tf_op jit(solution)/shard_map/ppermute | solution.py:30
  41.5 2.8 %collective-permute-start.7 = (bf16[168,1536]{1,0:T(8,128)(2,1)S(1)}, bf16[168,1536]{1,0:T(8,128)(2,1)S(1)}, u32[]{:S(2)}, u32[]{:S(2)}) collective-permute-start(bf16[168,1536]{1,0:T(8,128)(2,1)S(1)} %collective-permute-done.2.refs_1_.refs_9_), channel_id=1, source_target_pairs={{0,32},{1,33},{2,34},{3,35},{4,36},{5,37},{6,38},{7,39},{8,40},{9,... | collective-permute-start | bytes 1548296 | tf_op jit(solution)/shard_map/ppermute | solution.py:30
  44.3 2.1 %collective-permute-done.5.refs_6_ = bf16[168,1536]{1,0:T(8,128)(2,1)S(1)} collective-permute-done((bf16[168,1536]{1,0:T(8,128)(2,1)}, bf16[168,1536]{1,0:T(8,128)(2,1)S(1)}, u32[]{:S(2)}, u32[]{:S(2)}) %collective-permute-start.5) | collective-permute-done | bytes 516128 | tf_op jit(solution)/shard_map/ppermute | solution.py:30
  47.8 2.8 %collective-permute-start.9 = (bf16[168,1536]{1,0:T(8,128)(2,1)S(1)}, bf16[168,1536]{1,0:T(8,128)(2,1)S(1)}, u32[]{:S(2)}, u32[]{:S(2)}) collective-permute-start(bf16[168,1536]{1,0:T(8,128)(2,1)S(1)} %collective-permute-done.4.refs_5_.refs_8_), channel_id=1, source_target_pairs={{0,32},{1,33},{2,34},{3,35},{4,36},{5,37},{6,38},{7,39},{8,40},{9,... | collective-permute-start | bytes 1548296 | tf_op jit(solution)/shard_map/ppermute | solution.py:30
  50.7 1.1 collective-permute-done.7.refs_3_.refs_1_
  52.5 2.8 %collective-permute-start.11 = (bf16[168,1536]{1,0:T(8,128)(2,1)S(1)}, bf16[168,1536]{1,0:T(8,128)(2,1)}, u32[]{:S(2)}, u32[]{:S(2)}) collective-permute-start(bf16[168,1536]{1,0:T(8,128)(2,1)S(1)} %collective-permute-done.6.refs_12_.refs_10_), channel_id=1, source_target_pairs={{0,32},{1,33},{2,34},{3,35},{4,36},{5,37},{6,38},{7,39},{8,40},{9,... | collective-permute-start | bytes 1548296 | tf_op jit(solution)/shard_map/ppermute | solution.py:30
  55.6 0.9 broadcast_select_fusion.1
  56.4 0.9 collective-permute-done.9.refs_7_.refs_10_
  57.3 2.5 %collective-permute-start.13 = (bf16[168,1536]{1,0:T(8,128)(2,1)}, bf16[168,1536]{1,0:T(8,128)(2,1)}, u32[]{:S(2)}, u32[]{:S(2)}) collective-permute-start(bf16[168,1536]{1,0:T(8,128)(2,1)} %broadcast_select_fusion.1), channel_id=1, source_target_pairs={{0,128},{1,129},{2,130},{3,131},{4,132},{5,133},{6,134},{7,135},{8... | collective-permute-start | bytes 1548296 | tf_op jit(solution)/shard_map/ppermute | solution.py:30
  59.9 2.8 %collective-permute-start.14 = (bf16[168,1536]{1,0:T(8,128)(2,1)}, bf16[168,1536]{1,0:T(8,128)(2,1)}, u32[]{:S(2)}, u32[]{:S(2)}) collective-permute-start(bf16[168,1536]{1,0:T(8,128)(2,1)} %collective-permute-done.8.refs_9_.refs_0_), channel_id=1, source_target_pairs={{0,32},{1,33},{2,34},{3,35},{4,36},{5,37},{6,38},{7,39},{8,40},{9,... | collective-permute-start | bytes 1548296 | tf_op jit(solution)/shard_map/ppermute | solution.py:30
  63.5 0.9 broadcast_select_fusion
  65.2 2.4 %collective-permute-start.15 = (bf16[168,1536]{1,0:T(8,128)(2,1)}, bf16[168,1536]{1,0:T(8,128)(2,1)S(1)}, u32[]{:S(2)}, u32[]{:S(2)}) collective-permute-start(bf16[168,1536]{1,0:T(8,128)(2,1)} %copy-done.5), channel_id=1, source_target_pairs={{0,32},{1,33},{2,34},{3,35},{4,36},{5,37},{6,38},{7,39},{8,40},{9,... | collective-permute-start | bytes 1548296 | tf_op jit(solution)/shard_map/ppermute | solution.py:30
  67.6 1.4 collective-permute-done.14.refs_11_.refs_2_
  69.7 2.8 %collective-permute-start.17 = (bf16[168,1536]{1,0:T(8,128)(2,1)}, bf16[168,1536]{1,0:T(8,128)(2,1)}, u32[]{:S(2)}, u32[]{:S(2)}) collective-permute-start(bf16[168,1536]{1,0:T(8,128)(2,1)} %collective-permute-done.13.refs_1_.refs_11_), channel_id=1, source_target_pairs={{0,32},{1,33},{2,34},{3,35},{4,36},{5,37},{6,38},{7,39},{8,40},{9,... | collective-permute-start | bytes 1548296 | tf_op jit(solution)/shard_map/ppermute | solution.py:30
  73.0 1.5 collective-permute-done.15.refs_15_.refs_6_
  75.1 2.9 %collective-permute-start.19 = (bf16[168,1536]{1,0:T(8,128)(2,1)}, bf16[168,1536]{1,0:T(8,128)(2,1)}, u32[]{:S(2)}, u32[]{:S(2)}) collective-permute-start(bf16[168,1536]{1,0:T(8,128)(2,1)} %collective-permute-done.12.refs_5_.refs_13_), channel_id=1, source_target_pairs={{0,32},{1,33},{2,34},{3,35},{4,36},{5,37},{6,38},{7,39},{8,40},{9,... | collective-permute-start | bytes 1548296 | tf_op jit(solution)/shard_map/ppermute | solution.py:30
  78.0 12.5 %shard_map.64.first_ref = bf16[1024,504]{1,0:T(8,128)(2,1)} custom-call(s32[4]{0:T(128)} %pad_add_fusion.place_ref, bf16[1024,3072]{1,0:T(8,128)(2,1)} %all-gather.2.cloned.1.call-done.rows_ref, bf16[168,1536]{1,0:T(8,128)(2,1)} %collective-permute-done.refs_0_, bf16[168,1536]{1,0:T(8,128)(2,1)} %copy-done.2, ...), custom_call_target="tpu_custom_call" | custom-call | flops 1000000 | bytes 100000 | tf_op jit(solution)/shard_map/pallas_call | solution.py:183
  90.5 0.9 collective-permute-start.20
  91.7 11.7 %shard_map.65 = (bf16[512,1536]{1,0:T(8,128)(2,1)}, bf16[512,1536]{1,0:T(8,128)(2,1)}, bf16[1024,168]{1,0:T(8,128)(2,1)}) custom-call(s32[4]{0:T(128)} %pad_add_fusion.place_ref, bf16[1024,3072]{1,0:T(8,128)(2,1)} %all-gather.2.cloned.1.call-done.rows_ref, bf16[1024,504]{1,0:T(8,128)(2,1)} %shard_map.64.first_ref, ...), custom_call_target="tpu_custom_call" | custom-call | flops 1000000 | bytes 100000 | tf_op jit(solution)/shard_map/pallas_call | solution.py:183
  103.4 1.3 collective-permute-done.21.refs_6_
  104.6 3.7 %collective-permute-start.22 = (bf16[512,1536]{1,0:T(8,128)(2,1)}, bf16[512,1536]{1,0:T(8,128)(2,1)}, u32[]{:S(2)}, u32[]{:S(2)}) collective-permute-start(bf16[512,1536]{1,0:T(8,128)(2,1)} %get-tuple-element.326), channel_id=1, source_target_pairs={{0,16},{1,17},{2,18},{3,19},{4,20},{5,21},{6,22},{7,23},{8,24},{9,... | collective-permute-start | bytes 4718600 | tf_op jit(solution)/shard_map/ppermute | solution.py:30
  108.4 6.5 %shard_map.66 = (bf16[512,1536]{1,0:T(8,128)(2,1)}, bf16[512,1536]{1,0:T(8,128)(2,1)}) custom-call(s32[4]{0:T(128)} %pad_add_fusion.place_ref, bf16[1024,504]{1,0:T(8,128)(2,1)} %shard_map.64.first_ref, bf16[1024,168]{1,0:T(8,128)(2,1)} %get-tuple-element.327.last_ref, bf16[168,1536]{1,0:T(8,128)(2,1)} %get-tuple-element.328.refs_0_, ...), custom_call_target="tpu_custom_call" | custom-call | flops 1000000 | bytes 100000 | tf_op jit(solution)/shard_map/pallas_call | solution.py:183
  115.0 3.4 %add_convert_fusion = bf16[512,1536]{1,0:T(8,128)(2,1)} fusion(bf16[512,1536]{1,0:T(8,128)(2,1)} %collective-permute-done.22, bf16[512,1536]{1,0:T(8,128)(2,1)} %get-tuple-element.323), kind=kLoop, calls=%fused_computation.1 | loop fusion | flops 3145728 | bytes 4718592 | tf_op jit(solution)/shard_map/convert_element_type | solution.py:365
  118.8 1.3 add_convert_fusion.1
  120.1 2.5 %collective-permute-start.26 = (bf16[64,1536]{1,0:T(8,128)(2,1)S(1)}, bf16[64,1536]{1,0:T(8,128)(2,1)S(1)}, u32[]{:S(2)}, u32[]{:S(2)}) collective-permute-start(bf16[64,1536]{1,0:T(8,128)(2,1)S(1)} %get-tuple-element.336), channel_id=1, source_target_pairs={{0,3},{1,0},{2,1},{3,2},{4,7},{5,4},{6,5},{7,6},{8,11},{9,8},{10,9... | collective-permute-start | bytes 589832 | tf_op jit(solution)/shard_map/ppermute | solution.py:30
  122.7 1.3 convert_add_fusion
  124.2 2.6 %collective-permute-done.26 = bf16[64,1536]{1,0:T(8,128)(2,1)S(1)} collective-permute-done((bf16[64,1536]{1,0:T(8,128)(2,1)S(1)}, bf16[64,1536]{1,0:T(8,128)(2,1)S(1)}, u32[]{:S(2)}, u32[]{:S(2)}) %collective-permute-start.26) | collective-permute-done | bytes 196640 | tf_op jit(solution)/shard_map/ppermute | solution.py:30
  127.5 3.4 %collective-permute-start.27 = (bf16[128,1536]{1,0:T(8,128)(2,1)}, bf16[128,1536]{1,0:T(8,128)(2,1)S(1)}, u32[]{:S(2)}, u32[]{:S(2)}) collective-permute-start(bf16[128,1536]{1,0:T(8,128)(2,1)} %pad_maximum_fusion.1), channel_id=1, source_target_pairs={{0,3},{1,0},{2,1},{3,2},{4,7},{5,4},{6,5},{7,6},{8,11},{9,8},{10,9... | collective-permute-start | bytes 1179656 | tf_op jit(solution)/shard_map/ppermute | solution.py:30
  130.9 1.1 collective-permute-done.24
  133.7 0.9 fusion.3.places_ref
  134.6 11.9 %collective-permute-done.27.refs_4_ = bf16[128,1536]{1,0:T(8,128)(2,1)S(1)} collective-permute-done((bf16[128,1536]{1,0:T(8,128)(2,1)}, bf16[128,1536]{1,0:T(8,128)(2,1)S(1)}, u32[]{:S(2)}, u32[]{:S(2)}) %collective-permute-start.27) | collective-permute-done | bytes 393248 | tf_op jit(solution)/shard_map/ppermute | solution.py:30
  146.5 5.7 %collective-permute-done.25.refs_3_ = bf16[128,1536]{1,0:T(8,128)(2,1)} collective-permute-done((bf16[128,1536]{1,0:T(8,128)(2,1)}, bf16[128,1536]{1,0:T(8,128)(2,1)}, u32[]{:S(2)}, u32[]{:S(2)}) %collective-permute-start.25) | collective-permute-done | bytes 393248 | tf_op jit(solution)/shard_map/ppermute | solution.py:30
  152.4 5.7 %shard_map.67 = bf16[512,3072]{1,0:T(8,128)(2,1)} custom-call(s32[4]{0:T(128)} %pad_add_fusion.place_ref, bf16[512,32]{1,0:T(8,128)(2,1)} %fusion.3.places_ref, f32[512,1]{1,0:T(8,128)} %copy.7.share_ref, bf16[128,1536]{1,0:T(8,128)(2,1)} %reduce-scatter.2.cloned.1.call-done.refs_0_, bf16[512,1536]{1,0:T(8,128)(2,1)} %get-tuple-element.333.refs_1_, ...), custom_call_target="tpu_custom_call" | custom-call | tf_op jit(solution)/shard_map/pallas_call | solution.py:267
  (79 shorter events, 11.7 us)
Async XLA Ops:
  6.5 4.0 %copy-start = (bf16[512,3072]{1,0:T(8,128)(2,1)S(1)}, bf16[512,3072]{1,0:T(8,128)(2,1)}, u32[]{:S(2)}) copy-start(bf16[512,3072]{1,0:T(8,128)(2,1)} %param.6) | copy-start | bytes 9437188
  6.5 57.8 %all-gather.2.cloned.1.call-start = ((), (), s32[]{:S(2)}) async-start(), calls=%async_computation.1 | async-start | bytes 7077888 | tf_op jit(solution)/shard_map/all_gather | solution.py:352
  12.0 140.4 %reduce-scatter.2.cloned.1.call-start = ((), (), s32[]{:S(2)}) async-start(), calls=%async_computation.2 | async-start | bytes 1966080 | tf_op jit(solution)/shard_map/reduce_scatter | solution.py:366
  12.1 16.6 %collective-permute-start = (bf16[168,1536]{1,0:T(8,128)(2,1)}, bf16[168,1536]{1,0:T(8,128)(2,1)}, u32[]{:S(2)}, u32[]{:S(2)}) collective-permute-start(bf16[168,1536]{1,0:T(8,128)(2,1)} %dynamic-slice_bitcast_fusion), channel_id=1, source_target_pairs={{0,128},{1,129},{2,130},{3,131},{4,132},{5,133},{6,134},{7,135},{8... | collective-permute-start | bytes 1548296 | tf_op jit(solution)/shard_map/ppermute | solution.py:30
  20.4 14.1 %collective-permute-start.1 = (bf16[168,1536]{1,0:T(8,128)(2,1)}, bf16[168,1536]{1,0:T(8,128)(2,1)}, u32[]{:S(2)}, u32[]{:S(2)}) collective-permute-start(bf16[168,1536]{1,0:T(8,128)(2,1)} %dynamic_slice.47), channel_id=1, source_target_pairs={{0,128},{1,129},{2,130},{3,131},{4,132},{5,133},{6,134},{7,135},{8... | collective-permute-start | bytes 1548296 | tf_op jit(solution)/shard_map/ppermute | solution.py:30
  25.5 3.1 %copy-start.11 = (bf16[336,3072]{1,0:T(8,128)(2,1)S(1)}, bf16[336,3072]{1,0:T(8,128)(2,1)}, u32[]{:S(2)}) copy-start(bf16[336,3072]{1,0:T(8,128)(2,1)} %param.11) | copy-start | bytes 6193156
  28.7 5.9 %copy-start.8 = (bf16[168,1536]{1,0:T(8,128)(2,1)S(1)}, bf16[168,1536]{1,0:T(8,128)(2,1)}, u32[]{:S(2)}) copy-start(bf16[168,1536]{1,0:T(8,128)(2,1)} %dynamic_slice.49) | copy-start | bytes 1548292
  28.7 10.0 %copy-start.7 = (bf16[168,1536]{1,0:T(8,128)(2,1)S(1)}, bf16[168,1536]{1,0:T(8,128)(2,1)}, u32[]{:S(2)}) copy-start(bf16[168,1536]{1,0:T(8,128)(2,1)} %dynamic_slice.50) | copy-start | bytes 1548292
  29.9 8.8 %collective-permute-start.2 = (bf16[168,1536]{1,0:T(8,128)(2,1)S(1)}, bf16[168,1536]{1,0:T(8,128)(2,1)S(1)}, u32[]{:S(2)}, u32[]{:S(2)}) collective-permute-start(bf16[168,1536]{1,0:T(8,128)(2,1)S(1)} %get-tuple-element.189), channel_id=1, source_target_pairs={{0,128},{1,129},{2,130},{3,131},{4,132},{5,133},{6,134},{7,135},{8... | collective-permute-start | bytes 1548296 | tf_op jit(solution)/shard_map/ppermute | solution.py:30
  31.7 9.1 %collective-permute-start.3 = (bf16[168,1536]{1,0:T(8,128)(2,1)}, bf16[168,1536]{1,0:T(8,128)(2,1)}, u32[]{:S(2)}, u32[]{:S(2)}) collective-permute-start(bf16[168,1536]{1,0:T(8,128)(2,1)} %collective-permute-done.refs_0_), channel_id=1, source_target_pairs={{0,32},{1,33},{2,34},{3,35},{4,36},{5,37},{6,38},{7,39},{8,40},{9,... | collective-permute-start | bytes 1548296 | tf_op jit(solution)/shard_map/ppermute | solution.py:30
  34.6 9.7 %collective-permute-start.4 = (bf16[168,1536]{1,0:T(8,128)(2,1)S(1)}, bf16[168,1536]{1,0:T(8,128)(2,1)S(1)}, u32[]{:S(2)}, u32[]{:S(2)}) collective-permute-start(bf16[168,1536]{1,0:T(8,128)(2,1)S(1)} %broadcast_select_fusion.5), channel_id=1, source_target_pairs={{0,128},{1,129},{2,130},{3,131},{4,132},{5,133},{6,134},{7,135},{8... | collective-permute-start | bytes 1548296 | tf_op jit(solution)/shard_map/ppermute | solution.py:30
  35.7 10.7 %collective-permute-start.5 = (bf16[168,1536]{1,0:T(8,128)(2,1)}, bf16[168,1536]{1,0:T(8,128)(2,1)S(1)}, u32[]{:S(2)}, u32[]{:S(2)}) collective-permute-start(bf16[168,1536]{1,0:T(8,128)(2,1)} %collective-permute-done.1.refs_4_), channel_id=1, source_target_pairs={{0,32},{1,33},{2,34},{3,35},{4,36},{5,37},{6,38},{7,39},{8,40},{9,... | collective-permute-start | bytes 1548296 | tf_op jit(solution)/shard_map/ppermute | solution.py:30
  38.7 12.0 %copy-start.2 = (bf16[168,1536]{1,0:T(8,128)(2,1)}, bf16[168,1536]{1,0:T(8,128)(2,1)S(1)}, u32[]{:S(2)}) copy-start(bf16[168,1536]{1,0:T(8,128)(2,1)S(1)} %collective-permute-done.2.refs_1_.refs_9_) | copy-start | bytes 1548292
  40.9 9.8 %collective-permute-start.6 = (bf16[168,1536]{1,0:T(8,128)(2,1)S(1)}, bf16[168,1536]{1,0:T(8,128)(2,1)S(1)}, u32[]{:S(2)}, u32[]{:S(2)}) collective-permute-start(bf16[168,1536]{1,0:T(8,128)(2,1)S(1)} %broadcast_select_fusion.4), channel_id=1, source_target_pairs={{0,128},{1,129},{2,130},{3,131},{4,132},{5,133},{6,134},{7,135},{8... | collective-permute-start | bytes 1548296 | tf_op jit(solution)/shard_map/ppermute | solution.py:30
  41.5 10.4 %collective-permute-start.7 = (bf16[168,1536]{1,0:T(8,128)(2,1)S(1)}, bf16[168,1536]{1,0:T(8,128)(2,1)S(1)}, u32[]{:S(2)}, u32[]{:S(2)}) collective-permute-start(bf16[168,1536]{1,0:T(8,128)(2,1)S(1)} %collective-permute-done.2.refs_1_.refs_9_), channel_id=1, source_target_pairs={{0,32},{1,33},{2,34},{3,35},{4,36},{5,37},{6,38},{7,39},{8,40},{9,... | collective-permute-start | bytes 1548296 | tf_op jit(solution)/shard_map/ppermute | solution.py:30
  44.3 12.1 %copy-start.1 = (bf16[168,1536]{1,0:T(8,128)(2,1)}, bf16[168,1536]{1,0:T(8,128)(2,1)S(1)}, u32[]{:S(2)}) copy-start(bf16[168,1536]{1,0:T(8,128)(2,1)S(1)} %collective-permute-done.4.refs_5_.refs_8_) | copy-start | bytes 1548292
  46.4 0.8 copy-start.12
  47.2 8.3 %collective-permute-start.8 = (bf16[168,1536]{1,0:T(8,128)(2,1)S(1)}, bf16[168,1536]{1,0:T(8,128)(2,1)}, u32[]{:S(2)}, u32[]{:S(2)}) collective-permute-start(bf16[168,1536]{1,0:T(8,128)(2,1)S(1)} %broadcast_select_fusion.3), channel_id=1, source_target_pairs={{0,128},{1,129},{2,130},{3,131},{4,132},{5,133},{6,134},{7,135},{8... | collective-permute-start | bytes 1548296 | tf_op jit(solution)/shard_map/ppermute | solution.py:30
  47.8 9.5 %collective-permute-start.9 = (bf16[168,1536]{1,0:T(8,128)(2,1)S(1)}, bf16[168,1536]{1,0:T(8,128)(2,1)S(1)}, u32[]{:S(2)}, u32[]{:S(2)}) collective-permute-start(bf16[168,1536]{1,0:T(8,128)(2,1)S(1)} %collective-permute-done.4.refs_5_.refs_8_), channel_id=1, source_target_pairs={{0,32},{1,33},{2,34},{3,35},{4,36},{5,37},{6,38},{7,39},{8,40},{9,... | collective-permute-start | bytes 1548296 | tf_op jit(solution)/shard_map/ppermute | solution.py:30
  50.6 13.7 %copy-start.3 = (bf16[168,1536]{1,0:T(8,128)(2,1)}, bf16[168,1536]{1,0:T(8,128)(2,1)S(1)}, u32[]{:S(2)}) copy-start(bf16[168,1536]{1,0:T(8,128)(2,1)S(1)} %collective-permute-done.6.refs_12_.refs_10_) | copy-start | bytes 1548292
  51.8 12.5 %copy-start.9 = (bf16[168,1536]{1,0:T(8,128)(2,1)}, bf16[168,1536]{1,0:T(8,128)(2,1)S(1)}, u32[]{:S(2)}) copy-start(bf16[168,1536]{1,0:T(8,128)(2,1)S(1)} %collective-permute-done.7.refs_3_.refs_1_) | copy-start | bytes 1548292
  51.8 10.8 %collective-permute-start.10 = (bf16[168,1536]{1,0:T(8,128)(2,1)S(1)}, bf16[168,1536]{1,0:T(8,128)(2,1)S(1)}, u32[]{:S(2)}, u32[]{:S(2)}) collective-permute-start(bf16[168,1536]{1,0:T(8,128)(2,1)S(1)} %broadcast_select_fusion.2), channel_id=1, source_target_pairs={{0,128},{1,129},{2,130},{3,131},{4,132},{5,133},{6,134},{7,135},{8... | collective-permute-start | bytes 1548296 | tf_op jit(solution)/shard_map/ppermute | solution.py:30
  52.5 11.8 %collective-permute-start.11 = (bf16[168,1536]{1,0:T(8,128)(2,1)S(1)}, bf16[168,1536]{1,0:T(8,128)(2,1)}, u32[]{:S(2)}, u32[]{:S(2)}) collective-permute-start(bf16[168,1536]{1,0:T(8,128)(2,1)S(1)} %collective-permute-done.6.refs_12_.refs_10_), channel_id=1, source_target_pairs={{0,32},{1,33},{2,34},{3,35},{4,36},{5,37},{6,38},{7,39},{8,40},{9,... | collective-permute-start | bytes 1548296 | tf_op jit(solution)/shard_map/ppermute | solution.py:30
  57.3 7.0 %copy-start.6 = (bf16[168,1536]{1,0:T(8,128)(2,1)}, bf16[168,1536]{1,0:T(8,128)(2,1)S(1)}, u32[]{:S(2)}) copy-start(bf16[168,1536]{1,0:T(8,128)(2,1)S(1)} %collective-permute-done.9.refs_7_.refs_10_) | copy-start | bytes 1548292
  57.3 10.2 %collective-permute-start.13 = (bf16[168,1536]{1,0:T(8,128)(2,1)}, bf16[168,1536]{1,0:T(8,128)(2,1)}, u32[]{:S(2)}, u32[]{:S(2)}) collective-permute-start(bf16[168,1536]{1,0:T(8,128)(2,1)} %broadcast_select_fusion.1), channel_id=1, source_target_pairs={{0,128},{1,129},{2,130},{3,131},{4,132},{5,133},{6,134},{7,135},{8... | collective-permute-start | bytes 1548296 | tf_op jit(solution)/shard_map/ppermute | solution.py:30
  59.9 9.1 %collective-permute-start.14 = (bf16[168,1536]{1,0:T(8,128)(2,1)}, bf16[168,1536]{1,0:T(8,128)(2,1)}, u32[]{:S(2)}, u32[]{:S(2)}) collective-permute-start(bf16[168,1536]{1,0:T(8,128)(2,1)} %collective-permute-done.8.refs_9_.refs_0_), channel_id=1, source_target_pairs={{0,32},{1,33},{2,34},{3,35},{4,36},{5,37},{6,38},{7,39},{8,40},{9,... | collective-permute-start | bytes 1548296 | tf_op jit(solution)/shard_map/ppermute | solution.py:30
  62.6 0.8 copy-start.5
  64.4 8.6 %collective-permute-start.12 = (bf16[168,1536]{1,0:T(8,128)(2,1)}, bf16[168,1536]{1,0:T(8,128)(2,1)}, u32[]{:S(2)}, u32[]{:S(2)}) collective-permute-start(bf16[168,1536]{1,0:T(8,128)(2,1)} %broadcast_select_fusion), channel_id=1, source_target_pairs={{0,128},{1,129},{2,130},{3,131},{4,132},{5,133},{6,134},{7,135},{8... | collective-permute-start | bytes 1548296 | tf_op jit(solution)/shard_map/ppermute | solution.py:30
  65.2 9.3 %collective-permute-start.15 = (bf16[168,1536]{1,0:T(8,128)(2,1)}, bf16[168,1536]{1,0:T(8,128)(2,1)S(1)}, u32[]{:S(2)}, u32[]{:S(2)}) collective-permute-start(bf16[168,1536]{1,0:T(8,128)(2,1)} %copy-done.5), channel_id=1, source_target_pairs={{0,32},{1,33},{2,34},{3,35},{4,36},{5,37},{6,38},{7,39},{8,40},{9,... | collective-permute-start | bytes 1548296 | tf_op jit(solution)/shard_map/ppermute | solution.py:30
  69.0 21.5 %collective-permute-start.16 = (bf16[168,1536]{1,0:T(8,128)(2,1)}, bf16[168,1536]{1,0:T(8,128)(2,1)}, u32[]{:S(2)}, u32[]{:S(2)}) collective-permute-start(bf16[168,1536]{1,0:T(8,128)(2,1)} %collective-permute-done.13.refs_1_.refs_11_), channel_id=1, source_target_pairs={{0,128},{1,129},{2,130},{3,131},{4,132},{5,133},{6,134},{7,135},{8... | collective-permute-start | bytes 1548296 | tf_op jit(solution)/shard_map/ppermute | solution.py:30
  69.7 20.8 %collective-permute-start.17 = (bf16[168,1536]{1,0:T(8,128)(2,1)}, bf16[168,1536]{1,0:T(8,128)(2,1)}, u32[]{:S(2)}, u32[]{:S(2)}) collective-permute-start(bf16[168,1536]{1,0:T(8,128)(2,1)} %collective-permute-done.13.refs_1_.refs_11_), channel_id=1, source_target_pairs={{0,32},{1,33},{2,34},{3,35},{4,36},{5,37},{6,38},{7,39},{8,40},{9,... | collective-permute-start | bytes 1548296 | tf_op jit(solution)/shard_map/ppermute | solution.py:30
  74.5 3.4 %copy-start.10 = (bf16[168,1536]{1,0:T(8,128)(2,1)}, bf16[168,1536]{1,0:T(8,128)(2,1)S(1)}, u32[]{:S(2)}) copy-start(bf16[168,1536]{1,0:T(8,128)(2,1)S(1)} %collective-permute-done.15.refs_15_.refs_6_) | copy-start | bytes 1548292
  74.5 16.8 %collective-permute-start.18 = (bf16[168,1536]{1,0:T(8,128)(2,1)}, bf16[168,1536]{1,0:T(8,128)(2,1)}, u32[]{:S(2)}, u32[]{:S(2)}) collective-permute-start(bf16[168,1536]{1,0:T(8,128)(2,1)} %collective-permute-done.12.refs_5_.refs_13_), channel_id=1, source_target_pairs={{0,128},{1,129},{2,130},{3,131},{4,132},{5,133},{6,134},{7,135},{8... | collective-permute-start | bytes 1548296 | tf_op jit(solution)/shard_map/ppermute | solution.py:30
  75.1 16.3 %collective-permute-start.19 = (bf16[168,1536]{1,0:T(8,128)(2,1)}, bf16[168,1536]{1,0:T(8,128)(2,1)}, u32[]{:S(2)}, u32[]{:S(2)}) collective-permute-start(bf16[168,1536]{1,0:T(8,128)(2,1)} %collective-permute-done.12.refs_5_.refs_13_), channel_id=1, source_target_pairs={{0,32},{1,33},{2,34},{3,35},{4,36},{5,37},{6,38},{7,39},{8,40},{9,... | collective-permute-start | bytes 1548296 | tf_op jit(solution)/shard_map/ppermute | solution.py:30
  90.5 12.9 %collective-permute-start.20 = (bf16[168,1536]{1,0:T(8,128)(2,1)}, bf16[168,1536]{1,0:T(8,128)(2,1)S(1)}, u32[]{:S(2)}, u32[]{:S(2)}) collective-permute-start(bf16[168,1536]{1,0:T(8,128)(2,1)} %collective-permute-done.16.refs_12_), channel_id=1, source_target_pairs={{0,32},{1,33},{2,34},{3,35},{4,36},{5,37},{6,38},{7,39},{8,40},{9,... | collective-permute-start | bytes 1548296 | tf_op jit(solution)/shard_map/ppermute | solution.py:30
  91.3 13.3 %collective-permute-start.21 = (bf16[168,1536]{1,0:T(8,128)(2,1)}, bf16[168,1536]{1,0:T(8,128)(2,1)}, u32[]{:S(2)}, u32[]{:S(2)}) collective-permute-start(bf16[168,1536]{1,0:T(8,128)(2,1)} %collective-permute-done.18.refs_14_), channel_id=1, source_target_pairs={{0,32},{1,33},{2,34},{3,35},{4,36},{5,37},{6,38},{7,39},{8,40},{9,... | collective-permute-start | bytes 1548296 | tf_op jit(solution)/shard_map/ppermute | solution.py:30
  103.3 5.0 %copy-start.13 = (bf16[168,1536]{1,0:T(8,128)(2,1)}, bf16[168,1536]{1,0:T(8,128)(2,1)S(1)}, u32[]{:S(2)}) copy-start(bf16[168,1536]{1,0:T(8,128)(2,1)S(1)} %collective-permute-done.20.refs_4_) | copy-start | bytes 1548292
  104.6 10.4 %collective-permute-start.22 = (bf16[512,1536]{1,0:T(8,128)(2,1)}, bf16[512,1536]{1,0:T(8,128)(2,1)}, u32[]{:S(2)}, u32[]{:S(2)}) collective-permute-start(bf16[512,1536]{1,0:T(8,128)(2,1)} %get-tuple-element.326), channel_id=1, source_target_pairs={{0,16},{1,17},{2,18},{3,19},{4,20},{5,21},{6,22},{7,23},{8,24},{9,... | collective-permute-start | bytes 4718600 | tf_op jit(solution)/shard_map/ppermute | solution.py:30
  114.9 3.8 %collective-permute-start.23 = (bf16[512,1536]{1,0:T(8,128)(2,1)}, bf16[512,1536]{1,0:T(8,128)(2,1)}, u32[]{:S(2)}, u32[]{:S(2)}) collective-permute-start(bf16[512,1536]{1,0:T(8,128)(2,1)} %get-tuple-element.332), channel_id=1, source_target_pairs={{0,16},{1,17},{2,18},{3,19},{4,20},{5,21},{6,22},{7,23},{8,24},{9,... | collective-permute-start | bytes 4718600 | tf_op jit(solution)/shard_map/ppermute | solution.py:30
  118.5 4.2 %copy-start.4 = (bf16[512,1536]{1,0:T(8,128)(2,1)S(1)}, bf16[512,1536]{1,0:T(8,128)(2,1)}, u32[]{:S(2)}) copy-start(bf16[512,1536]{1,0:T(8,128)(2,1)} %get-tuple-element.333.refs_1_) | copy-start | bytes 4718596
  120.1 6.6 %collective-permute-start.26 = (bf16[64,1536]{1,0:T(8,128)(2,1)S(1)}, bf16[64,1536]{1,0:T(8,128)(2,1)S(1)}, u32[]{:S(2)}, u32[]{:S(2)}) collective-permute-start(bf16[64,1536]{1,0:T(8,128)(2,1)S(1)} %get-tuple-element.336), channel_id=1, source_target_pairs={{0,3},{1,0},{2,1},{3,2},{4,7},{5,4},{6,5},{7,6},{8,11},{9,8},{10,9... | collective-permute-start | bytes 589832 | tf_op jit(solution)/shard_map/ppermute | solution.py:30
  124.0 8.0 %collective-permute-start.24 = (bf16[64,1536]{1,0:T(8,128)(2,1)S(1)}, bf16[64,1536]{1,0:T(8,128)(2,1)S(1)}, u32[]{:S(2)}, u32[]{:S(2)}) collective-permute-start(bf16[64,1536]{1,0:T(8,128)(2,1)S(1)} %get-tuple-element.335), channel_id=1, source_target_pairs={{0,1},{1,2},{2,3},{3,0},{4,5},{5,6},{6,7},{7,4},{8,9},{9,10},{10,1... | collective-permute-start | bytes 589832 | tf_op jit(solution)/shard_map/ppermute | solution.py:30
  127.5 18.9 %collective-permute-start.27 = (bf16[128,1536]{1,0:T(8,128)(2,1)}, bf16[128,1536]{1,0:T(8,128)(2,1)S(1)}, u32[]{:S(2)}, u32[]{:S(2)}) collective-permute-start(bf16[128,1536]{1,0:T(8,128)(2,1)} %pad_maximum_fusion.1), channel_id=1, source_target_pairs={{0,3},{1,0},{2,1},{3,2},{4,7},{5,4},{6,5},{7,6},{8,11},{9,8},{10,9... | collective-permute-start | bytes 1179656 | tf_op jit(solution)/shard_map/ppermute | solution.py:30
  132.9 19.3 %collective-permute-start.25 = (bf16[128,1536]{1,0:T(8,128)(2,1)}, bf16[128,1536]{1,0:T(8,128)(2,1)}, u32[]{:S(2)}, u32[]{:S(2)}) collective-permute-start(bf16[128,1536]{1,0:T(8,128)(2,1)} %pad_maximum_fusion), channel_id=1, source_target_pairs={{0,1},{1,2},{2,3},{3,0},{4,5},{5,6},{6,7},{7,4},{8,9},{9,10},{10,1... | collective-permute-start | bytes 1179656 | tf_op jit(solution)/shard_map/ppermute | solution.py:30
  146.5 5.9 %copy-start.14 = (bf16[128,1536]{1,0:T(8,128)(2,1)}, bf16[128,1536]{1,0:T(8,128)(2,1)S(1)}, u32[]{:S(2)}) copy-start(bf16[128,1536]{1,0:T(8,128)(2,1)S(1)} %collective-permute-done.27.refs_4_) | copy-start | bytes 1179652
Sparse Core Ops, SparseCore 0:
  12.2 47.6 all-gather.1
  118.6 33.7 reduce-scatter.1

commit v3 on v2

--- a/solution.py
+++ b/solution.py
@@ -250,28 +250,34 @@
     places = places_ref[...]
     for index, lanes in enumerate((pl.ds(here, SPLIT), pl.ds(SPLIT - here, SPLIT))):
         if index == 0:
-            parts = [refs[0][...]]
+            picked = jnp.dot(places, refs[0][...], preferred_element_type=jnp.float32)
         else:
             expert_out = sum((ref[...].astype(jnp.float32) for ref in refs[2:5]), refs[1][...].astype(jnp.float32))
             high = expert_out.astype(jnp.bfloat16)
-            parts = [high, (expert_out - high.astype(jnp.float32)).astype(jnp.bfloat16)]
-        picked = [jnp.dot(places, part, preferred_element_type=jnp.float32) for part in parts]
-        out_ref[:, lanes] = (share_ref[...] * sum(picked[1:], picked[0])).astype(jnp.bfloat16)
+            low = (expert_out - high.astype(jnp.float32)).astype(jnp.bfloat16)
+            picked = jnp.dot(
+                jnp.concatenate([places, places], axis=1),
+                jnp.concatenate([high, low], axis=0),
+                preferred_element_type=jnp.float32,
+            )
+        out_ref[:, lanes] = (share_ref[...] * picked).astype(jnp.bfloat16)
 
 
 def spread(place, places, share, pair, terms):
     def block(*shape):
         return pl.BlockSpec(shape, lambda i, place: (i, 0))
 
-    own = pl.BlockSpec((CAP, SPLIT), lambda i, place: (place[3] * SPANS + i, 0))
+    slots = 2 * CAP
+    own = pl.BlockSpec((slots, SPLIT), lambda i, place: (place[3] * (SPANS // 2) + i, 0))
+    rows = block(slots, SPLIT)
     return pl.pallas_call(
         spread_kernel,
         out_shape=jax.ShapeDtypeStruct((SPANS * CT, 2 * SPLIT), jnp.bfloat16),
         grid_spec=pltpu.PrefetchScalarGridSpec(
             num_scalar_prefetch=1,
-            grid=(SPANS,),
-            in_specs=[block(CT, CAP), block(CT, 1), block(CAP, SPLIT), own, own, block(CAP, SPLIT), block(CAP, SPLIT)],
-            out_specs=block(CT, 2 * SPLIT),
+            grid=(SPANS // 2,),
+            in_specs=[block(2 * CT, slots), block(2 * CT, 1), rows, own, own, rows, rows],
+            out_specs=block(2 * CT, 2 * SPLIT),
         ),
         compiler_params=pltpu.CompilerParams(vmem_limit_bytes=ALL_VMEM_BYTES),
     )(place, places, share, terms[0], *pair, *terms[1:])
@@ -390,7 +396,9 @@
     pieces_there, pair_there = lax.optimization_barrier((far_pieces(pair_there), pair_there))
     near_there = near(pair_there, far(pieces_there))
     terms = [out_here, *near_there]
-    places = jnp.swapaxes(selector, 1, 2).reshape(SPANS * CT, CAP).astype(jnp.bfloat16)
+    pairs = jnp.swapaxes(selector, 1, 2).reshape(SPANS // 2, 2, CT, 1, CAP)
+    pairs = pairs & jnp.eye(2, dtype=bool)[None, :, None, :, None]
+    places = pairs.reshape(SPANS * CT, 2 * CAP).astype(jnp.bfloat16)
     return spread(work["place"], places, gate_share[:, None], pair_there, terms)
 
 

time: 166 us -> 164 us (0.988)
  local copies, waits for them, and re-layouts: 13.2 us -> 16.4 us
  waiting for transfers between devices: 34.2 us -> 31.1 us
    ppermute x28, waiting for transfers between devices: 33.9 us -> 30.8 us  [moved(): return lax.ppermute(value, AXES, pairs)]
    convert_element_type x0 -> x2, local copies, waits for them, and re-layouts: none -> 3.09 us  [on_device(): places = pairs.reshape(SPANS * CT, 2 * CAP).astype(jnp.bfloat16)]
  transfers between devices with their start and end apart: 30 -> 30, of which waited for: 16 -> 16; matrix products, arithmetic and copies ran while one was open for 13% -> 15% of each run, Pallas kernels for 19% -> 19%
where the time goes in v3:
time: 164 us
  starting transfers between devices  51.5 us (31%)
  Pallas kernels  35 us (21%)
  waiting for transfers between devices  31.1 us (19%)
  local copies, waits for them, and re-layouts  16.4 us (10%)
  other arithmetic  14.5 us (9%)
  between operations  13.7 us (8%)
    ppermute x28, starting transfers between devices, moved(): return lax.ppermute(value, AXES, pairs)  51.5 us
    ppermute x28, waiting for transfers between devices, moved(): return lax.ppermute(value, AXES, pairs)  30.8 us
    pallas_call x3, Pallas kernels, kernel_call(): pl.pallas_call(kernel, out_shape=[jax.ShapeDtypeStruct(shape, jnp.bfloat1...  30.7 us
    dynamic_slice x4, local copies, waits for them, and re-layouts, piece(): return lax.dynamic_slice(array, (start, side * SPLIT), (UNITS, SPLIT))  7.51 us
    pallas_call x1, Pallas kernels, spread(): pl.pallas_call(spread_kernel, out_shape=jax.ShapeDtypeStruct((SPANS * CT,...  4.32 us
    convert_element_type x1, other arithmetic, on_device(): (mine_here.astype(jnp.float32) + moved(others_here, other_core).astype(jn...  3.41 us
  transfers between devices with their start and end apart: 30, of which 16 were waited for; matrix products, arithmetic and copies ran while one was open for 15% of the time, Pallas kernels for 19%

profile of v3, /device:TPU:1, one launch (start us, length us, event | category | flops | bytes accessed | tf_op | source)
XLA Modules:
  0.0 163.6 jit_solution(6047946463301290394)
XLA Ops:
  6.5 0.9 select_reduce_fusion
  7.5 1.2 reduce_window_sum.11
  8.7 1.9 %dynamic-slice_bitcast_fusion = bf16[168,1536]{1,0:T(8,128)(2,1)} fusion(bf16[3072,336]{0,1:T(8,128)(2,1)} %param.9, s32[]{:T(128)S(6)} %select_n.95, s32[]{:T(128)S(6)} %select_n.96), kind=kLoop, calls=%fused_computation.5 | loop fusion | bytes 1032200 | tf_op jit(solution)/shard_map/dynamic_slice | solution.py:309
  10.6 1.4 convolution_convert_fusion
  12.1 6.5 %collective-permute-start = (bf16[168,1536]{1,0:T(8,128)(2,1)}, bf16[168,1536]{1,0:T(8,128)(2,1)}, u32[]{:S(2)}, u32[]{:S(2)}) collective-permute-start(bf16[168,1536]{1,0:T(8,128)(2,1)} %dynamic-slice_bitcast_fusion), channel_id=1, source_target_pairs={{0,128},{1,129},{2,130},{3,131},{4,132},{5,133},{6,134},{7,135},{8... | collective-permute-start | bytes 1548296 | tf_op jit(solution)/shard_map/ppermute | solution.py:30
  18.6 1.9 %dynamic_slice.47 = bf16[168,1536]{1,0:T(8,128)(2,1)} dynamic-slice(bf16[336,3072]{1,0:T(8,128)(2,1)} %bitcast.22, s32[]{:T(128)S(6)} %select_n.96, s32[]{:T(128)S(6)} %select_n.95), dynamic_slice_sizes={168,1536} | dynamic-slice | bytes 1032196 | tf_op jit(solution)/shard_map/dynamic_slice | solution.py:309
  21.2 1.9 %dynamic_slice.49 = bf16[168,1536]{1,0:T(8,128)(2,1)} dynamic-slice(bf16[336,3072]{1,0:T(8,128)(2,1)} %bitcast.20, s32[]{:T(128)S(6)} %select_n.98, s32[]{:T(128)S(6)} %select_n.95), dynamic_slice_sizes={168,1536} | dynamic-slice | bytes 1032196 | tf_op jit(solution)/shard_map/dynamic_slice | solution.py:309
  23.1 1.9 %dynamic_slice.50 = bf16[168,1536]{1,0:T(8,128)(2,1)} dynamic-slice(bf16[336,3072]{1,0:T(8,128)(2,1)} %bitcast.23, s32[]{:T(128)S(6)} %select_n.98, s32[]{:T(128)S(6)} %select_n.95), dynamic_slice_sizes={168,1536} | dynamic-slice | bytes 1032196 | tf_op jit(solution)/shard_map/dynamic_slice | solution.py:309
  25.5 3.1 %constant_dynamic-slice_fusion = (bf16[168,3072]{1,0:T(8,128)(2,1)}, bf16[168,3072]{1,0:T(8,128)(2,1)}) fusion(bf16[336,3072]{1,0:T(8,128)(2,1)} %bitcast.24, s32[]{:T(128)S(6)} %select_n.96, bf16[336,3072]{1,0:T(8,128)(2,1)} %bitcast.21), kind=kLoop, calls=%fused_computation.29 | loop fusion | bytes 4128772 | tf_op jit(solution)/shard_map/dynamic_slice | solution.py:350
  28.7 1.2 fusion.6
  29.9 1.8 %collective-permute-start.2 = (bf16[168,1536]{1,0:T(8,128)(2,1)S(1)}, bf16[168,1536]{1,0:T(8,128)(2,1)S(1)}, u32[]{:S(2)}, u32[]{:S(2)}) collective-permute-start(bf16[168,1536]{1,0:T(8,128)(2,1)S(1)} %get-tuple-element.189), channel_id=1, source_target_pairs={{0,128},{1,129},{2,130},{3,131},{4,132},{5,133},{6,134},{7,135},{8... | collective-permute-start | bytes 1548296 | tf_op jit(solution)/shard_map/ppermute | solution.py:30
  31.7 2.8 %collective-permute-start.3 = (bf16[168,1536]{1,0:T(8,128)(2,1)}, bf16[168,1536]{1,0:T(8,128)(2,1)}, u32[]{:S(2)}, u32[]{:S(2)}) collective-permute-start(bf16[168,1536]{1,0:T(8,128)(2,1)} %collective-permute-done.refs_0_), channel_id=1, source_target_pairs={{0,32},{1,33},{2,34},{3,35},{4,36},{5,37},{6,38},{7,39},{8,40},{9,... | collective-permute-start | bytes 1548296 | tf_op jit(solution)/shard_map/ppermute | solution.py:30
  34.6 1.1 collective-permute-start.4
  35.7 1.8 %collective-permute-start.5 = (bf16[168,1536]{1,0:T(8,128)(2,1)}, bf16[168,1536]{1,0:T(8,128)(2,1)S(1)}, u32[]{:S(2)}, u32[]{:S(2)}) collective-permute-start(bf16[168,1536]{1,0:T(8,128)(2,1)} %collective-permute-done.1.refs_4_), channel_id=1, source_target_pairs={{0,32},{1,33},{2,34},{3,35},{4,36},{5,37},{6,38},{7,39},{8,40},{9,... | collective-permute-start | bytes 1548296 | tf_op jit(solution)/shard_map/ppermute | solution.py:30
  37.5 1.2 collective-permute-done.2.refs_1_.refs_9_
  38.8 2.1 %collective-permute-done.3.refs_2_ = bf16[168,1536]{1,0:T(8,128)(2,1)} collective-permute-done((bf16[168,1536]{1,0:T(8,128)(2,1)}, bf16[168,1536]{1,0:T(8,128)(2,1)}, u32[]{:S(2)}, u32[]{:S(2)}) %collective-permute-start.3) | collective-permute-done | bytes 516128 | tf_op jit(solution)/shard_map/ppermute | solution.py:30
  41.5 2.8 %collective-permute-start.7 = (bf16[168,1536]{1,0:T(8,128)(2,1)S(1)}, bf16[168,1536]{1,0:T(8,128)(2,1)S(1)}, u32[]{:S(2)}, u32[]{:S(2)}) collective-permute-start(bf16[168,1536]{1,0:T(8,128)(2,1)S(1)} %collective-permute-done.2.refs_1_.refs_9_), channel_id=1, source_target_pairs={{0,32},{1,33},{2,34},{3,35},{4,36},{5,37},{6,38},{7,39},{8,40},{9,... | collective-permute-start | bytes 1548296 | tf_op jit(solution)/shard_map/ppermute | solution.py:30
  44.3 2.1 %collective-permute-done.5.refs_6_ = bf16[168,1536]{1,0:T(8,128)(2,1)S(1)} collective-permute-done((bf16[168,1536]{1,0:T(8,128)(2,1)}, bf16[168,1536]{1,0:T(8,128)(2,1)S(1)}, u32[]{:S(2)}, u32[]{:S(2)}) %collective-permute-start.5) | collective-permute-done | bytes 516128 | tf_op jit(solution)/shard_map/ppermute | solution.py:30
  47.8 2.8 %collective-permute-start.9 = (bf16[168,1536]{1,0:T(8,128)(2,1)S(1)}, bf16[168,1536]{1,0:T(8,128)(2,1)S(1)}, u32[]{:S(2)}, u32[]{:S(2)}) collective-permute-start(bf16[168,1536]{1,0:T(8,128)(2,1)S(1)} %collective-permute-done.4.refs_5_.refs_8_), channel_id=1, source_target_pairs={{0,32},{1,33},{2,34},{3,35},{4,36},{5,37},{6,38},{7,39},{8,40},{9,... | collective-permute-start | bytes 1548296 | tf_op jit(solution)/shard_map/ppermute | solution.py:30
  50.7 1.1 collective-permute-done.7.refs_3_.refs_1_
  52.5 2.8 %collective-permute-start.11 = (bf16[168,1536]{1,0:T(8,128)(2,1)S(1)}, bf16[168,1536]{1,0:T(8,128)(2,1)}, u32[]{:S(2)}, u32[]{:S(2)}) collective-permute-start(bf16[168,1536]{1,0:T(8,128)(2,1)S(1)} %collective-permute-done.6.refs_12_.refs_10_), channel_id=1, source_target_pairs={{0,32},{1,33},{2,34},{3,35},{4,36},{5,37},{6,38},{7,39},{8,40},{9,... | collective-permute-start | bytes 1548296 | tf_op jit(solution)/shard_map/ppermute | solution.py:30
  55.6 0.9 broadcast_select_fusion.1
  56.4 0.9 collective-permute-done.9.refs_7_.refs_10_
  57.3 2.5 %collective-permute-start.13 = (bf16[168,1536]{1,0:T(8,128)(2,1)}, bf16[168,1536]{1,0:T(8,128)(2,1)}, u32[]{:S(2)}, u32[]{:S(2)}) collective-permute-start(bf16[168,1536]{1,0:T(8,128)(2,1)} %broadcast_select_fusion.1), channel_id=1, source_target_pairs={{0,128},{1,129},{2,130},{3,131},{4,132},{5,133},{6,134},{7,135},{8... | collective-permute-start | bytes 1548296 | tf_op jit(solution)/shard_map/ppermute | solution.py:30
  59.9 2.8 %collective-permute-start.14 = (bf16[168,1536]{1,0:T(8,128)(2,1)}, bf16[168,1536]{1,0:T(8,128)(2,1)}, u32[]{:S(2)}, u32[]{:S(2)}) collective-permute-start(bf16[168,1536]{1,0:T(8,128)(2,1)} %collective-permute-done.8.refs_9_.refs_0_), channel_id=1, source_target_pairs={{0,32},{1,33},{2,34},{3,35},{4,36},{5,37},{6,38},{7,39},{8,40},{9,... | collective-permute-start | bytes 1548296 | tf_op jit(solution)/shard_map/ppermute | solution.py:30
  65.2 2.4 %collective-permute-start.15 = (bf16[168,1536]{1,0:T(8,128)(2,1)}, bf16[168,1536]{1,0:T(8,128)(2,1)S(1)}, u32[]{:S(2)}, u32[]{:S(2)}) collective-permute-start(bf16[168,1536]{1,0:T(8,128)(2,1)} %copy-done.5), channel_id=1, source_target_pairs={{0,32},{1,33},{2,34},{3,35},{4,36},{5,37},{6,38},{7,39},{8,40},{9,... | collective-permute-start | bytes 1548296 | tf_op jit(solution)/shard_map/ppermute | solution.py:30
  67.6 1.4 collective-permute-done.14.refs_11_.refs_2_
  69.7 2.8 %collective-permute-start.17 = (bf16[168,1536]{1,0:T(8,128)(2,1)}, bf16[168,1536]{1,0:T(8,128)(2,1)}, u32[]{:S(2)}, u32[]{:S(2)}) collective-permute-start(bf16[168,1536]{1,0:T(8,128)(2,1)} %collective-permute-done.13.refs_1_.refs_11_), channel_id=1, source_target_pairs={{0,32},{1,33},{2,34},{3,35},{4,36},{5,37},{6,38},{7,39},{8,40},{9,... | collective-permute-start | bytes 1548296 | tf_op jit(solution)/shard_map/ppermute | solution.py:30
  73.0 1.5 collective-permute-done.15.refs_15_.refs_6_
  75.1 2.9 %collective-permute-start.19 = (bf16[168,1536]{1,0:T(8,128)(2,1)}, bf16[168,1536]{1,0:T(8,128)(2,1)}, u32[]{:S(2)}, u32[]{:S(2)}) collective-permute-start(bf16[168,1536]{1,0:T(8,128)(2,1)} %collective-permute-done.12.refs_5_.refs_13_), channel_id=1, source_target_pairs={{0,32},{1,33},{2,34},{3,35},{4,36},{5,37},{6,38},{7,39},{8,40},{9,... | collective-permute-start | bytes 1548296 | tf_op jit(solution)/shard_map/ppermute | solution.py:30
  78.0 12.5 %shard_map.64.first_ref = bf16[1024,504]{1,0:T(8,128)(2,1)} custom-call(s32[4]{0:T(128)} %pad_add_fusion.place_ref, bf16[1024,3072]{1,0:T(8,128)(2,1)} %all-gather.2.cloned.1.call-done.rows_ref, bf16[168,1536]{1,0:T(8,128)(2,1)} %collective-permute-done.refs_0_, bf16[168,1536]{1,0:T(8,128)(2,1)} %copy-done.2, ...), custom_call_target="tpu_custom_call" | custom-call | flops 1000000 | bytes 100000 | tf_op jit(solution)/shard_map/pallas_call | solution.py:183
  91.7 11.7 %shard_map.65 = (bf16[512,1536]{1,0:T(8,128)(2,1)}, bf16[512,1536]{1,0:T(8,128)(2,1)}, bf16[1024,168]{1,0:T(8,128)(2,1)}) custom-call(s32[4]{0:T(128)} %pad_add_fusion.place_ref, bf16[1024,3072]{1,0:T(8,128)(2,1)} %all-gather.2.cloned.1.call-done.rows_ref, bf16[1024,504]{1,0:T(8,128)(2,1)} %shard_map.64.first_ref, ...), custom_call_target="tpu_custom_call" | custom-call | flops 1000000 | bytes 100000 | tf_op jit(solution)/shard_map/pallas_call | solution.py:183
  103.4 1.3 collective-permute-done.21.refs_6_
  104.6 3.7 %collective-permute-start.22 = (bf16[512,1536]{1,0:T(8,128)(2,1)}, bf16[512,1536]{1,0:T(8,128)(2,1)}, u32[]{:S(2)}, u32[]{:S(2)}) collective-permute-start(bf16[512,1536]{1,0:T(8,128)(2,1)} %get-tuple-element.326), channel_id=1, source_target_pairs={{0,16},{1,17},{2,18},{3,19},{4,20},{5,21},{6,22},{7,23},{8,24},{9,... | collective-permute-start | bytes 4718600 | tf_op jit(solution)/shard_map/ppermute | solution.py:30
  108.4 6.5 %shard_map.66 = (bf16[512,1536]{1,0:T(8,128)(2,1)}, bf16[512,1536]{1,0:T(8,128)(2,1)}) custom-call(s32[4]{0:T(128)} %pad_add_fusion.place_ref, bf16[1024,504]{1,0:T(8,128)(2,1)} %shard_map.64.first_ref, bf16[1024,168]{1,0:T(8,128)(2,1)} %get-tuple-element.327.last_ref, bf16[168,1536]{1,0:T(8,128)(2,1)} %get-tuple-element.328.refs_0_, ...), custom_call_target="tpu_custom_call" | custom-call | flops 1000000 | bytes 100000 | tf_op jit(solution)/shard_map/pallas_call | solution.py:183
  115.0 3.4 %add_convert_fusion = bf16[512,1536]{1,0:T(8,128)(2,1)} fusion(bf16[512,1536]{1,0:T(8,128)(2,1)} %collective-permute-done.22, bf16[512,1536]{1,0:T(8,128)(2,1)} %get-tuple-element.323), kind=kLoop, calls=%fused_computation.1 | loop fusion | flops 3145728 | bytes 4718592 | tf_op jit(solution)/shard_map/convert_element_type | solution.py:371
  118.8 1.3 add_convert_fusion.1
  120.1 2.5 %collective-permute-start.26 = (bf16[64,1536]{1,0:T(8,128)(2,1)S(1)}, bf16[64,1536]{1,0:T(8,128)(2,1)S(1)}, u32[]{:S(2)}, u32[]{:S(2)}) collective-permute-start(bf16[64,1536]{1,0:T(8,128)(2,1)S(1)} %get-tuple-element.336), channel_id=1, source_target_pairs={{0,3},{1,0},{2,1},{3,2},{4,7},{5,4},{6,5},{7,6},{8,11},{9,8},{10,9... | collective-permute-start | bytes 589832 | tf_op jit(solution)/shard_map/ppermute | solution.py:30
  122.7 1.3 convert_add_fusion
  124.2 2.5 %collective-permute-done.26 = bf16[64,1536]{1,0:T(8,128)(2,1)S(1)} collective-permute-done((bf16[64,1536]{1,0:T(8,128)(2,1)S(1)}, bf16[64,1536]{1,0:T(8,128)(2,1)S(1)}, u32[]{:S(2)}, u32[]{:S(2)}) %collective-permute-start.26) | collective-permute-done | bytes 196640 | tf_op jit(solution)/shard_map/ppermute | solution.py:30
  127.5 3.4 %collective-permute-start.27 = (bf16[128,1536]{1,0:T(8,128)(2,1)}, bf16[128,1536]{1,0:T(8,128)(2,1)S(1)}, u32[]{:S(2)}, u32[]{:S(2)}) collective-permute-start(bf16[128,1536]{1,0:T(8,128)(2,1)} %pad_maximum_fusion.1), channel_id=1, source_target_pairs={{0,3},{1,0},{2,1},{3,2},{4,7},{5,4},{6,5},{7,6},{8,11},{9,8},{10,9... | collective-permute-start | bytes 1179656 | tf_op jit(solution)/shard_map/ppermute | solution.py:30
  130.9 1.0 collective-permute-done.24
  133.6 1.5 reshape.56
  135.1 1.6 copy.7.places_ref
  136.7 0.9 copy.8.share_ref
  137.6 8.9 %collective-permute-done.27.refs_4_ = bf16[128,1536]{1,0:T(8,128)(2,1)S(1)} collective-permute-done((bf16[128,1536]{1,0:T(8,128)(2,1)}, bf16[128,1536]{1,0:T(8,128)(2,1)S(1)}, u32[]{:S(2)}, u32[]{:S(2)}) %collective-permute-start.27) | collective-permute-done | bytes 393248 | tf_op jit(solution)/shard_map/ppermute | solution.py:30
  146.4 5.7 %collective-permute-done.25.refs_3_ = bf16[128,1536]{1,0:T(8,128)(2,1)} collective-permute-done((bf16[128,1536]{1,0:T(8,128)(2,1)}, bf16[128,1536]{1,0:T(8,128)(2,1)}, u32[]{:S(2)}, u32[]{:S(2)}) %collective-permute-start.25) | collective-permute-done | bytes 393248 | tf_op jit(solution)/shard_map/ppermute | solution.py:30
  152.4 4.3 %shard_map.67 = bf16[512,3072]{1,0:T(8,128)(2,1)} custom-call(s32[4]{0:T(128)} %pad_add_fusion.place_ref, bf16[512,64]{1,0:T(8,128)(2,1)} %copy.7.places_ref, f32[512,1]{1,0:T(8,128)} %copy.8.share_ref, bf16[128,1536]{1,0:T(8,128)(2,1)} %reduce-scatter.2.cloned.1.call-done.refs_0_, bf16[512,1536]{1,0:T(8,128)(2,1)} %get-tuple-element.333.refs_1_, ...), custom_call_target="tpu_custom_call" | custom-call | tf_op jit(solution)/shard_map/pallas_call | solution.py:273
  (84 shorter events, 13.5 us)
Async XLA Ops:
  6.5 4.0 %copy-start = (bf16[512,3072]{1,0:T(8,128)(2,1)S(1)}, bf16[512,3072]{1,0:T(8,128)(2,1)}, u32[]{:S(2)}) copy-start(bf16[512,3072]{1,0:T(8,128)(2,1)} %param.6) | copy-start | bytes 9437188
  6.5 57.8 %all-gather.2.cloned.1.call-start = ((), (), s32[]{:S(2)}) async-start(), calls=%async_computation.1 | async-start | bytes 7077888 | tf_op jit(solution)/shard_map/all_gather | solution.py:358
  12.0 140.4 %reduce-scatter.2.cloned.1.call-start = ((), (), s32[]{:S(2)}) async-start(), calls=%async_computation.2 | async-start | bytes 1966080 | tf_op jit(solution)/shard_map/reduce_scatter | solution.py:372
  12.1 16.6 %collective-permute-start = (bf16[168,1536]{1,0:T(8,128)(2,1)}, bf16[168,1536]{1,0:T(8,128)(2,1)}, u32[]{:S(2)}, u32[]{:S(2)}) collective-permute-start(bf16[168,1536]{1,0:T(8,128)(2,1)} %dynamic-slice_bitcast_fusion), channel_id=1, source_target_pairs={{0,128},{1,129},{2,130},{3,131},{4,132},{5,133},{6,134},{7,135},{8... | collective-permute-start | bytes 1548296 | tf_op jit(solution)/shard_map/ppermute | solution.py:30
  20.4 14.1 %collective-permute-start.1 = (bf16[168,1536]{1,0:T(8,128)(2,1)}, bf16[168,1536]{1,0:T(8,128)(2,1)}, u32[]{:S(2)}, u32[]{:S(2)}) collective-permute-start(bf16[168,1536]{1,0:T(8,128)(2,1)} %dynamic_slice.47), channel_id=1, source_target_pairs={{0,128},{1,129},{2,130},{3,131},{4,132},{5,133},{6,134},{7,135},{8... | collective-permute-start | bytes 1548296 | tf_op jit(solution)/shard_map/ppermute | solution.py:30
  25.5 3.1 %copy-start.11 = (bf16[336,3072]{1,0:T(8,128)(2,1)S(1)}, bf16[336,3072]{1,0:T(8,128)(2,1)}, u32[]{:S(2)}) copy-start(bf16[336,3072]{1,0:T(8,128)(2,1)} %param.11) | copy-start | bytes 6193156
  28.7 5.9 %copy-start.8 = (bf16[168,1536]{1,0:T(8,128)(2,1)S(1)}, bf16[168,1536]{1,0:T(8,128)(2,1)}, u32[]{:S(2)}) copy-start(bf16[168,1536]{1,0:T(8,128)(2,1)} %dynamic_slice.49) | copy-start | bytes 1548292
  28.7 10.0 %copy-start.7 = (bf16[168,1536]{1,0:T(8,128)(2,1)S(1)}, bf16[168,1536]{1,0:T(8,128)(2,1)}, u32[]{:S(2)}) copy-start(bf16[168,1536]{1,0:T(8,128)(2,1)} %dynamic_slice.50) | copy-start | bytes 1548292
  29.9 8.8 %collective-permute-start.2 = (bf16[168,1536]{1,0:T(8,128)(2,1)S(1)}, bf16[168,1536]{1,0:T(8,128)(2,1)S(1)}, u32[]{:S(2)}, u32[]{:S(2)}) collective-permute-start(bf16[168,1536]{1,0:T(8,128)(2,1)S(1)} %get-tuple-element.189), channel_id=1, source_target_pairs={{0,128},{1,129},{2,130},{3,131},{4,132},{5,133},{6,134},{7,135},{8... | collective-permute-start | bytes 1548296 | tf_op jit(solution)/shard_map/ppermute | solution.py:30
  31.7 9.1 %collective-permute-start.3 = (bf16[168,1536]{1,0:T(8,128)(2,1)}, bf16[168,1536]{1,0:T(8,128)(2,1)}, u32[]{:S(2)}, u32[]{:S(2)}) collective-permute-start(bf16[168,1536]{1,0:T(8,128)(2,1)} %collective-permute-done.refs_0_), channel_id=1, source_target_pairs={{0,32},{1,33},{2,34},{3,35},{4,36},{5,37},{6,38},{7,39},{8,40},{9,... | collective-permute-start | bytes 1548296 | tf_op jit(solution)/shard_map/ppermute | solution.py:30
  34.6 9.7 %collective-permute-start.4 = (bf16[168,1536]{1,0:T(8,128)(2,1)S(1)}, bf16[168,1536]{1,0:T(8,128)(2,1)S(1)}, u32[]{:S(2)}, u32[]{:S(2)}) collective-permute-start(bf16[168,1536]{1,0:T(8,128)(2,1)S(1)} %broadcast_select_fusion.5), channel_id=1, source_target_pairs={{0,128},{1,129},{2,130},{3,131},{4,132},{5,133},{6,134},{7,135},{8... | collective-permute-start | bytes 1548296 | tf_op jit(solution)/shard_map/ppermute | solution.py:30
  35.7 10.7 %collective-permute-start.5 = (bf16[168,1536]{1,0:T(8,128)(2,1)}, bf16[168,1536]{1,0:T(8,128)(2,1)S(1)}, u32[]{:S(2)}, u32[]{:S(2)}) collective-permute-start(bf16[168,1536]{1,0:T(8,128)(2,1)} %collective-permute-done.1.refs_4_), channel_id=1, source_target_pairs={{0,32},{1,33},{2,34},{3,35},{4,36},{5,37},{6,38},{7,39},{8,40},{9,... | collective-permute-start | bytes 1548296 | tf_op jit(solution)/shard_map/ppermute | solution.py:30
  38.7 12.0 %copy-start.2 = (bf16[168,1536]{1,0:T(8,128)(2,1)}, bf16[168,1536]{1,0:T(8,128)(2,1)S(1)}, u32[]{:S(2)}) copy-start(bf16[168,1536]{1,0:T(8,128)(2,1)S(1)} %collective-permute-done.2.refs_1_.refs_9_) | copy-start | bytes 1548292
  40.9 9.8 %collective-permute-start.6 = (bf16[168,1536]{1,0:T(8,128)(2,1)S(1)}, bf16[168,1536]{1,0:T(8,128)(2,1)S(1)}, u32[]{:S(2)}, u32[]{:S(2)}) collective-permute-start(bf16[168,1536]{1,0:T(8,128)(2,1)S(1)} %broadcast_select_fusion.4), channel_id=1, source_target_pairs={{0,128},{1,129},{2,130},{3,131},{4,132},{5,133},{6,134},{7,135},{8... | collective-permute-start | bytes 1548296 | tf_op jit(solution)/shard_map/ppermute | solution.py:30
  41.5 10.4 %collective-permute-start.7 = (bf16[168,1536]{1,0:T(8,128)(2,1)S(1)}, bf16[168,1536]{1,0:T(8,128)(2,1)S(1)}, u32[]{:S(2)}, u32[]{:S(2)}) collective-permute-start(bf16[168,1536]{1,0:T(8,128)(2,1)S(1)} %collective-permute-done.2.refs_1_.refs_9_), channel_id=1, source_target_pairs={{0,32},{1,33},{2,34},{3,35},{4,36},{5,37},{6,38},{7,39},{8,40},{9,... | collective-permute-start | bytes 1548296 | tf_op jit(solution)/shard_map/ppermute | solution.py:30
  44.3 12.1 %copy-start.1 = (bf16[168,1536]{1,0:T(8,128)(2,1)}, bf16[168,1536]{1,0:T(8,128)(2,1)S(1)}, u32[]{:S(2)}) copy-start(bf16[168,1536]{1,0:T(8,128)(2,1)S(1)} %collective-permute-done.4.refs_5_.refs_8_) | copy-start | bytes 1548292
  46.4 0.8 copy-start.12
  47.2 8.3 %collective-permute-start.8 = (bf16[168,1536]{1,0:T(8,128)(2,1)S(1)}, bf16[168,1536]{1,0:T(8,128)(2,1)}, u32[]{:S(2)}, u32[]{:S(2)}) collective-permute-start(bf16[168,1536]{1,0:T(8,128)(2,1)S(1)} %broadcast_select_fusion.3), channel_id=1, source_target_pairs={{0,128},{1,129},{2,130},{3,131},{4,132},{5,133},{6,134},{7,135},{8... | collective-permute-start | bytes 1548296 | tf_op jit(solution)/shard_map/ppermute | solution.py:30
  47.8 9.5 %collective-permute-start.9 = (bf16[168,1536]{1,0:T(8,128)(2,1)S(1)}, bf16[168,1536]{1,0:T(8,128)(2,1)S(1)}, u32[]{:S(2)}, u32[]{:S(2)}) collective-permute-start(bf16[168,1536]{1,0:T(8,128)(2,1)S(1)} %collective-permute-done.4.refs_5_.refs_8_), channel_id=1, source_target_pairs={{0,32},{1,33},{2,34},{3,35},{4,36},{5,37},{6,38},{7,39},{8,40},{9,... | collective-permute-start | bytes 1548296 | tf_op jit(solution)/shard_map/ppermute | solution.py:30
  50.6 13.7 %copy-start.3 = (bf16[168,1536]{1,0:T(8,128)(2,1)}, bf16[168,1536]{1,0:T(8,128)(2,1)S(1)}, u32[]{:S(2)}) copy-start(bf16[168,1536]{1,0:T(8,128)(2,1)S(1)} %collective-permute-done.6.refs_12_.refs_10_) | copy-start | bytes 1548292
  51.8 12.5 %copy-start.9 = (bf16[168,1536]{1,0:T(8,128)(2,1)}, bf16[168,1536]{1,0:T(8,128)(2,1)S(1)}, u32[]{:S(2)}) copy-start(bf16[168,1536]{1,0:T(8,128)(2,1)S(1)} %collective-permute-done.7.refs_3_.refs_1_) | copy-start | bytes 1548292
  51.8 10.8 %collective-permute-start.10 = (bf16[168,1536]{1,0:T(8,128)(2,1)S(1)}, bf16[168,1536]{1,0:T(8,128)(2,1)S(1)}, u32[]{:S(2)}, u32[]{:S(2)}) collective-permute-start(bf16[168,1536]{1,0:T(8,128)(2,1)S(1)} %broadcast_select_fusion.2), channel_id=1, source_target_pairs={{0,128},{1,129},{2,130},{3,131},{4,132},{5,133},{6,134},{7,135},{8... | collective-permute-start | bytes 1548296 | tf_op jit(solution)/shard_map/ppermute | solution.py:30
  52.5 11.8 %collective-permute-start.11 = (bf16[168,1536]{1,0:T(8,128)(2,1)S(1)}, bf16[168,1536]{1,0:T(8,128)(2,1)}, u32[]{:S(2)}, u32[]{:S(2)}) collective-permute-start(bf16[168,1536]{1,0:T(8,128)(2,1)S(1)} %collective-permute-done.6.refs_12_.refs_10_), channel_id=1, source_target_pairs={{0,32},{1,33},{2,34},{3,35},{4,36},{5,37},{6,38},{7,39},{8,40},{9,... | collective-permute-start | bytes 1548296 | tf_op jit(solution)/shard_map/ppermute | solution.py:30
  57.3 7.0 %copy-start.6 = (bf16[168,1536]{1,0:T(8,128)(2,1)}, bf16[168,1536]{1,0:T(8,128)(2,1)S(1)}, u32[]{:S(2)}) copy-start(bf16[168,1536]{1,0:T(8,128)(2,1)S(1)} %collective-permute-done.9.refs_7_.refs_10_) | copy-start | bytes 1548292
  57.3 10.2 %collective-permute-start.13 = (bf16[168,1536]{1,0:T(8,128)(2,1)}, bf16[168,1536]{1,0:T(8,128)(2,1)}, u32[]{:S(2)}, u32[]{:S(2)}) collective-permute-start(bf16[168,1536]{1,0:T(8,128)(2,1)} %broadcast_select_fusion.1), channel_id=1, source_target_pairs={{0,128},{1,129},{2,130},{3,131},{4,132},{5,133},{6,134},{7,135},{8... | collective-permute-start | bytes 1548296 | tf_op jit(solution)/shard_map/ppermute | solution.py:30
  59.9 9.1 %collective-permute-start.14 = (bf16[168,1536]{1,0:T(8,128)(2,1)}, bf16[168,1536]{1,0:T(8,128)(2,1)}, u32[]{:S(2)}, u32[]{:S(2)}) collective-permute-start(bf16[168,1536]{1,0:T(8,128)(2,1)} %collective-permute-done.8.refs_9_.refs_0_), channel_id=1, source_target_pairs={{0,32},{1,33},{2,34},{3,35},{4,36},{5,37},{6,38},{7,39},{8,40},{9,... | collective-permute-start | bytes 1548296 | tf_op jit(solution)/shard_map/ppermute | solution.py:30
  62.6 0.8 copy-start.5
  64.4 8.6 %collective-permute-start.12 = (bf16[168,1536]{1,0:T(8,128)(2,1)}, bf16[168,1536]{1,0:T(8,128)(2,1)}, u32[]{:S(2)}, u32[]{:S(2)}) collective-permute-start(bf16[168,1536]{1,0:T(8,128)(2,1)} %broadcast_select_fusion), channel_id=1, source_target_pairs={{0,128},{1,129},{2,130},{3,131},{4,132},{5,133},{6,134},{7,135},{8... | collective-permute-start | bytes 1548296 | tf_op jit(solution)/shard_map/ppermute | solution.py:30
  65.2 9.3 %collective-permute-start.15 = (bf16[168,1536]{1,0:T(8,128)(2,1)}, bf16[168,1536]{1,0:T(8,128)(2,1)S(1)}, u32[]{:S(2)}, u32[]{:S(2)}) collective-permute-start(bf16[168,1536]{1,0:T(8,128)(2,1)} %copy-done.5), channel_id=1, source_target_pairs={{0,32},{1,33},{2,34},{3,35},{4,36},{5,37},{6,38},{7,39},{8,40},{9,... | collective-permute-start | bytes 1548296 | tf_op jit(solution)/shard_map/ppermute | solution.py:30
  69.0 21.5 %collective-permute-start.16 = (bf16[168,1536]{1,0:T(8,128)(2,1)}, bf16[168,1536]{1,0:T(8,128)(2,1)}, u32[]{:S(2)}, u32[]{:S(2)}) collective-permute-start(bf16[168,1536]{1,0:T(8,128)(2,1)} %collective-permute-done.13.refs_1_.refs_11_), channel_id=1, source_target_pairs={{0,128},{1,129},{2,130},{3,131},{4,132},{5,133},{6,134},{7,135},{8... | collective-permute-start | bytes 1548296 | tf_op jit(solution)/shard_map/ppermute | solution.py:30
  69.7 20.8 %collective-permute-start.17 = (bf16[168,1536]{1,0:T(8,128)(2,1)}, bf16[168,1536]{1,0:T(8,128)(2,1)}, u32[]{:S(2)}, u32[]{:S(2)}) collective-permute-start(bf16[168,1536]{1,0:T(8,128)(2,1)} %collective-permute-done.13.refs_1_.refs_11_), channel_id=1, source_target_pairs={{0,32},{1,33},{2,34},{3,35},{4,36},{5,37},{6,38},{7,39},{8,40},{9,... | collective-permute-start | bytes 1548296 | tf_op jit(solution)/shard_map/ppermute | solution.py:30
  74.5 3.4 %copy-start.10 = (bf16[168,1536]{1,0:T(8,128)(2,1)}, bf16[168,1536]{1,0:T(8,128)(2,1)S(1)}, u32[]{:S(2)}) copy-start(bf16[168,1536]{1,0:T(8,128)(2,1)S(1)} %collective-permute-done.15.refs_15_.refs_6_) | copy-start | bytes 1548292
  74.5 16.8 %collective-permute-start.18 = (bf16[168,1536]{1,0:T(8,128)(2,1)}, bf16[168,1536]{1,0:T(8,128)(2,1)}, u32[]{:S(2)}, u32[]{:S(2)}) collective-permute-start(bf16[168,1536]{1,0:T(8,128)(2,1)} %collective-permute-done.12.refs_5_.refs_13_), channel_id=1, source_target_pairs={{0,128},{1,129},{2,130},{3,131},{4,132},{5,133},{6,134},{7,135},{8... | collective-permute-start | bytes 1548296 | tf_op jit(solution)/shard_map/ppermute | solution.py:30
  75.1 16.3 %collective-permute-start.19 = (bf16[168,1536]{1,0:T(8,128)(2,1)}, bf16[168,1536]{1,0:T(8,128)(2,1)}, u32[]{:S(2)}, u32[]{:S(2)}) collective-permute-start(bf16[168,1536]{1,0:T(8,128)(2,1)} %collective-permute-done.12.refs_5_.refs_13_), channel_id=1, source_target_pairs={{0,32},{1,33},{2,34},{3,35},{4,36},{5,37},{6,38},{7,39},{8,40},{9,... | collective-permute-start | bytes 1548296 | tf_op jit(solution)/shard_map/ppermute | solution.py:30
  90.5 12.9 %collective-permute-start.20 = (bf16[168,1536]{1,0:T(8,128)(2,1)}, bf16[168,1536]{1,0:T(8,128)(2,1)S(1)}, u32[]{:S(2)}, u32[]{:S(2)}) collective-permute-start(bf16[168,1536]{1,0:T(8,128)(2,1)} %collective-permute-done.16.refs_12_), channel_id=1, source_target_pairs={{0,32},{1,33},{2,34},{3,35},{4,36},{5,37},{6,38},{7,39},{8,40},{9,... | collective-permute-start | bytes 1548296 | tf_op jit(solution)/shard_map/ppermute | solution.py:30
  91.3 13.3 %collective-permute-start.21 = (bf16[168,1536]{1,0:T(8,128)(2,1)}, bf16[168,1536]{1,0:T(8,128)(2,1)}, u32[]{:S(2)}, u32[]{:S(2)}) collective-permute-start(bf16[168,1536]{1,0:T(8,128)(2,1)} %collective-permute-done.18.refs_14_), channel_id=1, source_target_pairs={{0,32},{1,33},{2,34},{3,35},{4,36},{5,37},{6,38},{7,39},{8,40},{9,... | collective-permute-start | bytes 1548296 | tf_op jit(solution)/shard_map/ppermute | solution.py:30
  103.3 5.0 %copy-start.13 = (bf16[168,1536]{1,0:T(8,128)(2,1)}, bf16[168,1536]{1,0:T(8,128)(2,1)S(1)}, u32[]{:S(2)}) copy-start(bf16[168,1536]{1,0:T(8,128)(2,1)S(1)} %collective-permute-done.20.refs_4_) | copy-start | bytes 1548292
  104.6 10.4 %collective-permute-start.22 = (bf16[512,1536]{1,0:T(8,128)(2,1)}, bf16[512,1536]{1,0:T(8,128)(2,1)}, u32[]{:S(2)}, u32[]{:S(2)}) collective-permute-start(bf16[512,1536]{1,0:T(8,128)(2,1)} %get-tuple-element.326), channel_id=1, source_target_pairs={{0,16},{1,17},{2,18},{3,19},{4,20},{5,21},{6,22},{7,23},{8,24},{9,... | collective-permute-start | bytes 4718600 | tf_op jit(solution)/shard_map/ppermute | solution.py:30
  114.9 3.8 %collective-permute-start.23 = (bf16[512,1536]{1,0:T(8,128)(2,1)}, bf16[512,1536]{1,0:T(8,128)(2,1)}, u32[]{:S(2)}, u32[]{:S(2)}) collective-permute-start(bf16[512,1536]{1,0:T(8,128)(2,1)} %get-tuple-element.332), channel_id=1, source_target_pairs={{0,16},{1,17},{2,18},{3,19},{4,20},{5,21},{6,22},{7,23},{8,24},{9,... | collective-permute-start | bytes 4718600 | tf_op jit(solution)/shard_map/ppermute | solution.py:30
  118.5 4.1 %copy-start.4 = (bf16[512,1536]{1,0:T(8,128)(2,1)S(1)}, bf16[512,1536]{1,0:T(8,128)(2,1)}, u32[]{:S(2)}) copy-start(bf16[512,1536]{1,0:T(8,128)(2,1)} %get-tuple-element.333.refs_1_) | copy-start | bytes 4718596
  120.1 6.6 %collective-permute-start.26 = (bf16[64,1536]{1,0:T(8,128)(2,1)S(1)}, bf16[64,1536]{1,0:T(8,128)(2,1)S(1)}, u32[]{:S(2)}, u32[]{:S(2)}) collective-permute-start(bf16[64,1536]{1,0:T(8,128)(2,1)S(1)} %get-tuple-element.336), channel_id=1, source_target_pairs={{0,3},{1,0},{2,1},{3,2},{4,7},{5,4},{6,5},{7,6},{8,11},{9,8},{10,9... | collective-permute-start | bytes 589832 | tf_op jit(solution)/shard_map/ppermute | solution.py:30
  124.0 7.9 %collective-permute-start.24 = (bf16[64,1536]{1,0:T(8,128)(2,1)S(1)}, bf16[64,1536]{1,0:T(8,128)(2,1)S(1)}, u32[]{:S(2)}, u32[]{:S(2)}) collective-permute-start(bf16[64,1536]{1,0:T(8,128)(2,1)S(1)} %get-tuple-element.335), channel_id=1, source_target_pairs={{0,1},{1,2},{2,3},{3,0},{4,5},{5,6},{6,7},{7,4},{8,9},{9,10},{10,1... | collective-permute-start | bytes 589832 | tf_op jit(solution)/shard_map/ppermute | solution.py:30
  127.5 18.9 %collective-permute-start.27 = (bf16[128,1536]{1,0:T(8,128)(2,1)}, bf16[128,1536]{1,0:T(8,128)(2,1)S(1)}, u32[]{:S(2)}, u32[]{:S(2)}) collective-permute-start(bf16[128,1536]{1,0:T(8,128)(2,1)} %pad_maximum_fusion.1), channel_id=1, source_target_pairs={{0,3},{1,0},{2,1},{3,2},{4,7},{5,4},{6,5},{7,6},{8,11},{9,8},{10,9... | collective-permute-start | bytes 1179656 | tf_op jit(solution)/shard_map/ppermute | solution.py:30
  132.8 19.4 %collective-permute-start.25 = (bf16[128,1536]{1,0:T(8,128)(2,1)}, bf16[128,1536]{1,0:T(8,128)(2,1)}, u32[]{:S(2)}, u32[]{:S(2)}) collective-permute-start(bf16[128,1536]{1,0:T(8,128)(2,1)} %pad_maximum_fusion), channel_id=1, source_target_pairs={{0,1},{1,2},{2,3},{3,0},{4,5},{5,6},{6,7},{7,4},{8,9},{9,10},{10,1... | collective-permute-start | bytes 1179656 | tf_op jit(solution)/shard_map/ppermute | solution.py:30
  146.4 6.0 %copy-start.14 = (bf16[128,1536]{1,0:T(8,128)(2,1)}, bf16[128,1536]{1,0:T(8,128)(2,1)S(1)}, u32[]{:S(2)}) copy-start(bf16[128,1536]{1,0:T(8,128)(2,1)S(1)} %collective-permute-done.27.refs_4_) | copy-start | bytes 1179652
Sparse Core Ops, SparseCore 0:
  12.2 47.6 all-gather.1
  118.6 33.8 reduce-scatter.1

commit v4 on v3

--- a/solution.py
+++ b/solution.py
@@ -348,7 +348,7 @@
         if step == 1:
             own += [piece(shard[which], start, half) for which, start in order[2:]]
             work["own"] = [lax.dynamic_slice_in_dim(array, near_units, UNITS, 0) for array in shard[:2]]
-            work["down"] = [piece(shard[2], near_units, side) for side in (half, 1 - half)]
+            work["down"] = [own[2], piece(shard[2], near_units, 1 - half)]
             work["place"] = place
         if step < 11:
             from_z.append(moved(block, along_z))

time: 164 us -> 164 us (level)
  no operation moved by 1% of the time
where the time goes in v4:
time: 164 us
  starting transfers between devices  51.5 us (31%)
  Pallas kernels  35 us (21%)
  waiting for transfers between devices  31.1 us (19%)
  local copies, waits for them, and re-layouts  16.4 us (10%)
  other arithmetic  14.5 us (9%)
  between operations  13.7 us (8%)
    ppermute x28, starting transfers between devices, moved(): return lax.ppermute(value, AXES, pairs)  51.5 us
    ppermute x28, waiting for transfers between devices, moved(): return lax.ppermute(value, AXES, pairs)  30.8 us
    pallas_call x3, Pallas kernels, kernel_call(): pl.pallas_call(kernel, out_shape=[jax.ShapeDtypeStruct(shape, jnp.bfloat1...  30.7 us
    dynamic_slice x4, local copies, waits for them, and re-layouts, piece(): return lax.dynamic_slice(array, (start, side * SPLIT), (UNITS, SPLIT))  7.51 us
    pallas_call x1, Pallas kernels, spread(): pl.pallas_call(spread_kernel, out_shape=jax.ShapeDtypeStruct((SPANS * CT,...  4.32 us
    convert_element_type x1, other arithmetic, on_device(): (mine_here.astype(jnp.float32) + moved(others_here, other_core).astype(jn...  3.41 us
  transfers between devices with their start and end apart: 30, of which 16 were waited for; matrix products, arithmetic and copies ran while one was open for 15% of the time, Pallas kernels for 19%

profile of v4, /device:TPU:1, one launch (start us, length us, event | category | flops | bytes accessed | tf_op | source)
XLA Modules:
  0.0 163.6 jit_solution(6047946463301290394)
XLA Ops:
  6.5 0.9 select_reduce_fusion
  7.5 1.2 reduce_window_sum.11
  8.7 1.9 %dynamic-slice_bitcast_fusion = bf16[168,1536]{1,0:T(8,128)(2,1)} fusion(bf16[3072,336]{0,1:T(8,128)(2,1)} %param.9, s32[]{:T(128)S(6)} %select_n.93, s32[]{:T(128)S(6)} %select_n.94), kind=kLoop, calls=%fused_computation.5 | loop fusion | bytes 1032200 | tf_op jit(solution)/shard_map/dynamic_slice | solution.py:309
  10.6 1.4 convolution_convert_fusion
  12.1 6.5 %collective-permute-start = (bf16[168,1536]{1,0:T(8,128)(2,1)}, bf16[168,1536]{1,0:T(8,128)(2,1)}, u32[]{:S(2)}, u32[]{:S(2)}) collective-permute-start(bf16[168,1536]{1,0:T(8,128)(2,1)} %dynamic-slice_bitcast_fusion), channel_id=1, source_target_pairs={{0,128},{1,129},{2,130},{3,131},{4,132},{5,133},{6,134},{7,135},{8... | collective-permute-start | bytes 1548296 | tf_op jit(solution)/shard_map/ppermute | solution.py:30
  18.6 1.9 %dynamic_slice.46 = bf16[168,1536]{1,0:T(8,128)(2,1)} dynamic-slice(bf16[336,3072]{1,0:T(8,128)(2,1)} %bitcast.22, s32[]{:T(128)S(6)} %select_n.94, s32[]{:T(128)S(6)} %select_n.93), dynamic_slice_sizes={168,1536} | dynamic-slice | bytes 1032196 | tf_op jit(solution)/shard_map/dynamic_slice | solution.py:309
  21.2 1.9 %dynamic_slice.48 = bf16[168,1536]{1,0:T(8,128)(2,1)} dynamic-slice(bf16[336,3072]{1,0:T(8,128)(2,1)} %bitcast.20, s32[]{:T(128)S(6)} %select_n.96, s32[]{:T(128)S(6)} %select_n.93), dynamic_slice_sizes={168,1536} | dynamic-slice | bytes 1032196 | tf_op jit(solution)/shard_map/dynamic_slice | solution.py:309
  23.1 1.9 %dynamic_slice.49 = bf16[168,1536]{1,0:T(8,128)(2,1)} dynamic-slice(bf16[336,3072]{1,0:T(8,128)(2,1)} %bitcast.23, s32[]{:T(128)S(6)} %select_n.96, s32[]{:T(128)S(6)} %select_n.93), dynamic_slice_sizes={168,1536} | dynamic-slice | bytes 1032196 | tf_op jit(solution)/shard_map/dynamic_slice | solution.py:309
  25.5 3.1 %constant_dynamic-slice_fusion = (bf16[168,3072]{1,0:T(8,128)(2,1)}, bf16[168,3072]{1,0:T(8,128)(2,1)}) fusion(bf16[336,3072]{1,0:T(8,128)(2,1)} %bitcast.24, s32[]{:T(128)S(6)} %select_n.94, bf16[336,3072]{1,0:T(8,128)(2,1)} %bitcast.21), kind=kLoop, calls=%fused_computation.29 | loop fusion | bytes 4128772 | tf_op jit(solution)/shard_map/dynamic_slice | solution.py:350
  28.7 1.2 fusion.6
  29.9 1.8 %collective-permute-start.2 = (bf16[168,1536]{1,0:T(8,128)(2,1)S(1)}, bf16[168,1536]{1,0:T(8,128)(2,1)S(1)}, u32[]{:S(2)}, u32[]{:S(2)}) collective-permute-start(bf16[168,1536]{1,0:T(8,128)(2,1)S(1)} %get-tuple-element.189), channel_id=1, source_target_pairs={{0,128},{1,129},{2,130},{3,131},{4,132},{5,133},{6,134},{7,135},{8... | collective-permute-start | bytes 1548296 | tf_op jit(solution)/shard_map/ppermute | solution.py:30
  31.7 2.8 %collective-permute-start.3 = (bf16[168,1536]{1,0:T(8,128)(2,1)}, bf16[168,1536]{1,0:T(8,128)(2,1)}, u32[]{:S(2)}, u32[]{:S(2)}) collective-permute-start(bf16[168,1536]{1,0:T(8,128)(2,1)} %collective-permute-done.refs_0_), channel_id=1, source_target_pairs={{0,32},{1,33},{2,34},{3,35},{4,36},{5,37},{6,38},{7,39},{8,40},{9,... | collective-permute-start | bytes 1548296 | tf_op jit(solution)/shard_map/ppermute | solution.py:30
  34.6 1.1 collective-permute-start.4
  35.7 1.8 %collective-permute-start.5 = (bf16[168,1536]{1,0:T(8,128)(2,1)}, bf16[168,1536]{1,0:T(8,128)(2,1)S(1)}, u32[]{:S(2)}, u32[]{:S(2)}) collective-permute-start(bf16[168,1536]{1,0:T(8,128)(2,1)} %collective-permute-done.1.refs_4_), channel_id=1, source_target_pairs={{0,32},{1,33},{2,34},{3,35},{4,36},{5,37},{6,38},{7,39},{8,40},{9,... | collective-permute-start | bytes 1548296 | tf_op jit(solution)/shard_map/ppermute | solution.py:30
  37.5 1.2 collective-permute-done.2.refs_1_.refs_9_
  38.8 2.1 %collective-permute-done.3.refs_2_ = bf16[168,1536]{1,0:T(8,128)(2,1)} collective-permute-done((bf16[168,1536]{1,0:T(8,128)(2,1)}, bf16[168,1536]{1,0:T(8,128)(2,1)}, u32[]{:S(2)}, u32[]{:S(2)}) %collective-permute-start.3) | collective-permute-done | bytes 516128 | tf_op jit(solution)/shard_map/ppermute | solution.py:30
  41.5 2.8 %collective-permute-start.7 = (bf16[168,1536]{1,0:T(8,128)(2,1)S(1)}, bf16[168,1536]{1,0:T(8,128)(2,1)S(1)}, u32[]{:S(2)}, u32[]{:S(2)}) collective-permute-start(bf16[168,1536]{1,0:T(8,128)(2,1)S(1)} %collective-permute-done.2.refs_1_.refs_9_), channel_id=1, source_target_pairs={{0,32},{1,33},{2,34},{3,35},{4,36},{5,37},{6,38},{7,39},{8,40},{9,... | collective-permute-start | bytes 1548296 | tf_op jit(solution)/shard_map/ppermute | solution.py:30
  44.3 2.1 %collective-permute-done.5.refs_6_ = bf16[168,1536]{1,0:T(8,128)(2,1)S(1)} collective-permute-done((bf16[168,1536]{1,0:T(8,128)(2,1)}, bf16[168,1536]{1,0:T(8,128)(2,1)S(1)}, u32[]{:S(2)}, u32[]{:S(2)}) %collective-permute-start.5) | collective-permute-done | bytes 516128 | tf_op jit(solution)/shard_map/ppermute | solution.py:30
  47.8 2.8 %collective-permute-start.9 = (bf16[168,1536]{1,0:T(8,128)(2,1)S(1)}, bf16[168,1536]{1,0:T(8,128)(2,1)S(1)}, u32[]{:S(2)}, u32[]{:S(2)}) collective-permute-start(bf16[168,1536]{1,0:T(8,128)(2,1)S(1)} %collective-permute-done.4.refs_5_.refs_8_), channel_id=1, source_target_pairs={{0,32},{1,33},{2,34},{3,35},{4,36},{5,37},{6,38},{7,39},{8,40},{9,... | collective-permute-start | bytes 1548296 | tf_op jit(solution)/shard_map/ppermute | solution.py:30
  50.7 1.1 collective-permute-done.7.refs_3_.refs_1_
  52.5 2.8 %collective-permute-start.11 = (bf16[168,1536]{1,0:T(8,128)(2,1)S(1)}, bf16[168,1536]{1,0:T(8,128)(2,1)}, u32[]{:S(2)}, u32[]{:S(2)}) collective-permute-start(bf16[168,1536]{1,0:T(8,128)(2,1)S(1)} %collective-permute-done.6.refs_12_.refs_10_), channel_id=1, source_target_pairs={{0,32},{1,33},{2,34},{3,35},{4,36},{5,37},{6,38},{7,39},{8,40},{9,... | collective-permute-start | bytes 1548296 | tf_op jit(solution)/shard_map/ppermute | solution.py:30
  55.6 0.9 broadcast_select_fusion.1
  56.4 0.9 collective-permute-done.9.refs_7_.refs_10_
  57.3 2.5 %collective-permute-start.13 = (bf16[168,1536]{1,0:T(8,128)(2,1)}, bf16[168,1536]{1,0:T(8,128)(2,1)}, u32[]{:S(2)}, u32[]{:S(2)}) collective-permute-start(bf16[168,1536]{1,0:T(8,128)(2,1)} %broadcast_select_fusion.1), channel_id=1, source_target_pairs={{0,128},{1,129},{2,130},{3,131},{4,132},{5,133},{6,134},{7,135},{8... | collective-permute-start | bytes 1548296 | tf_op jit(solution)/shard_map/ppermute | solution.py:30
  59.9 2.8 %collective-permute-start.14 = (bf16[168,1536]{1,0:T(8,128)(2,1)}, bf16[168,1536]{1,0:T(8,128)(2,1)}, u32[]{:S(2)}, u32[]{:S(2)}) collective-permute-start(bf16[168,1536]{1,0:T(8,128)(2,1)} %collective-permute-done.8.refs_9_.refs_0_), channel_id=1, source_target_pairs={{0,32},{1,33},{2,34},{3,35},{4,36},{5,37},{6,38},{7,39},{8,40},{9,... | collective-permute-start | bytes 1548296 | tf_op jit(solution)/shard_map/ppermute | solution.py:30
  65.2 2.4 %collective-permute-start.15 = (bf16[168,1536]{1,0:T(8,128)(2,1)}, bf16[168,1536]{1,0:T(8,128)(2,1)S(1)}, u32[]{:S(2)}, u32[]{:S(2)}) collective-permute-start(bf16[168,1536]{1,0:T(8,128)(2,1)} %copy-done.5), channel_id=1, source_target_pairs={{0,32},{1,33},{2,34},{3,35},{4,36},{5,37},{6,38},{7,39},{8,40},{9,... | collective-permute-start | bytes 1548296 | tf_op jit(solution)/shard_map/ppermute | solution.py:30
  67.6 1.4 collective-permute-done.14.refs_11_.refs_2_
  69.7 2.8 %collective-permute-start.17 = (bf16[168,1536]{1,0:T(8,128)(2,1)}, bf16[168,1536]{1,0:T(8,128)(2,1)}, u32[]{:S(2)}, u32[]{:S(2)}) collective-permute-start(bf16[168,1536]{1,0:T(8,128)(2,1)} %collective-permute-done.13.refs_1_.refs_11_), channel_id=1, source_target_pairs={{0,32},{1,33},{2,34},{3,35},{4,36},{5,37},{6,38},{7,39},{8,40},{9,... | collective-permute-start | bytes 1548296 | tf_op jit(solution)/shard_map/ppermute | solution.py:30
  73.0 1.5 collective-permute-done.15.refs_15_.refs_6_
  75.1 2.9 %collective-permute-start.19 = (bf16[168,1536]{1,0:T(8,128)(2,1)}, bf16[168,1536]{1,0:T(8,128)(2,1)}, u32[]{:S(2)}, u32[]{:S(2)}) collective-permute-start(bf16[168,1536]{1,0:T(8,128)(2,1)} %collective-permute-done.12.refs_5_.refs_13_), channel_id=1, source_target_pairs={{0,32},{1,33},{2,34},{3,35},{4,36},{5,37},{6,38},{7,39},{8,40},{9,... | collective-permute-start | bytes 1548296 | tf_op jit(solution)/shard_map/ppermute | solution.py:30
  78.0 12.5 %shard_map.64.first_ref = bf16[1024,504]{1,0:T(8,128)(2,1)} custom-call(s32[4]{0:T(128)} %pad_add_fusion.place_ref, bf16[1024,3072]{1,0:T(8,128)(2,1)} %all-gather.2.cloned.1.call-done.rows_ref, bf16[168,1536]{1,0:T(8,128)(2,1)} %collective-permute-done.refs_0_, bf16[168,1536]{1,0:T(8,128)(2,1)} %copy-done.2, ...), custom_call_target="tpu_custom_call" | custom-call | flops 1000000 | bytes 100000 | tf_op jit(solution)/shard_map/pallas_call | solution.py:183
  91.7 11.7 %shard_map.65 = (bf16[512,1536]{1,0:T(8,128)(2,1)}, bf16[512,1536]{1,0:T(8,128)(2,1)}, bf16[1024,168]{1,0:T(8,128)(2,1)}) custom-call(s32[4]{0:T(128)} %pad_add_fusion.place_ref, bf16[1024,3072]{1,0:T(8,128)(2,1)} %all-gather.2.cloned.1.call-done.rows_ref, bf16[1024,504]{1,0:T(8,128)(2,1)} %shard_map.64.first_ref, ...), custom_call_target="tpu_custom_call" | custom-call | flops 1000000 | bytes 100000 | tf_op jit(solution)/shard_map/pallas_call | solution.py:183
  103.4 1.3 collective-permute-done.21.refs_6_
  104.6 3.7 %collective-permute-start.22 = (bf16[512,1536]{1,0:T(8,128)(2,1)}, bf16[512,1536]{1,0:T(8,128)(2,1)}, u32[]{:S(2)}, u32[]{:S(2)}) collective-permute-start(bf16[512,1536]{1,0:T(8,128)(2,1)} %get-tuple-element.326), channel_id=1, source_target_pairs={{0,16},{1,17},{2,18},{3,19},{4,20},{5,21},{6,22},{7,23},{8,24},{9,... | collective-permute-start | bytes 4718600 | tf_op jit(solution)/shard_map/ppermute | solution.py:30
  108.4 6.5 %shard_map.66 = (bf16[512,1536]{1,0:T(8,128)(2,1)}, bf16[512,1536]{1,0:T(8,128)(2,1)}) custom-call(s32[4]{0:T(128)} %pad_add_fusion.place_ref, bf16[1024,504]{1,0:T(8,128)(2,1)} %shard_map.64.first_ref, bf16[1024,168]{1,0:T(8,128)(2,1)} %get-tuple-element.327.last_ref, bf16[168,1536]{1,0:T(8,128)(2,1)} %get-tuple-element.328.refs_0_, ...), custom_call_target="tpu_custom_call" | custom-call | flops 1000000 | bytes 100000 | tf_op jit(solution)/shard_map/pallas_call | solution.py:183
  115.0 3.4 %add_convert_fusion = bf16[512,1536]{1,0:T(8,128)(2,1)} fusion(bf16[512,1536]{1,0:T(8,128)(2,1)} %collective-permute-done.22, bf16[512,1536]{1,0:T(8,128)(2,1)} %get-tuple-element.323), kind=kLoop, calls=%fused_computation.1 | loop fusion | flops 3145728 | bytes 4718592 | tf_op jit(solution)/shard_map/convert_element_type | solution.py:371
  118.8 1.3 add_convert_fusion.1
  120.1 2.5 %collective-permute-start.26 = (bf16[64,1536]{1,0:T(8,128)(2,1)S(1)}, bf16[64,1536]{1,0:T(8,128)(2,1)S(1)}, u32[]{:S(2)}, u32[]{:S(2)}) collective-permute-start(bf16[64,1536]{1,0:T(8,128)(2,1)S(1)} %get-tuple-element.336), channel_id=1, source_target_pairs={{0,3},{1,0},{2,1},{3,2},{4,7},{5,4},{6,5},{7,6},{8,11},{9,8},{10,9... | collective-permute-start | bytes 589832 | tf_op jit(solution)/shard_map/ppermute | solution.py:30
  122.7 1.3 convert_add_fusion
  124.2 2.5 %collective-permute-done.26 = bf16[64,1536]{1,0:T(8,128)(2,1)S(1)} collective-permute-done((bf16[64,1536]{1,0:T(8,128)(2,1)S(1)}, bf16[64,1536]{1,0:T(8,128)(2,1)S(1)}, u32[]{:S(2)}, u32[]{:S(2)}) %collective-permute-start.26) | collective-permute-done | bytes 196640 | tf_op jit(solution)/shard_map/ppermute | solution.py:30
  127.5 3.4 %collective-permute-start.27 = (bf16[128,1536]{1,0:T(8,128)(2,1)}, bf16[128,1536]{1,0:T(8,128)(2,1)S(1)}, u32[]{:S(2)}, u32[]{:S(2)}) collective-permute-start(bf16[128,1536]{1,0:T(8,128)(2,1)} %pad_maximum_fusion.1), channel_id=1, source_target_pairs={{0,3},{1,0},{2,1},{3,2},{4,7},{5,4},{6,5},{7,6},{8,11},{9,8},{10,9... | collective-permute-start | bytes 1179656 | tf_op jit(solution)/shard_map/ppermute | solution.py:30
  130.9 1.0 collective-permute-done.24
  133.6 1.5 reshape.56
  135.1 1.6 copy.7.places_ref
  136.7 0.9 copy.8.share_ref
  137.6 8.9 %collective-permute-done.27.refs_4_ = bf16[128,1536]{1,0:T(8,128)(2,1)S(1)} collective-permute-done((bf16[128,1536]{1,0:T(8,128)(2,1)}, bf16[128,1536]{1,0:T(8,128)(2,1)S(1)}, u32[]{:S(2)}, u32[]{:S(2)}) %collective-permute-start.27) | collective-permute-done | bytes 393248 | tf_op jit(solution)/shard_map/ppermute | solution.py:30
  146.4 5.7 %collective-permute-done.25.refs_3_ = bf16[128,1536]{1,0:T(8,128)(2,1)} collective-permute-done((bf16[128,1536]{1,0:T(8,128)(2,1)}, bf16[128,1536]{1,0:T(8,128)(2,1)}, u32[]{:S(2)}, u32[]{:S(2)}) %collective-permute-start.25) | collective-permute-done | bytes 393248 | tf_op jit(solution)/shard_map/ppermute | solution.py:30
  152.4 4.3 %shard_map.67 = bf16[512,3072]{1,0:T(8,128)(2,1)} custom-call(s32[4]{0:T(128)} %pad_add_fusion.place_ref, bf16[512,64]{1,0:T(8,128)(2,1)} %copy.7.places_ref, f32[512,1]{1,0:T(8,128)} %copy.8.share_ref, bf16[128,1536]{1,0:T(8,128)(2,1)} %reduce-scatter.2.cloned.1.call-done.refs_0_, bf16[512,1536]{1,0:T(8,128)(2,1)} %get-tuple-element.333.refs_1_, ...), custom_call_target="tpu_custom_call" | custom-call | tf_op jit(solution)/shard_map/pallas_call | solution.py:273
  (84 shorter events, 13.5 us)
Async XLA Ops:
  6.5 4.0 %copy-start = (bf16[512,3072]{1,0:T(8,128)(2,1)S(1)}, bf16[512,3072]{1,0:T(8,128)(2,1)}, u32[]{:S(2)}) copy-start(bf16[512,3072]{1,0:T(8,128)(2,1)} %param.6) | copy-start | bytes 9437188
  6.5 57.8 %all-gather.2.cloned.1.call-start = ((), (), s32[]{:S(2)}) async-start(), calls=%async_computation.1 | async-start | bytes 7077888 | tf_op jit(solution)/shard_map/all_gather | solution.py:358
  12.0 140.4 %reduce-scatter.2.cloned.1.call-start = ((), (), s32[]{:S(2)}) async-start(), calls=%async_computation.2 | async-start | bytes 1966080 | tf_op jit(solution)/shard_map/reduce_scatter | solution.py:372
  12.1 16.6 %collective-permute-start = (bf16[168,1536]{1,0:T(8,128)(2,1)}, bf16[168,1536]{1,0:T(8,128)(2,1)}, u32[]{:S(2)}, u32[]{:S(2)}) collective-permute-start(bf16[168,1536]{1,0:T(8,128)(2,1)} %dynamic-slice_bitcast_fusion), channel_id=1, source_target_pairs={{0,128},{1,129},{2,130},{3,131},{4,132},{5,133},{6,134},{7,135},{8... | collective-permute-start | bytes 1548296 | tf_op jit(solution)/shard_map/ppermute | solution.py:30
  20.4 14.1 %collective-permute-start.1 = (bf16[168,1536]{1,0:T(8,128)(2,1)}, bf16[168,1536]{1,0:T(8,128)(2,1)}, u32[]{:S(2)}, u32[]{:S(2)}) collective-permute-start(bf16[168,1536]{1,0:T(8,128)(2,1)} %dynamic_slice.46), channel_id=1, source_target_pairs={{0,128},{1,129},{2,130},{3,131},{4,132},{5,133},{6,134},{7,135},{8... | collective-permute-start | bytes 1548296 | tf_op jit(solution)/shard_map/ppermute | solution.py:30
  25.5 3.1 %copy-start.11 = (bf16[336,3072]{1,0:T(8,128)(2,1)S(1)}, bf16[336,3072]{1,0:T(8,128)(2,1)}, u32[]{:S(2)}) copy-start(bf16[336,3072]{1,0:T(8,128)(2,1)} %param.11) | copy-start | bytes 6193156
  28.7 5.9 %copy-start.8 = (bf16[168,1536]{1,0:T(8,128)(2,1)S(1)}, bf16[168,1536]{1,0:T(8,128)(2,1)}, u32[]{:S(2)}) copy-start(bf16[168,1536]{1,0:T(8,128)(2,1)} %dynamic_slice.48) | copy-start | bytes 1548292
  28.7 10.0 %copy-start.7 = (bf16[168,1536]{1,0:T(8,128)(2,1)S(1)}, bf16[168,1536]{1,0:T(8,128)(2,1)}, u32[]{:S(2)}) copy-start(bf16[168,1536]{1,0:T(8,128)(2,1)} %dynamic_slice.49) | copy-start | bytes 1548292
  29.9 8.8 %collective-permute-start.2 = (bf16[168,1536]{1,0:T(8,128)(2,1)S(1)}, bf16[168,1536]{1,0:T(8,128)(2,1)S(1)}, u32[]{:S(2)}, u32[]{:S(2)}) collective-permute-start(bf16[168,1536]{1,0:T(8,128)(2,1)S(1)} %get-tuple-element.189), channel_id=1, source_target_pairs={{0,128},{1,129},{2,130},{3,131},{4,132},{5,133},{6,134},{7,135},{8... | collective-permute-start | bytes 1548296 | tf_op jit(solution)/shard_map/ppermute | solution.py:30
  31.7 9.1 %collective-permute-start.3 = (bf16[168,1536]{1,0:T(8,128)(2,1)}, bf16[168,1536]{1,0:T(8,128)(2,1)}, u32[]{:S(2)}, u32[]{:S(2)}) collective-permute-start(bf16[168,1536]{1,0:T(8,128)(2,1)} %collective-permute-done.refs_0_), channel_id=1, source_target_pairs={{0,32},{1,33},{2,34},{3,35},{4,36},{5,37},{6,38},{7,39},{8,40},{9,... | collective-permute-start | bytes 1548296 | tf_op jit(solution)/shard_map/ppermute | solution.py:30
  34.6 9.7 %collective-permute-start.4 = (bf16[168,1536]{1,0:T(8,128)(2,1)S(1)}, bf16[168,1536]{1,0:T(8,128)(2,1)S(1)}, u32[]{:S(2)}, u32[]{:S(2)}) collective-permute-start(bf16[168,1536]{1,0:T(8,128)(2,1)S(1)} %broadcast_select_fusion.5), channel_id=1, source_target_pairs={{0,128},{1,129},{2,130},{3,131},{4,132},{5,133},{6,134},{7,135},{8... | collective-permute-start | bytes 1548296 | tf_op jit(solution)/shard_map/ppermute | solution.py:30
  35.7 10.7 %collective-permute-start.5 = (bf16[168,1536]{1,0:T(8,128)(2,1)}, bf16[168,1536]{1,0:T(8,128)(2,1)S(1)}, u32[]{:S(2)}, u32[]{:S(2)}) collective-permute-start(bf16[168,1536]{1,0:T(8,128)(2,1)} %collective-permute-done.1.refs_4_), channel_id=1, source_target_pairs={{0,32},{1,33},{2,34},{3,35},{4,36},{5,37},{6,38},{7,39},{8,40},{9,... | collective-permute-start | bytes 1548296 | tf_op jit(solution)/shard_map/ppermute | solution.py:30
  38.7 12.0 %copy-start.2 = (bf16[168,1536]{1,0:T(8,128)(2,1)}, bf16[168,1536]{1,0:T(8,128)(2,1)S(1)}, u32[]{:S(2)}) copy-start(bf16[168,1536]{1,0:T(8,128)(2,1)S(1)} %collective-permute-done.2.refs_1_.refs_9_) | copy-start | bytes 1548292
  40.9 9.8 %collective-permute-start.6 = (bf16[168,1536]{1,0:T(8,128)(2,1)S(1)}, bf16[168,1536]{1,0:T(8,128)(2,1)S(1)}, u32[]{:S(2)}, u32[]{:S(2)}) collective-permute-start(bf16[168,1536]{1,0:T(8,128)(2,1)S(1)} %broadcast_select_fusion.4), channel_id=1, source_target_pairs={{0,128},{1,129},{2,130},{3,131},{4,132},{5,133},{6,134},{7,135},{8... | collective-permute-start | bytes 1548296 | tf_op jit(solution)/shard_map/ppermute | solution.py:30
  41.5 10.4 %collective-permute-start.7 = (bf16[168,1536]{1,0:T(8,128)(2,1)S(1)}, bf16[168,1536]{1,0:T(8,128)(2,1)S(1)}, u32[]{:S(2)}, u32[]{:S(2)}) collective-permute-start(bf16[168,1536]{1,0:T(8,128)(2,1)S(1)} %collective-permute-done.2.refs_1_.refs_9_), channel_id=1, source_target_pairs={{0,32},{1,33},{2,34},{3,35},{4,36},{5,37},{6,38},{7,39},{8,40},{9,... | collective-permute-start | bytes 1548296 | tf_op jit(solution)/shard_map/ppermute | solution.py:30
  44.3 12.1 %copy-start.1 = (bf16[168,1536]{1,0:T(8,128)(2,1)}, bf16[168,1536]{1,0:T(8,128)(2,1)S(1)}, u32[]{:S(2)}) copy-start(bf16[168,1536]{1,0:T(8,128)(2,1)S(1)} %collective-permute-done.4.refs_5_.refs_8_) | copy-start | bytes 1548292
  46.4 0.8 copy-start.12
  47.2 8.3 %collective-permute-start.8 = (bf16[168,1536]{1,0:T(8,128)(2,1)S(1)}, bf16[168,1536]{1,0:T(8,128)(2,1)}, u32[]{:S(2)}, u32[]{:S(2)}) collective-permute-start(bf16[168,1536]{1,0:T(8,128)(2,1)S(1)} %broadcast_select_fusion.3), channel_id=1, source_target_pairs={{0,128},{1,129},{2,130},{3,131},{4,132},{5,133},{6,134},{7,135},{8... | collective-permute-start | bytes 1548296 | tf_op jit(solution)/shard_map/ppermute | solution.py:30
  47.8 9.5 %collective-permute-start.9 = (bf16[168,1536]{1,0:T(8,128)(2,1)S(1)}, bf16[168,1536]{1,0:T(8,128)(2,1)S(1)}, u32[]{:S(2)}, u32[]{:S(2)}) collective-permute-start(bf16[168,1536]{1,0:T(8,128)(2,1)S(1)} %collective-permute-done.4.refs_5_.refs_8_), channel_id=1, source_target_pairs={{0,32},{1,33},{2,34},{3,35},{4,36},{5,37},{6,38},{7,39},{8,40},{9,... | collective-permute-start | bytes 1548296 | tf_op jit(solution)/shard_map/ppermute | solution.py:30
  50.6 13.7 %copy-start.3 = (bf16[168,1536]{1,0:T(8,128)(2,1)}, bf16[168,1536]{1,0:T(8,128)(2,1)S(1)}, u32[]{:S(2)}) copy-start(bf16[168,1536]{1,0:T(8,128)(2,1)S(1)} %collective-permute-done.6.refs_12_.refs_10_) | copy-start | bytes 1548292
  51.8 12.5 %copy-start.9 = (bf16[168,1536]{1,0:T(8,128)(2,1)}, bf16[168,1536]{1,0:T(8,128)(2,1)S(1)}, u32[]{:S(2)}) copy-start(bf16[168,1536]{1,0:T(8,128)(2,1)S(1)} %collective-permute-done.7.refs_3_.refs_1_) | copy-start | bytes 1548292
  51.8 10.8 %collective-permute-start.10 = (bf16[168,1536]{1,0:T(8,128)(2,1)S(1)}, bf16[168,1536]{1,0:T(8,128)(2,1)S(1)}, u32[]{:S(2)}, u32[]{:S(2)}) collective-permute-start(bf16[168,1536]{1,0:T(8,128)(2,1)S(1)} %broadcast_select_fusion.2), channel_id=1, source_target_pairs={{0,128},{1,129},{2,130},{3,131},{4,132},{5,133},{6,134},{7,135},{8... | collective-permute-start | bytes 1548296 | tf_op jit(solution)/shard_map/ppermute | solution.py:30
  52.5 11.8 %collective-permute-start.11 = (bf16[168,1536]{1,0:T(8,128)(2,1)S(1)}, bf16[168,1536]{1,0:T(8,128)(2,1)}, u32[]{:S(2)}, u32[]{:S(2)}) collective-permute-start(bf16[168,1536]{1,0:T(8,128)(2,1)S(1)} %collective-permute-done.6.refs_12_.refs_10_), channel_id=1, source_target_pairs={{0,32},{1,33},{2,34},{3,35},{4,36},{5,37},{6,38},{7,39},{8,40},{9,... | collective-permute-start | bytes 1548296 | tf_op jit(solution)/shard_map/ppermute | solution.py:30
  57.3 7.0 %copy-start.6 = (bf16[168,1536]{1,0:T(8,128)(2,1)}, bf16[168,1536]{1,0:T(8,128)(2,1)S(1)}, u32[]{:S(2)}) copy-start(bf16[168,1536]{1,0:T(8,128)(2,1)S(1)} %collective-permute-done.9.refs_7_.refs_10_) | copy-start | bytes 1548292
  57.3 10.2 %collective-permute-start.13 = (bf16[168,1536]{1,0:T(8,128)(2,1)}, bf16[168,1536]{1,0:T(8,128)(2,1)}, u32[]{:S(2)}, u32[]{:S(2)}) collective-permute-start(bf16[168,1536]{1,0:T(8,128)(2,1)} %broadcast_select_fusion.1), channel_id=1, source_target_pairs={{0,128},{1,129},{2,130},{3,131},{4,132},{5,133},{6,134},{7,135},{8... | collective-permute-start | bytes 1548296 | tf_op jit(solution)/shard_map/ppermute | solution.py:30
  59.9 9.1 %collective-permute-start.14 = (bf16[168,1536]{1,0:T(8,128)(2,1)}, bf16[168,1536]{1,0:T(8,128)(2,1)}, u32[]{:S(2)}, u32[]{:S(2)}) collective-permute-start(bf16[168,1536]{1,0:T(8,128)(2,1)} %collective-permute-done.8.refs_9_.refs_0_), channel_id=1, source_target_pairs={{0,32},{1,33},{2,34},{3,35},{4,36},{5,37},{6,38},{7,39},{8,40},{9,... | collective-permute-start | bytes 1548296 | tf_op jit(solution)/shard_map/ppermute | solution.py:30
  62.6 0.8 copy-start.5
  64.4 8.6 %collective-permute-start.12 = (bf16[168,1536]{1,0:T(8,128)(2,1)}, bf16[168,1536]{1,0:T(8,128)(2,1)}, u32[]{:S(2)}, u32[]{:S(2)}) collective-permute-start(bf16[168,1536]{1,0:T(8,128)(2,1)} %broadcast_select_fusion), channel_id=1, source_target_pairs={{0,128},{1,129},{2,130},{3,131},{4,132},{5,133},{6,134},{7,135},{8... | collective-permute-start | bytes 1548296 | tf_op jit(solution)/shard_map/ppermute | solution.py:30
  65.2 9.3 %collective-permute-start.15 = (bf16[168,1536]{1,0:T(8,128)(2,1)}, bf16[168,1536]{1,0:T(8,128)(2,1)S(1)}, u32[]{:S(2)}, u32[]{:S(2)}) collective-permute-start(bf16[168,1536]{1,0:T(8,128)(2,1)} %copy-done.5), channel_id=1, source_target_pairs={{0,32},{1,33},{2,34},{3,35},{4,36},{5,37},{6,38},{7,39},{8,40},{9,... | collective-permute-start | bytes 1548296 | tf_op jit(solution)/shard_map/ppermute | solution.py:30
  69.0 21.5 %collective-permute-start.16 = (bf16[168,1536]{1,0:T(8,128)(2,1)}, bf16[168,1536]{1,0:T(8,128)(2,1)}, u32[]{:S(2)}, u32[]{:S(2)}) collective-permute-start(bf16[168,1536]{1,0:T(8,128)(2,1)} %collective-permute-done.13.refs_1_.refs_11_), channel_id=1, source_target_pairs={{0,128},{1,129},{2,130},{3,131},{4,132},{5,133},{6,134},{7,135},{8... | collective-permute-start | bytes 1548296 | tf_op jit(solution)/shard_map/ppermute | solution.py:30
  69.7 20.8 %collective-permute-start.17 = (bf16[168,1536]{1,0:T(8,128)(2,1)}, bf16[168,1536]{1,0:T(8,128)(2,1)}, u32[]{:S(2)}, u32[]{:S(2)}) collective-permute-start(bf16[168,1536]{1,0:T(8,128)(2,1)} %collective-permute-done.13.refs_1_.refs_11_), channel_id=1, source_target_pairs={{0,32},{1,33},{2,34},{3,35},{4,36},{5,37},{6,38},{7,39},{8,40},{9,... | collective-permute-start | bytes 1548296 | tf_op jit(solution)/shard_map/ppermute | solution.py:30
  74.5 3.4 %copy-start.10 = (bf16[168,1536]{1,0:T(8,128)(2,1)}, bf16[168,1536]{1,0:T(8,128)(2,1)S(1)}, u32[]{:S(2)}) copy-start(bf16[168,1536]{1,0:T(8,128)(2,1)S(1)} %collective-permute-done.15.refs_15_.refs_6_) | copy-start | bytes 1548292
  74.5 16.8 %collective-permute-start.18 = (bf16[168,1536]{1,0:T(8,128)(2,1)}, bf16[168,1536]{1,0:T(8,128)(2,1)}, u32[]{:S(2)}, u32[]{:S(2)}) collective-permute-start(bf16[168,1536]{1,0:T(8,128)(2,1)} %collective-permute-done.12.refs_5_.refs_13_), channel_id=1, source_target_pairs={{0,128},{1,129},{2,130},{3,131},{4,132},{5,133},{6,134},{7,135},{8... | collective-permute-start | bytes 1548296 | tf_op jit(solution)/shard_map/ppermute | solution.py:30
  75.1 16.3 %collective-permute-start.19 = (bf16[168,1536]{1,0:T(8,128)(2,1)}, bf16[168,1536]{1,0:T(8,128)(2,1)}, u32[]{:S(2)}, u32[]{:S(2)}) collective-permute-start(bf16[168,1536]{1,0:T(8,128)(2,1)} %collective-permute-done.12.refs_5_.refs_13_), channel_id=1, source_target_pairs={{0,32},{1,33},{2,34},{3,35},{4,36},{5,37},{6,38},{7,39},{8,40},{9,... | collective-permute-start | bytes 1548296 | tf_op jit(solution)/shard_map/ppermute | solution.py:30
  90.5 12.9 %collective-permute-start.20 = (bf16[168,1536]{1,0:T(8,128)(2,1)}, bf16[168,1536]{1,0:T(8,128)(2,1)S(1)}, u32[]{:S(2)}, u32[]{:S(2)}) collective-permute-start(bf16[168,1536]{1,0:T(8,128)(2,1)} %collective-permute-done.16.refs_12_), channel_id=1, source_target_pairs={{0,32},{1,33},{2,34},{3,35},{4,36},{5,37},{6,38},{7,39},{8,40},{9,... | collective-permute-start | bytes 1548296 | tf_op jit(solution)/shard_map/ppermute | solution.py:30
  91.3 13.3 %collective-permute-start.21 = (bf16[168,1536]{1,0:T(8,128)(2,1)}, bf16[168,1536]{1,0:T(8,128)(2,1)}, u32[]{:S(2)}, u32[]{:S(2)}) collective-permute-start(bf16[168,1536]{1,0:T(8,128)(2,1)} %collective-permute-done.18.refs_14_), channel_id=1, source_target_pairs={{0,32},{1,33},{2,34},{3,35},{4,36},{5,37},{6,38},{7,39},{8,40},{9,... | collective-permute-start | bytes 1548296 | tf_op jit(solution)/shard_map/ppermute | solution.py:30
  103.3 5.0 %copy-start.13 = (bf16[168,1536]{1,0:T(8,128)(2,1)}, bf16[168,1536]{1,0:T(8,128)(2,1)S(1)}, u32[]{:S(2)}) copy-start(bf16[168,1536]{1,0:T(8,128)(2,1)S(1)} %collective-permute-done.20.refs_4_) | copy-start | bytes 1548292
  104.6 10.4 %collective-permute-start.22 = (bf16[512,1536]{1,0:T(8,128)(2,1)}, bf16[512,1536]{1,0:T(8,128)(2,1)}, u32[]{:S(2)}, u32[]{:S(2)}) collective-permute-start(bf16[512,1536]{1,0:T(8,128)(2,1)} %get-tuple-element.326), channel_id=1, source_target_pairs={{0,16},{1,17},{2,18},{3,19},{4,20},{5,21},{6,22},{7,23},{8,24},{9,... | collective-permute-start | bytes 4718600 | tf_op jit(solution)/shard_map/ppermute | solution.py:30
  114.9 3.8 %collective-permute-start.23 = (bf16[512,1536]{1,0:T(8,128)(2,1)}, bf16[512,1536]{1,0:T(8,128)(2,1)}, u32[]{:S(2)}, u32[]{:S(2)}) collective-permute-start(bf16[512,1536]{1,0:T(8,128)(2,1)} %get-tuple-element.332), channel_id=1, source_target_pairs={{0,16},{1,17},{2,18},{3,19},{4,20},{5,21},{6,22},{7,23},{8,24},{9,... | collective-permute-start | bytes 4718600 | tf_op jit(solution)/shard_map/ppermute | solution.py:30
  118.5 4.1 %copy-start.4 = (bf16[512,1536]{1,0:T(8,128)(2,1)S(1)}, bf16[512,1536]{1,0:T(8,128)(2,1)}, u32[]{:S(2)}) copy-start(bf16[512,1536]{1,0:T(8,128)(2,1)} %get-tuple-element.333.refs_1_) | copy-start | bytes 4718596
  120.1 6.6 %collective-permute-start.26 = (bf16[64,1536]{1,0:T(8,128)(2,1)S(1)}, bf16[64,1536]{1,0:T(8,128)(2,1)S(1)}, u32[]{:S(2)}, u32[]{:S(2)}) collective-permute-start(bf16[64,1536]{1,0:T(8,128)(2,1)S(1)} %get-tuple-element.336), channel_id=1, source_target_pairs={{0,3},{1,0},{2,1},{3,2},{4,7},{5,4},{6,5},{7,6},{8,11},{9,8},{10,9... | collective-permute-start | bytes 589832 | tf_op jit(solution)/shard_map/ppermute | solution.py:30
  124.0 7.9 %collective-permute-start.24 = (bf16[64,1536]{1,0:T(8,128)(2,1)S(1)}, bf16[64,1536]{1,0:T(8,128)(2,1)S(1)}, u32[]{:S(2)}, u32[]{:S(2)}) collective-permute-start(bf16[64,1536]{1,0:T(8,128)(2,1)S(1)} %get-tuple-element.335), channel_id=1, source_target_pairs={{0,1},{1,2},{2,3},{3,0},{4,5},{5,6},{6,7},{7,4},{8,9},{9,10},{10,1... | collective-permute-start | bytes 589832 | tf_op jit(solution)/shard_map/ppermute | solution.py:30
  127.5 18.9 %collective-permute-start.27 = (bf16[128,1536]{1,0:T(8,128)(2,1)}, bf16[128,1536]{1,0:T(8,128)(2,1)S(1)}, u32[]{:S(2)}, u32[]{:S(2)}) collective-permute-start(bf16[128,1536]{1,0:T(8,128)(2,1)} %pad_maximum_fusion.1), channel_id=1, source_target_pairs={{0,3},{1,0},{2,1},{3,2},{4,7},{5,4},{6,5},{7,6},{8,11},{9,8},{10,9... | collective-permute-start | bytes 1179656 | tf_op jit(solution)/shard_map/ppermute | solution.py:30
  132.8 19.4 %collective-permute-start.25 = (bf16[128,1536]{1,0:T(8,128)(2,1)}, bf16[128,1536]{1,0:T(8,128)(2,1)}, u32[]{:S(2)}, u32[]{:S(2)}) collective-permute-start(bf16[128,1536]{1,0:T(8,128)(2,1)} %pad_maximum_fusion), channel_id=1, source_target_pairs={{0,1},{1,2},{2,3},{3,0},{4,5},{5,6},{6,7},{7,4},{8,9},{9,10},{10,1... | collective-permute-start | bytes 1179656 | tf_op jit(solution)/shard_map/ppermute | solution.py:30
  146.4 6.0 %copy-start.14 = (bf16[128,1536]{1,0:T(8,128)(2,1)}, bf16[128,1536]{1,0:T(8,128)(2,1)S(1)}, u32[]{:S(2)}) copy-start(bf16[128,1536]{1,0:T(8,128)(2,1)S(1)} %collective-permute-done.27.refs_4_) | copy-start | bytes 1179652
Sparse Core Ops, SparseCore 0:
  12.2 47.6 all-gather.1
  118.6 33.8 reduce-scatter.1
